TPU v7x, 32 devices: a whole 2x2x4 slice. The times are simulated.
32 devices in a mesh: rep: 4 (over x, core), shard: 8 (over z, y).
Axes of the slice: x: 2, y: 2, z: 4, core: 2. Of those that a mesh axis runs over, the one named last changes fastest.
Arguments:
- tokens: bfloat16 [20480, 1536], P(('rep', 'shard')), may hold values from -6 to 6
- norm_gains: bfloat16 [2, 1536], P(None, 'shard'), may hold values from 0.25 to 1.75
- qkv_weight: bfloat16 [1536, 2560], P('shard'), may hold values from -0.21875 to 0.21875
- out_weight: bfloat16 [1536, 1536], P('shard'), may hold values from -0.625 to 0.625
- router_weight: bfloat16 [1536, 16], P('shard'), may hold values from -0.078125 to 0.078125
- gate_up_weight: bfloat16 [16, 1536, 1024], P(None, 'shard'), may hold values from -0.15625 to 0.15625
- down_weight: bfloat16 [16, 512, 1536], P(None, 'shard'), may hold values from -1 to 1
- routes: int32 [20480, 8], P(('rep', 'shard')), may hold values from 0 to 15, all different within a row; in each aligned block of 640 rows (0 to 639, 640 to 1279, ...) at most 352 rows name the same one
- placement: int32 [160], replicated, may hold values from 0 to 19, as said below
- parents: int32 [8, 20], replicated, may hold values from 0 to 11, as said below
- cotangent: bfloat16 [20480, 1536], P(('rep', 'shard')), may hold values from -6 to 6
Outputs:
- block_out: bfloat16 [20480, 1536], P(('rep', 'shard'))
- token_grad: float32 [20480, 1536], P(('rep', 'shard'))
- gains_grad: float32 [2, 1536], P(None, 'shard')
- qkv_grad: float32 [1536, 2560], P('shard')
- out_grad: float32 [1536, 1536], P('shard')
- router_grad: float32 [1536, 16], P('shard')
- gate_up_grad: float32 [16, 1536, 1024], P(None, 'shard')
- down_grad: float32 [16, 512, 1536], P(None, 'shard')
Inputs may be any that keep to these rules, and one draw needn't show every extreme that they name: `routes`: in the rows of one device no expert is named by more than 352 rows, a bound that some block reaches. `placement`: each aligned run of 20 entries holds every number of its range once. `parents`: in every row, segment 0 is its own parent, segments 1 to 7 have the parent one less, segments 8 to 11 have the parent 8 - 1, and every other segment has one of those branch segments as parent; every branch segment is some segment's parent.
All inputs are finite; a program needn't handle non-finite values.
Results may differ from a plain program's by a relative error of at most 0.019.
Values may be sent and summed in bfloat16 or wider, within the bound.
A program may use at most 448 MiB of HBM per device.

v0:
```python
import jax
import jax.numpy as jnp
from jax import lax
from jax.sharding import PartitionSpec as P

D = 1536
H = 24
KVH = 8
HD = 64
FF = 512
TOP = 8
E = 16
SEG = 128
TRUNK = 8
TREE_DEVS = 4
TREE_SEGS = 20
CAP = 352


EPS = 1e-06
MASK_VALUE = -1e30


def partner(block, axis, stride):
    count = lax.axis_size(axis)
    route = []
    for low in range(count):
        high = low | 1 << stride
        if high != low and high < count:
            route += [(low, high), (high, low)]
    return lax.ppermute(block, axis, route)


def norm_rows(values, gain):
    scale_rows = lax.rsqrt(jnp.mean(values * values, axis=-1, keepdims=True) + EPS)
    return (values * scale_rows * gain, scale_rows)


def norm_back(values, scale_rows, gain, upstream):
    scaled = upstream * gain
    inner = jnp.mean(scaled * values, axis=-1, keepdims=True)
    through = scale_rows * scaled - values * (scale_rows * scale_rows * scale_rows) * inner
    gain_grad = jnp.sum(upstream * values * scale_rows, axis=0)
    return (through, gain_grad)


def table_lookup(table, index):
    positions = jnp.arange(table.shape[0], dtype=jnp.int32)
    return jnp.sum(jnp.where(index[:, None] == positions[None, :], table[None, :], 0), axis=1)


def find_slot(group_ids, wanted):
    positions = jnp.arange(group_ids.shape[0], dtype=jnp.int32)
    return jnp.sum(jnp.where(group_ids[None, :] == wanted[:, None], positions[None, :], 0), axis=1)


def ancestor_slots(local_ids, group_ids, group_parents, depth):
    flat_parents = group_parents.reshape(-1)
    tree_index = local_ids // TREE_SEGS
    current = local_ids % TREE_SEGS
    alive = jnp.ones(local_ids.shape, dtype=bool)
    slot_list = []
    alive_list = []
    for level in range(depth):
        wanted = tree_index * TREE_SEGS + current
        slot_list.append(find_slot(group_ids, wanted))
        alive_list.append(alive)
        parent_seg = table_lookup(flat_parents, wanted)
        alive = alive & (parent_seg != current)
        current = parent_seg
    return (jnp.stack(slot_list, axis=1), jnp.stack(alive_list, axis=1))


def head_scores(queries, keys, mask, scale):
    scores = jnp.einsum("sgqd,skd->sgqk", queries, keys, preferred_element_type=jnp.float32) * scale
    return jnp.where(mask[:, None], scores, MASK_VALUE)


def head_forward(operands, mask, scale):
    queries, keys, values = operands
    scores = head_scores(queries, keys, mask, scale)
    highest = jnp.max(scores, axis=-1, keepdims=True)
    weights = jnp.exp(scores - highest)
    totals = jnp.sum(weights, axis=-1, keepdims=True)
    probs = (weights / totals).astype(jnp.bfloat16)
    mixed = jnp.einsum("sgqk,skd->sgqd", probs, values, preferred_element_type=jnp.float32)
    return (mixed.astype(jnp.bfloat16), highest + jnp.log(totals))


def head_backward(operands, mask, scale):
    queries, keys, values, upstream, log_totals = operands
    scores = head_scores(queries, keys, mask, scale)
    probs = jnp.exp(scores - log_totals)
    value_grad = jnp.einsum(
        "sgqk,sgqd->skd", probs.astype(jnp.bfloat16), upstream, preferred_element_type=jnp.float32
    )
    prob_grad = jnp.einsum("sgqd,skd->sgqk", upstream, values, preferred_element_type=jnp.float32)
    inner = jnp.sum(probs * prob_grad, axis=-1, keepdims=True)
    score_grad = (probs * (prob_grad - inner)).astype(jnp.bfloat16)
    query_grad = (
        jnp.einsum("sgqk,skd->sgqd", score_grad, keys, preferred_element_type=jnp.float32) * scale
    )
    key_grad = (
        jnp.einsum("sgqk,sgqd->skd", score_grad, queries, preferred_element_type=jnp.float32)
        * scale
    )
    return (query_grad.astype(jnp.bfloat16), key_grad, value_grad)


def shards(
    tokens,
    norm_gains,
    qkv_weight,
    out_weight,
    router_weight,
    gate_up_weight,
    down_weight,
    routes,
    placement,
    parents,
    cotangent,
):
    shard_index = lax.axis_index("shard")
    rep_index = lax.axis_index("rep")
    shard_count = lax.axis_size("shard")
    token_count = tokens.shape[0]
    seg_dev = token_count // SEG
    depth = TRUNK + 2
    key_count = depth * SEG
    width_q = H * HD
    width_kv = KVH * HD
    groups_per = H // KVH
    scale = HD ** (-0.5)
    group_size = TREE_DEVS * seg_dev
    tree_count = group_size // TREE_SEGS
    member = shard_index % TREE_DEVS
    group = (rep_index * shard_count + shard_index) // TREE_DEVS
    group_ids = lax.dynamic_slice_in_dim(placement, group * group_size, group_size)
    group_parents = lax.dynamic_slice_in_dim(parents, group * tree_count, tree_count)
    local_ids = lax.dynamic_slice_in_dim(group_ids, member * seg_dev, seg_dev)
    path_slots, path_alive = ancestor_slots(local_ids, group_ids, group_parents, depth)
    key_level = jnp.arange(key_count, dtype=jnp.int32) // SEG
    key_pos = jnp.arange(key_count, dtype=jnp.int32) % SEG
    query_pos = jnp.arange(SEG, dtype=jnp.int32)
    level_alive = jnp.repeat(path_alive, SEG, axis=1)
    mask = level_alive[:, None, :] & (
        (key_level[None, None, :] > 0) | (key_pos[None, None, :] <= query_pos[None, :, None])
    )
    gathered = (
        lax.all_gather(norm_gains, "shard", axis=1, tiled=True),
        lax.all_gather(qkv_weight, "shard", axis=0, tiled=True),
        lax.all_gather(out_weight, "shard", axis=0, tiled=True),
        lax.all_gather(router_weight, "shard", axis=0, tiled=True),
        lax.all_gather(gate_up_weight, "shard", axis=1, tiled=True),
        lax.all_gather(down_weight, "shard", axis=1, tiled=True),
    )
    gains, w_qkv, w_out, w_router, w_gate_up, w_down = gathered
    gain_first = gains[0].astype(jnp.float32)
    gain_second = gains[1].astype(jnp.float32)
    token_values = tokens.astype(jnp.float32)
    normed_first, scale_first = norm_rows(token_values, gain_first)
    act_first = normed_first.astype(jnp.bfloat16)
    projected = jnp.dot(act_first, w_qkv, preferred_element_type=jnp.float32)
    queries = projected[:, :width_q].astype(jnp.bfloat16)
    own_kv = projected[:, width_q:].astype(jnp.bfloat16).reshape(seg_dev, SEG, 2 * width_kv)
    low_first = member % 2 == 0
    pair_first = member // 2 == 0
    near_kv = partner(own_kv, "shard", 0)
    pair_kv = jnp.where(
        low_first,
        jnp.concatenate([own_kv, near_kv], axis=0),
        jnp.concatenate([near_kv, own_kv], axis=0),
    )
    far_kv = partner(pair_kv, "shard", 1)
    group_kv = jnp.where(
        pair_first,
        jnp.concatenate([pair_kv, far_kv], axis=0),
        jnp.concatenate([far_kv, pair_kv], axis=0),
    )
    chosen_kv = group_kv[path_slots].reshape(seg_dev, key_count, 2, KVH, HD)
    head_kv = chosen_kv.transpose(3, 2, 0, 1, 4)
    head_keys = head_kv[:, 0]
    head_values = head_kv[:, 1]
    head_queries = queries.reshape(seg_dev, SEG, KVH, groups_per, HD).transpose(2, 0, 3, 1, 4)
    mixed, log_totals = lax.map(
        lambda operands: head_forward(operands, mask, scale), (head_queries, head_keys, head_values)
    )
    attended = mixed.transpose(1, 3, 0, 2, 4).reshape(token_count, width_q)
    residual = token_values + jnp.dot(attended, w_out, preferred_element_type=jnp.float32)
    normed_second, scale_second = norm_rows(residual, gain_second)
    act_second = normed_second.astype(jnp.bfloat16)
    logits = jnp.dot(act_second, w_router, preferred_element_type=jnp.float32)
    expert_ids = jnp.arange(E, dtype=jnp.int32)
    picks = routes[:, :, None] == expert_ids[None, None, :]
    chosen = jnp.sum(jnp.where(picks, logits[:, None, :], 0.0), axis=-1)
    gates = jax.nn.softmax(chosen, axis=-1)
    flat_picks = picks.reshape(token_count * TOP, E).astype(jnp.int32)
    before = jnp.cumsum(flat_picks, axis=0) - flat_picks
    place_in = jnp.sum(before * flat_picks, axis=1)
    slots = routes.reshape(-1) * CAP + place_in
    sources = jnp.arange(token_count * TOP, dtype=jnp.int32) // TOP
    slot_token = jnp.zeros((E * CAP,), jnp.int32).at[slots].set(sources)
    slot_gate = jnp.zeros((E * CAP,), jnp.float32).at[slots].set(gates.reshape(-1))
    dispatched = act_second[slot_token].reshape(E, CAP, D)
    gate_up = jnp.einsum("ecd,edf->ecf", dispatched, w_gate_up, preferred_element_type=jnp.float32)
    hidden = (jax.nn.silu(gate_up[..., :FF]) * gate_up[..., FF:]).astype(jnp.bfloat16)
    expert_out = jnp.einsum(
        "ecf,efd->ecd", hidden, w_down, preferred_element_type=jnp.float32
    ).reshape(E * CAP, D)
    slot_rows = slots.reshape(token_count, TOP)
    picked = expert_out[slot_rows]
    mixture = jnp.sum(gates[:, :, None] * picked, axis=1)
    block_out = (residual + mixture).astype(jnp.bfloat16)
    upstream = cotangent.astype(jnp.float32)
    gate_grads = jnp.sum(picked * upstream[:, None, :], axis=-1)
    back_weights = (
        lax.all_gather(norm_gains, "shard", axis=1, tiled=True),
        lax.all_gather(qkv_weight, "shard", axis=0, tiled=True),
        lax.all_gather(out_weight, "shard", axis=0, tiled=True),
        lax.all_gather(router_weight, "shard", axis=0, tiled=True),
        lax.all_gather(gate_up_weight, "shard", axis=1, tiled=True),
        lax.all_gather(down_weight, "shard", axis=1, tiled=True),
    )
    back_gains, back_qkv, back_out, back_router, back_gate_up, back_down = back_weights
    chosen_grad = gates * (gate_grads - jnp.sum(gates * gate_grads, axis=-1, keepdims=True))
    logit_grad = jnp.sum(jnp.where(picks, chosen_grad[:, :, None], 0.0), axis=1)
    router_grad = jnp.dot(
        act_second.astype(jnp.float32).T,
        logit_grad,
        precision=lax.Precision.HIGHEST,
        preferred_element_type=jnp.float32,
    )
    out_slot_grad = (
        (slot_gate[:, None] * upstream[slot_token]).astype(jnp.bfloat16).reshape(E, CAP, D)
    )
    gate_part = gate_up[..., :FF]
    up_part = gate_up[..., FF:]
    sig_gate = jax.nn.sigmoid(gate_part)
    hidden_grad = jnp.einsum(
        "ecd,efd->ecf", out_slot_grad, back_down, preferred_element_type=jnp.float32
    )
    gate_grad_part = hidden_grad * up_part * sig_gate * (1.0 + gate_part * (1.0 - sig_gate))
    up_grad_part = hidden_grad * gate_part * sig_gate
    gate_up_grad_slots = jnp.concatenate([gate_grad_part, up_grad_part], axis=-1).astype(
        jnp.bfloat16
    )
    down_grad = jnp.einsum(
        "ecf,ecd->efd", hidden, out_slot_grad, preferred_element_type=jnp.float32
    )
    gate_up_grad = jnp.einsum(
        "ecd,ecf->edf", dispatched, gate_up_grad_slots, preferred_element_type=jnp.float32
    )
    dispatched_grad = jnp.einsum(
        "ecf,edf->ecd", gate_up_grad_slots, back_gate_up, preferred_element_type=jnp.float32
    ).reshape(E * CAP, D)
    act_second_grad = jnp.sum(dispatched_grad[slot_rows], axis=1)
    act_second_grad = act_second_grad + jnp.dot(
        logit_grad,
        back_router.astype(jnp.float32).T,
        precision=lax.Precision.HIGHEST,
        preferred_element_type=jnp.float32,
    )
    through_second, gain_grad_second = norm_back(
        residual, scale_second, back_gains[1].astype(jnp.float32), act_second_grad
    )
    residual_grad = upstream + through_second
    branch_grad = residual_grad.astype(jnp.bfloat16)
    out_grad = jnp.dot(attended.T, branch_grad, preferred_element_type=jnp.float32)
    attended_grad = jnp.dot(branch_grad, back_out.T, preferred_element_type=jnp.float32).astype(
        jnp.bfloat16
    )
    head_upstream = attended_grad.reshape(seg_dev, SEG, KVH, groups_per, HD).transpose(
        2, 0, 3, 1, 4
    )
    query_grad, key_grad, value_grad = lax.map(
        lambda operands: head_backward(operands, mask, scale),
        (head_queries, head_keys, head_values, head_upstream, log_totals),
    )
    query_grad = query_grad.transpose(1, 3, 0, 2, 4).reshape(token_count, width_q)
    path_grad = (
        jnp.stack([key_grad, value_grad], axis=1)
        .transpose(2, 3, 1, 0, 4)
        .reshape(seg_dev, depth, SEG, 2 * width_kv)
    )
    group_grad = (
        jnp.zeros((group_size, SEG, 2 * width_kv), jnp.float32).at[path_slots].add(path_grad)
    )
    pair_part = jnp.where(pair_first, group_grad[: 2 * seg_dev], group_grad[2 * seg_dev :])
    far_part = jnp.where(pair_first, group_grad[2 * seg_dev :], group_grad[: 2 * seg_dev])
    pair_sum = pair_part + partner(far_part.astype(jnp.bfloat16), "shard", 1).astype(far_part.dtype)
    own_part = jnp.where(low_first, pair_sum[:seg_dev], pair_sum[seg_dev:])
    near_part = jnp.where(low_first, pair_sum[seg_dev:], pair_sum[:seg_dev])
    own_grad = own_part + partner(near_part.astype(jnp.bfloat16), "shard", 0).astype(
        near_part.dtype
    )
    projected_grad = jnp.concatenate(
        [query_grad, own_grad.reshape(token_count, 2 * width_kv).astype(jnp.bfloat16)], axis=1
    )
    qkv_grad = jnp.dot(act_first.T, projected_grad, preferred_element_type=jnp.float32)
    act_first_grad = jnp.dot(projected_grad, back_qkv.T, preferred_element_type=jnp.float32)
    through_first, gain_grad_first = norm_back(
        token_values, scale_first, back_gains[0].astype(jnp.float32), act_first_grad
    )
    token_grad = residual_grad + through_first
    gains_grad = jnp.stack([gain_grad_first, gain_grad_second], axis=0)
    shares = (
        lax.psum_scatter(gains_grad, "shard", scatter_dimension=1, tiled=True),
        lax.psum_scatter(qkv_grad, "shard", scatter_dimension=0, tiled=True),
        lax.psum_scatter(out_grad, "shard", scatter_dimension=0, tiled=True),
        lax.psum_scatter(router_grad, "shard", scatter_dimension=0, tiled=True),
        lax.psum_scatter(gate_up_grad, "shard", scatter_dimension=1, tiled=True),
        lax.psum_scatter(down_grad, "shard", scatter_dimension=1, tiled=True),
    )
    totals = (
        lax.psum(shares[0].astype(jnp.bfloat16), "rep").astype(jnp.float32),
        lax.psum(shares[1].astype(jnp.bfloat16), "rep").astype(jnp.float32),
        lax.psum(shares[2].astype(jnp.bfloat16), "rep").astype(jnp.float32),
        lax.psum(shares[3].astype(jnp.bfloat16), "rep").astype(jnp.float32),
        lax.psum(shares[4].astype(jnp.bfloat16), "rep").astype(jnp.float32),
        lax.psum(shares[5].astype(jnp.bfloat16), "rep").astype(jnp.float32),
    )
    return (block_out, token_grad, totals[0], totals[1], totals[2], totals[3], totals[4], totals[5])


def solution(mesh):
    in_specs = (
        P(("rep", "shard"), None),
        P(None, "shard"),
        P("shard", None),
        P("shard", None),
        P("shard", None),
        P(None, "shard", None),
        P(None, "shard", None),
        P(("rep", "shard"), None),
        P(),
        P(),
        P(("rep", "shard"), None),
    )
    out_specs = (
        P(("rep", "shard"), None),
        P(("rep", "shard"), None),
        P(None, "shard"),
        P("shard", None),
        P("shard", None),
        P("shard", None),
        P(None, "shard", None),
        P(None, "shard", None),
    )
    return jax.shard_map(shards, mesh=mesh, in_specs=in_specs, out_specs=out_specs, check_vma=False)
```

profile of v0, /device:TPU:9, one launch (start us, length us, event | category | flops | bytes accessed | tf_op | source)
XLA Modules:
  0.0 5445.7 jit_solution(3911537761570196086)
XLA Ops:
  10.7 15.1 all-gather
  35.9 91.6 %all-gather.7.cloned.1.call-done = bf16[1536,2560]{1,0:T(8,128)(2,1)} async-done(((bf16[192,2560]{1,0:T(8,128)(2,1)}), bf16[1536,2560]{1,0:T(8,128)(2,1)}) %all-gather.7.cloned.1.call-update) | async-done | bytes 7864336 | tf_op jit(solution)/shard_map/all_gather | solution.py:151
  127.5 8.9 convolution_convert_fusion
  139.0 40.3 collective-permute-done
  184.5 179.1 %all-gather.1 = bf16[8,192,16]{1,2,0:T(8,128)(2,1)S(1)} all-gather(bf16[1,192,16]{1,2,0:T(8,128)(2,1)S(1)} %bitcast.298), channel_id=1, replica_groups=mesh['rep'=4,'shard'=8] {'shard'}, dimensions={0}, use_global_device_ids=true | all-gather | bytes 55296 | tf_op jit(solution)/shard_map/all_gather | solution.py:153
  364.5 19.7 scatter_custom_fusion
  384.4 35.6 gather_fusion.3
  429.9 6.8 maximum_select_fusion
  436.7 9.3 gather_fusion
  446.0 20.5 copy.121
  466.5 30.3 reshape.726
  496.7 16.3 slice_bitcast_fusion
  513.0 8.5 copy.124
  521.6 8.5 copy.125
  531.9 96.3 %while.28 = (s32[]{:T(128)}, bf16[8,5,3,128,64]{3,4,2,1,0:T(8,128)(2,1)}, f32[8,5,3,128,1]{3,2,1,4,0:T(4,128)}, bf16[8,5,3,128,64]{3,4,2,1,0:T(8,128)(2,1)}, bf1...) while((s32[]{:T(128)}, ...), condition=%wide.region_23.24_spmd.clone, body=%wide.region_20.23_spmd.clone.sunk | while | flops 659576960 | bytes 35134312 | solution.py:185
  633.3 7.0 multiply_reduce_fusion.3
  642.6 19.5 gather_fusion.1
  664.4 19.4 scatter_custom_fusion.1
  683.9 505.0 %all-gather.11.cloned.1.call-done = bf16[16,1536,1024]{2,1,0:T(8,128)(2,1)} async-done(((bf16[16,192,1024]{2,1,0:T(8,128)(2,1)}), bf16[16,1536,1024]{2,1,0:T(8,128)(2,1)}) %all-gather.11.cloned.1.call-update) | async-done | bytes 50331664 | tf_op jit(solution)/shard_map/all_gather | solution.py:154
  1189.0 34.8 fusion.117
  1223.7 447.3 %all-gather.13.cloned.1.call-done = bf16[16,512,1536]{2,1,0:T(8,128)(2,1)} async-done(((bf16[16,64,1536]{2,1,0:T(8,128)(2,1)}), bf16[16,512,1536]{2,1,0:T(8,128)(2,1)}) %all-gather.13.cloned.1.call-update) | async-done | bytes 25165840 | tf_op jit(solution)/shard_map/all_gather | solution.py:155
  1671.0 38.6 multiply_convert_fusion.3
  1709.6 39.8 fusion.58
  1749.4 44.5 gather_fusion.4
  1793.9 16.4 bitcast_reduce_fusion
  1810.3 25.1 fusion.118
  1835.4 44.7 gather_fusion.2
  1880.2 15.8 fusion.55
  1929.8 296.3 %while.29 = (s32[]{:T(128)}, bf16[8,5,3,128,64]{3,4,2,1,0:T(8,128)(2,1)S(1)}, f32[8,5,1280,64]{2,3,1,0:T(8,128)}, f32[8,5,1280,64]{2,3,1,0:T(8,128)}, bf16[8,5,3...) while((s32[]{:T(128)}, ...), condition=%wide.region_41.42_spmd.clone, body=%wide.region_39.41_spmd.clone.sunk | while | flops 1596455040 | bytes 141525936 | solution.py:275
  1933.9 9.7 multiply_reduce_fusion.6
  1943.6 9.9 multiply_convert_fusion.9
  1971.1 9.7 multiply_reduce_fusion.6
  1980.9 9.9 multiply_convert_fusion.9
  2008.2 9.8 multiply_reduce_fusion.6
  2018.0 10.1 multiply_convert_fusion.9
  2045.5 9.7 multiply_reduce_fusion.6
  2055.3 9.9 multiply_convert_fusion.9
  2082.6 9.8 multiply_reduce_fusion.6
  2092.4 9.8 multiply_convert_fusion.9
  2119.5 9.7 multiply_reduce_fusion.6
  2129.3 9.8 multiply_convert_fusion.9
  2156.3 9.7 multiply_reduce_fusion.6
  2166.1 9.8 multiply_convert_fusion.9
  2193.1 9.7 multiply_reduce_fusion.6
  2202.9 9.8 multiply_convert_fusion.9
  2226.1 19.0 maximum_bitcast_fusion
  2245.1 42.2 copy.150
  2287.3 43.5 reshape.821
  2336.2 56.0 %scatter_fusion = f32[20,128,1024]{2,1,0:T(8,128)} fusion(f32[20,128,1024]{2,1,0:T(8,128)} %broadcast_in_dim.310, s32[50]{0:T(128)S(1)} %copy-done.49, f32[50,128,1024]{2,1,0:T(8,128)} %reshape.821), kind=kCustom, calls=%fused_computation.7 | custom fusion | flops 6553600 | bytes 78643400 | tf_op jit(solution)/shard_map/scatter-add | solution.py:286
  2396.8 58.2 %collective-permute-done.2 = bf16[10,128,1024]{2,1,0:T(8,128)(2,1)S(1)} collective-permute-done((bf16[10,128,1024]{2,1,0:T(8,128)(2,1)S(1)}, bf16[10,128,1024]{2,1,0:T(8,128)(2,1)S(1)}, u32[]{:S(2)}, u32[]{:S(2)}) %collective-permute-start.2) | collective-permute-done | bytes 2621472 | tf_op jit(solution)/shard_map/ppermute | solution.py:31
  2465.3 25.6 collective-permute-done.3
  2493.2 11.7 fusion.70
  2505.6 32.4 fusion.59
  2538.1 48.2 fusion.57
  2591.0 10.6 fusion.69
  2605.1 149.6 %reduce-scatter.11.cloned.1.call-done = f32[192,2560]{1,0:T(8,128)} async-done(((f32[1536,2560]{1,0:T(8,128)}), f32[192,2560]{1,0:T(8,128)}) %reduce-scatter.11.cloned.1.call-update) | async-done | bytes 1966096 | tf_op jit(solution)/shard_map/reduce_scatter | solution.py:308
  2757.3 790.8 %reduce-scatter.17.cloned.1.call-done = f32[16,64,1536]{2,1,0:T(8,128)} async-done(((f32[16,512,1536]{2,1,0:T(8,128)}), f32[16,64,1536]{2,1,0:T(8,128)}) %reduce-scatter.17.cloned.1.call-update) | async-done | bytes 6291472 | tf_op jit(solution)/shard_map/reduce_scatter | solution.py:312
  3552.9 1537.4 %reduce-scatter.15.cloned.1.call-done = f32[16,192,1024]{2,1,0:T(8,128)} async-done(((f32[16,1536,1024]{2,1,0:T(8,128)}), f32[16,192,1024]{2,1,0:T(8,128)}) %reduce-scatter.15.cloned.1.call-update) | async-done | bytes 12582928 | tf_op jit(solution)/shard_map/reduce_scatter | solution.py:311
  5090.4 8.3 convert_element_type.140
  5098.7 56.4 %reduce-scatter.21.cloned.1.call-done = f32[192,16]{1,0:T(8,128)} async-done(((f32[1536,16]{1,0:T(8,128)}), f32[192,16]{1,0:T(8,128)}) %reduce-scatter.21.cloned.1.call-update) | async-done | bytes 12304
  5162.4 58.3 %reduce-scatter.19.cloned.1.call-done = f32[192,2]{1,0:T(8,128)} async-done(((f32[1536,2]{1,0:T(8,128)}), f32[192,2]{1,0:T(8,128)}) %reduce-scatter.19.cloned.1.call-update) | async-done | bytes 1552
  5221.6 7.8 all-reduce
  5230.6 190.6 %all-reduce.4.cloned.1.call-done = (bf16[192,2560]{1,0:T(8,128)(2,1)}, bf16[192,1536]{1,0:T(8,128)(2,1)}, bf16[16,192,1024]{2,1,0:T(8,128)(2,1)}, bf16[16,64,1536]{2,1,0:T(8,128)(2,1)}) async-done(((bf16[192,2560]{1,0:T(8,128)(2,1)}, bf16[192,1536]{1,0:T(8,128)(2,1)}, bf16[16,192,1024]{2,1,0:T(8,128)(2,1)}, bf16[16,64,1536]{2,1,0:T(8,128)(2,1)}), (bf16[192,2560]{1,0:T(8,128)(2,1)}, ...) | async-done | bytes 11010064 | tf_op jit(solution)/shard_map/psum | solution.py:316
  5426.1 9.3 convert_element_type.141
  (399 shorter events, 368.7 us)
Async XLA Ops:
  7.2 20.5 copy-start
  7.2 120.3 %all-gather.7.cloned.1.call-start = ((), (), s32[]{:S(2)}) async-start(), calls=%async_computation.6 | async-start | bytes 8847360 | tf_op jit(solution)/shard_map/all_gather | solution.py:151
  7.9 625.3 %all-gather.9.cloned.1.call-start = ((), (), s32[]{:S(2)}) async-start(), calls=%async_computation.7 | async-start | bytes 5308416 | tf_op jit(solution)/shard_map/all_gather | solution.py:152
  8.7 17.7 copy-start.13
  8.7 18.8 copy-start.60
  8.7 1180.2 %all-gather.11.cloned.1.call-start = ((), (), s32[]{:S(2)}) async-start(), calls=%async_computation.8 | async-start | bytes 56623104 | tf_op jit(solution)/shard_map/all_gather | solution.py:154
  9.4 1661.6 %all-gather.13.cloned.1.call-start = ((), (), s32[]{:S(2)}) async-start(), calls=%async_computation.9 | async-start | bytes 28311552 | tf_op jit(solution)/shard_map/all_gather | solution.py:155
  10.0 2592.9 %reduce-scatter.13.cloned.1.call-start = ((), (), s32[]{:S(2)}) async-start(), calls=%async_computation.11 | async-start | bytes 10616832 | tf_op jit(solution)/shard_map/reduce_scatter | solution.py:309
  26.4 110.0 %copy-start.50 = (f32[1536]{0:T(1024)}, f32[1536]{0:T(1024)S(1)}, u32[]{:S(2)}) copy-start(f32[1536]{0:T(1024)S(1)} %get-tuple-element.253) | copy-start | bytes 18436
  27.5 109.0 %copy-start.55 = (f32[640]{0:T(1024)}, f32[640]{0:T(1024)S(1)}, u32[]{:S(2)}) copy-start(f32[640]{0:T(1024)S(1)} %get-tuple-element.329) | copy-start | bytes 7684
  138.2 43.7 copy-start.17
  138.4 40.9 collective-permute-start
  139.0 45.5 copy-start.58
  181.0 248.9 %collective-permute-start.1 = (bf16[10,128,1024]{2,1,0:T(8,128)(2,1)}, bf16[10,128,1024]{2,1,0:T(8,128)(2,1)}, u32[]{:S(2)}, u32[]{:S(2)}) collective-permute-start(bf16[10,128,1024]{2,1,0:T(8,128)(2,1)} %maximum_select_fusion.1), channel_id=1, source_target_pairs={{0,2},{2,0},{1,3},{3,1},{4,6},{6,4},{5,7},{7,5},{8,10},{10,8},{9,1... | collective-permute-start | bytes 7864328 | tf_op jit(solution)/shard_map/ppermute | solution.py:31
  181.7 238.3 %copy-start.48 = (s32[50]{0:T(128)}, s32[50]{0:T(128)S(1)}, u32[]{:S(2)}) copy-start(s32[50]{0:T(128)S(1)} %reshape.739) | copy-start | bytes 604
  364.5 19.8 copy-start.53
  384.3 35.6 copy-start.35
  531.9 101.4 %copy-start.14 = (bf16[640,1536]{1,0:T(8,128)(2,1)S(1)}, bf16[640,1536]{1,0:T(8,128)(2,1)}, u32[]{:S(2)}) copy-start(bf16[640,1536]{1,0:T(8,128)(2,1)} %param.15) | copy-start | bytes 5898244
  628.2 12.0 copy-start.9
  628.2 12.0 copy-start.25
  633.3 8.9 copy-start.40
  640.9 21.2 copy-start.44
  642.6 19.5 copy-start.2
  642.6 19.5 copy-start.29
  642.6 20.1 copy-start.38
  662.9 560.9 %copy-start.42 = (f32[640]{0:T(1024)}, f32[640]{0:T(1024)S(1)}, u32[]{:S(2)}) copy-start(f32[640]{0:T(1024)S(1)} %reduce_max.18) | copy-start | bytes 7684
  664.2 559.5 %copy-start.22 = (f32[640,8]{1,0:T(8,128)}, f32[640,8]{1,0:T(8,128)S(1)}, u32[]{:S(2)}) copy-start(f32[640,8]{1,0:T(8,128)S(1)} %copy.128) | copy-start | bytes 61444
  683.9 987.1 %copy-start.31 = (f32[16,352]{1,0:T(8,128)}, f32[16,352]{1,0:T(8,128)S(1)}, u32[]{:S(2)}) copy-start(f32[16,352]{1,0:T(8,128)S(1)} %mul.307) | copy-start | bytes 67588
  1709.6 39.8 copy-start.8
  1835.4 44.7 copy-start.23
  1880.1 16.0 copy-start.28
  1880.1 16.0 copy-start.43
  1880.1 16.0 copy-start.47
  1880.1 16.1 copy-start.39
  1880.2 16.1 copy-start.30
  1880.2 16.1 copy-start.41
  1880.2 16.1 copy-start.45
  1896.3 6.7 copy-start.33
  1896.3 6.7 copy-start.7
  1896.3 6.7 copy-start.12
  1896.3 6.7 copy-start.18
  1928.9 825.8 %reduce-scatter.11.cloned.1.call-start = ((), (), s32[]{:S(2)}) async-start(), calls=%async_computation.10 | async-start | bytes 17694720 | tf_op jit(solution)/shard_map/reduce_scatter | solution.py:308
  1932.8 10.9 copy-start.4
  1970.0 10.9 copy-start.4
  2007.1 10.9 copy-start.4
  2044.4 10.9 copy-start.4
  2081.5 10.9 copy-start.4
  2118.4 10.9 copy-start.4
  2155.2 10.9 copy-start.4
  2192.0 10.9 copy-start.4
  2396.7 58.2 %collective-permute-start.2 = (bf16[10,128,1024]{2,1,0:T(8,128)(2,1)S(1)}, bf16[10,128,1024]{2,1,0:T(8,128)(2,1)S(1)}, u32[]{:S(2)}, u32[]{:S(2)}) collective-permute-start(bf16[10,128,1024]{2,1,0:T(8,128)(2,1)S(1)} %select_convert_fusion), channel_id=1, source_target_pairs={{0,2},{2,0},{1,3},{3,1},{4,6},{6,4},{5,7},{7,5},{8,10},{10,8},{9,1... | collective-permute-start | bytes 7864328 | tf_op jit(solution)/shard_map/ppermute | solution.py:31
  2460.8 30.1 collective-permute-start.3
  2465.3 27.9 copy-start.15
  2465.3 27.9 copy-start.51
  2465.3 27.9 copy-start.56
  2504.9 1043.2 %reduce-scatter.17.cloned.1.call-start = ((), (), s32[]{:S(2)}) async-start(), calls=%async_computation.13 | async-start | bytes 56623104 | tf_op jit(solution)/shard_map/reduce_scatter | solution.py:312
  2538.1 2552.3 %reduce-scatter.15.cloned.1.call-start = ((), (), s32[]{:S(2)}) async-start(), calls=%async_computation.12 | async-start | bytes 113246208 | tf_op jit(solution)/shard_map/reduce_scatter | solution.py:311
  2586.3 2568.8 %reduce-scatter.21.cloned.1.call-start = ((), (), s32[]{:S(2)}) async-start(), calls=%async_computation.15 | async-start | bytes 884736
  2590.9 2629.7 %reduce-scatter.19.cloned.1.call-start = ((), (), s32[]{:S(2)}) async-start(), calls=%async_computation.14 | async-start | bytes 884736
  2602.8 2818.4 %all-reduce.4.cloned.1.call-start = ((), (), s32[]{:S(2)}) async-start(), calls=%async_computation.16 | async-start | bytes 22020096 | tf_op jit(solution)/shard_map/psum | solution.py:316
  5098.7 57.4 %copy-start.16 = (bf16[640,1536]{1,0:T(8,128)(2,1)S(1)}, bf16[640,1536]{1,0:T(8,128)(2,1)}, u32[]{:S(2)}) copy-start(bf16[640,1536]{1,0:T(8,128)(2,1)} %param.15) | copy-start | bytes 5898244
  5098.7 57.4 %copy-start.54 = (f32[640]{0:T(1024)S(1)}, f32[640]{0:T(1024)}, u32[]{:S(2)}) copy-start(f32[640]{0:T(1024)} %get-tuple-element.328) | copy-start | bytes 7684
  5426.1 9.3 copy-start.21
  5426.1 12.9 copy-start.1
  (27 other events, 78.0 us)
Sparse Core Ops, SparseCore 0:
  10.2 117.2 all-gather.6
  129.7 101.2 all-gather.8
  232.5 956.3 all-gather.10
  1190.3 480.6 all-gather.12
  1929.0 161.7 reduce-scatter.12
  2505.0 249.6 reduce-scatter.10
  2758.6 789.4 reduce-scatter.16
  3552.4 1537.9 reduce-scatter.14
  5093.7 61.4 reduce-scatter.20
  5159.2 61.3 reduce-scatter.18
  5224.0 197.1 all-reduce.3
where the time goes:
time: 5460 us; the launch traced here: 5450 us
  waiting for transfers between devices  3950 us (72%)
  matrix products  554 us (10%)
  local copies, waits for them, and re-layouts  420 us (8%)
  other arithmetic  298 us (5%)
  blocking collectives  202 us (4%)
    reduce_scatter x1, waiting for transfers between devices, shards(): lax.psum_scatter(gate_up_grad, 'shard', scatter_dimension=1, tiled=True)  1540 us
    reduce_scatter x1, waiting for transfers between devices, shards(): lax.psum_scatter(down_grad, 'shard', scatter_dimension=1, tiled=True)  791 us
    all_gather x1, waiting for transfers between devices, shards(): lax.all_gather(gate_up_weight, 'shard', axis=1, tiled=True)  505 us
    all_gather x1, waiting for transfers between devices, shards(): lax.all_gather(down_weight, 'shard', axis=1, tiled=True)  447 us
    psum x1, waiting for transfers between devices, shards(): lax.psum(shares[1].astype(jnp.bfloat16), 'rep').astype(jnp.float32)  191 us
    all_gather x1, blocking collectives, shards(): lax.all_gather(router_weight, 'shard', axis=0, tiled=True)  179 us
    reduce_scatter x1, waiting for transfers between devices, shards(): lax.psum_scatter(qkv_grad, 'shard', scatter_dimension=0, tiled=True)  150 us
    ppermute x4, waiting for transfers between devices, partner(): return lax.ppermute(block, axis, route)  124 us
  transfers between devices with their start and end apart: 15, of which 12 were waited for; matrix products, arithmetic and copies ran while one was open for 18% of the time, Pallas kernels for 0%

commit v1 on v0

--- a/solution.py
+++ b/solution.py
@@ -105,6 +105,27 @@
         * scale
     )
     return (query_grad.astype(jnp.bfloat16), key_grad, value_grad)
+
+
+def gather_columns(weight, rep_index, rep_count):
+    width = weight.shape[1] // rep_count
+    own = lax.dynamic_slice_in_dim(weight, rep_index * width, width, axis=1)
+    part = lax.all_gather(own, "shard", axis=0, tiled=True)
+    return lax.all_gather(part, "rep", axis=0)
+
+
+def spread_experts(grad):
+    share = lax.psum_scatter(grad.astype(jnp.bfloat16), "shard", scatter_dimension=1, tiled=True)
+    return lax.all_gather(share, "rep", axis=0, tiled=True).astype(jnp.float32)
+
+
+def spread_columns(grad, rep_count):
+    rows, width = grad.shape
+    pieces = grad.astype(jnp.bfloat16).reshape(rows, rep_count, width // rep_count).transpose(1, 0, 2)
+    part = lax.psum_scatter(pieces, "rep", scatter_dimension=0, tiled=True)[0]
+    share = lax.psum_scatter(part, "shard", scatter_dimension=0, tiled=True)
+    whole = lax.all_gather(share, "rep", axis=1, tiled=True)
+    return whole.astype(jnp.float32)
 
 
 def shards(
@@ -146,21 +167,27 @@
     mask = level_alive[:, None, :] & (
         (key_level[None, None, :] > 0) | (key_pos[None, None, :] <= query_pos[None, :, None])
     )
-    gathered = (
-        lax.all_gather(norm_gains, "shard", axis=1, tiled=True),
-        lax.all_gather(qkv_weight, "shard", axis=0, tiled=True),
-        lax.all_gather(out_weight, "shard", axis=0, tiled=True),
-        lax.all_gather(router_weight, "shard", axis=0, tiled=True),
-        lax.all_gather(gate_up_weight, "shard", axis=1, tiled=True),
-        lax.all_gather(down_weight, "shard", axis=1, tiled=True),
-    )
-    gains, w_qkv, w_out, w_router, w_gate_up, w_down = gathered
+    rep_count = lax.axis_size("rep")
+    own_experts = E // rep_count
+    first_expert = rep_index * own_experts
+    gains = lax.all_gather(norm_gains, "shard", axis=1, tiled=True)
+    w_router = lax.all_gather(router_weight, "shard", axis=0, tiled=True)
+    w_qkv = gather_columns(qkv_weight, rep_index, rep_count)
+    w_out = gather_columns(out_weight, rep_index, rep_count)
+    w_gate_up = lax.all_gather(
+        lax.dynamic_slice_in_dim(gate_up_weight, first_expert, own_experts), "shard", axis=1, tiled=True
+    )
+    w_down = lax.all_gather(
+        lax.dynamic_slice_in_dim(down_weight, first_expert, own_experts), "shard", axis=1, tiled=True
+    )
+    cot_all = lax.all_gather(cotangent, "rep", axis=0, tiled=True)
     gain_first = gains[0].astype(jnp.float32)
     gain_second = gains[1].astype(jnp.float32)
     token_values = tokens.astype(jnp.float32)
     normed_first, scale_first = norm_rows(token_values, gain_first)
     act_first = normed_first.astype(jnp.bfloat16)
-    projected = jnp.dot(act_first, w_qkv, preferred_element_type=jnp.float32)
+    projected = jnp.einsum("td,rdc->trc", act_first, w_qkv, preferred_element_type=jnp.float32)
+    projected = projected.reshape(token_count, width_q + 2 * width_kv)
     queries = projected[:, :width_q].astype(jnp.bfloat16)
     own_kv = projected[:, width_q:].astype(jnp.bfloat16).reshape(seg_dev, SEG, 2 * width_kv)
     low_first = member % 2 == 0
@@ -186,7 +213,8 @@
         lambda operands: head_forward(operands, mask, scale), (head_queries, head_keys, head_values)
     )
     attended = mixed.transpose(1, 3, 0, 2, 4).reshape(token_count, width_q)
-    residual = token_values + jnp.dot(attended, w_out, preferred_element_type=jnp.float32)
+    mixed_out = jnp.einsum("td,rdc->trc", attended, w_out, preferred_element_type=jnp.float32)
+    residual = token_values + mixed_out.reshape(token_count, D)
     normed_second, scale_second = norm_rows(residual, gain_second)
     act_second = normed_second.astype(jnp.bfloat16)
     logits = jnp.dot(act_second, w_router, preferred_element_type=jnp.float32)
@@ -194,81 +222,70 @@
     picks = routes[:, :, None] == expert_ids[None, None, :]
     chosen = jnp.sum(jnp.where(picks, logits[:, None, :], 0.0), axis=-1)
     gates = jax.nn.softmax(chosen, axis=-1)
-    flat_picks = picks.reshape(token_count * TOP, E).astype(jnp.int32)
-    before = jnp.cumsum(flat_picks, axis=0) - flat_picks
-    place_in = jnp.sum(before * flat_picks, axis=1)
-    slots = routes.reshape(-1) * CAP + place_in
-    sources = jnp.arange(token_count * TOP, dtype=jnp.int32) // TOP
-    slot_token = jnp.zeros((E * CAP,), jnp.int32).at[slots].set(sources)
-    slot_gate = jnp.zeros((E * CAP,), jnp.float32).at[slots].set(gates.reshape(-1))
-    dispatched = act_second[slot_token].reshape(E, CAP, D)
-    gate_up = jnp.einsum("ecd,edf->ecf", dispatched, w_gate_up, preferred_element_type=jnp.float32)
-    hidden = (jax.nn.silu(gate_up[..., :FF]) * gate_up[..., FF:]).astype(jnp.bfloat16)
-    expert_out = jnp.einsum(
-        "ecf,efd->ecd", hidden, w_down, preferred_element_type=jnp.float32
-    ).reshape(E * CAP, D)
-    slot_rows = slots.reshape(token_count, TOP)
-    picked = expert_out[slot_rows]
-    mixture = jnp.sum(gates[:, :, None] * picked, axis=1)
-    block_out = (residual + mixture).astype(jnp.bfloat16)
     upstream = cotangent.astype(jnp.float32)
-    gate_grads = jnp.sum(picked * upstream[:, None, :], axis=-1)
-    back_weights = (
-        lax.all_gather(norm_gains, "shard", axis=1, tiled=True),
-        lax.all_gather(qkv_weight, "shard", axis=0, tiled=True),
-        lax.all_gather(out_weight, "shard", axis=0, tiled=True),
-        lax.all_gather(router_weight, "shard", axis=0, tiled=True),
-        lax.all_gather(gate_up_weight, "shard", axis=1, tiled=True),
-        lax.all_gather(down_weight, "shard", axis=1, tiled=True),
-    )
-    back_gains, back_qkv, back_out, back_router, back_gate_up, back_down = back_weights
-    chosen_grad = gates * (gate_grads - jnp.sum(gates * gate_grads, axis=-1, keepdims=True))
-    logit_grad = jnp.sum(jnp.where(picks, chosen_grad[:, :, None], 0.0), axis=1)
+    gate_table = jnp.sum(jnp.where(picks, gates[:, :, None], 0.0), axis=1)
+    act_all = lax.all_gather(act_second, "rep", axis=0, tiled=True)
+    gate_all = lax.all_gather(gate_table, "rep", axis=0, tiled=True)
+    own_gate = lax.dynamic_slice_in_dim(gate_all, first_expert, own_experts, axis=1).T[:, :, None]
+    gate_up = jnp.einsum("td,edf->etf", act_all, w_gate_up, preferred_element_type=jnp.float32)
+    gate_part = gate_up[..., :FF]
+    up_part = gate_up[..., FF:]
+    sig_gate = jax.nn.sigmoid(gate_part)
+    hidden = gate_part * sig_gate * up_part
+    gated = (hidden * own_gate).astype(jnp.bfloat16)
+    mix_part = jnp.einsum("etf,efd->td", gated, w_down, preferred_element_type=jnp.float32)
+    mixture = lax.psum_scatter(mix_part.astype(jnp.bfloat16), "rep", scatter_dimension=0, tiled=True)
+    block_out = (residual + mixture.astype(jnp.float32)).astype(jnp.bfloat16)
+    raw_grad = jnp.einsum("td,efd->etf", cot_all, w_down, preferred_element_type=jnp.float32)
+    gate_grad_own = jnp.sum(hidden * raw_grad, axis=-1)
+    gate_grad_all = lax.all_gather(gate_grad_own, "rep", axis=0, tiled=True)
+    gate_grad_table = lax.dynamic_slice_in_dim(
+        gate_grad_all, rep_index * token_count, token_count, axis=1
+    ).T
+    inner_gate = jnp.sum(gate_table * gate_grad_table, axis=-1, keepdims=True)
+    logit_grad = gate_table * (gate_grad_table - inner_gate)
     router_grad = jnp.dot(
         act_second.astype(jnp.float32).T,
         logit_grad,
         precision=lax.Precision.HIGHEST,
         preferred_element_type=jnp.float32,
     )
-    out_slot_grad = (
-        (slot_gate[:, None] * upstream[slot_token]).astype(jnp.bfloat16).reshape(E, CAP, D)
-    )
-    gate_part = gate_up[..., :FF]
-    up_part = gate_up[..., FF:]
-    sig_gate = jax.nn.sigmoid(gate_part)
-    hidden_grad = jnp.einsum(
-        "ecd,efd->ecf", out_slot_grad, back_down, preferred_element_type=jnp.float32
-    )
+    hidden_grad = raw_grad * own_gate
     gate_grad_part = hidden_grad * up_part * sig_gate * (1.0 + gate_part * (1.0 - sig_gate))
     up_grad_part = hidden_grad * gate_part * sig_gate
-    gate_up_grad_slots = jnp.concatenate([gate_grad_part, up_grad_part], axis=-1).astype(
+    gate_up_grad_rows = jnp.concatenate([gate_grad_part, up_grad_part], axis=-1).astype(
         jnp.bfloat16
     )
-    down_grad = jnp.einsum(
-        "ecf,ecd->efd", hidden, out_slot_grad, preferred_element_type=jnp.float32
-    )
+    down_grad = jnp.einsum("etf,td->efd", gated, cot_all, preferred_element_type=jnp.float32)
     gate_up_grad = jnp.einsum(
-        "ecd,ecf->edf", dispatched, gate_up_grad_slots, preferred_element_type=jnp.float32
-    )
-    dispatched_grad = jnp.einsum(
-        "ecf,edf->ecd", gate_up_grad_slots, back_gate_up, preferred_element_type=jnp.float32
-    ).reshape(E * CAP, D)
-    act_second_grad = jnp.sum(dispatched_grad[slot_rows], axis=1)
+        "td,etf->edf", act_all, gate_up_grad_rows, preferred_element_type=jnp.float32
+    )
+    down_grad = spread_experts(down_grad)
+    gate_up_grad = spread_experts(gate_up_grad)
+    act_part = jnp.einsum(
+        "etf,edf->td", gate_up_grad_rows, w_gate_up, preferred_element_type=jnp.float32
+    )
+    act_second_grad = lax.psum_scatter(
+        act_part.astype(jnp.bfloat16), "rep", scatter_dimension=0, tiled=True
+    ).astype(jnp.float32)
     act_second_grad = act_second_grad + jnp.dot(
         logit_grad,
-        back_router.astype(jnp.float32).T,
+        w_router.astype(jnp.float32).T,
         precision=lax.Precision.HIGHEST,
         preferred_element_type=jnp.float32,
     )
     through_second, gain_grad_second = norm_back(
-        residual, scale_second, back_gains[1].astype(jnp.float32), act_second_grad
+        residual, scale_second, gains[1].astype(jnp.float32), act_second_grad
     )
     residual_grad = upstream + through_second
     branch_grad = residual_grad.astype(jnp.bfloat16)
     out_grad = jnp.dot(attended.T, branch_grad, preferred_element_type=jnp.float32)
-    attended_grad = jnp.dot(branch_grad, back_out.T, preferred_element_type=jnp.float32).astype(
-        jnp.bfloat16
-    )
+    attended_grad = jnp.einsum(
+        "trc,rdc->td",
+        branch_grad.reshape(token_count, rep_count, D // rep_count),
+        w_out,
+        preferred_element_type=jnp.float32,
+    ).astype(jnp.bfloat16)
     head_upstream = attended_grad.reshape(seg_dev, SEG, KVH, groups_per, HD).transpose(
         2, 0, 3, 1, 4
     )
@@ -297,29 +314,23 @@
         [query_grad, own_grad.reshape(token_count, 2 * width_kv).astype(jnp.bfloat16)], axis=1
     )
     qkv_grad = jnp.dot(act_first.T, projected_grad, preferred_element_type=jnp.float32)
-    act_first_grad = jnp.dot(projected_grad, back_qkv.T, preferred_element_type=jnp.float32)
+    act_first_grad = jnp.einsum(
+        "trc,rdc->td",
+        projected_grad.reshape(token_count, rep_count, -1),
+        w_qkv,
+        preferred_element_type=jnp.float32,
+    )
     through_first, gain_grad_first = norm_back(
-        token_values, scale_first, back_gains[0].astype(jnp.float32), act_first_grad
+        token_values, scale_first, gains[0].astype(jnp.float32), act_first_grad
     )
     token_grad = residual_grad + through_first
-    gains_grad = jnp.stack([gain_grad_first, gain_grad_second], axis=0)
-    shares = (
-        lax.psum_scatter(gains_grad, "shard", scatter_dimension=1, tiled=True),
-        lax.psum_scatter(qkv_grad, "shard", scatter_dimension=0, tiled=True),
-        lax.psum_scatter(out_grad, "shard", scatter_dimension=0, tiled=True),
-        lax.psum_scatter(router_grad, "shard", scatter_dimension=0, tiled=True),
-        lax.psum_scatter(gate_up_grad, "shard", scatter_dimension=1, tiled=True),
-        lax.psum_scatter(down_grad, "shard", scatter_dimension=1, tiled=True),
-    )
-    totals = (
-        lax.psum(shares[0].astype(jnp.bfloat16), "rep").astype(jnp.float32),
-        lax.psum(shares[1].astype(jnp.bfloat16), "rep").astype(jnp.float32),
-        lax.psum(shares[2].astype(jnp.bfloat16), "rep").astype(jnp.float32),
-        lax.psum(shares[3].astype(jnp.bfloat16), "rep").astype(jnp.float32),
-        lax.psum(shares[4].astype(jnp.bfloat16), "rep").astype(jnp.float32),
-        lax.psum(shares[5].astype(jnp.bfloat16), "rep").astype(jnp.float32),
-    )
-    return (block_out, token_grad, totals[0], totals[1], totals[2], totals[3], totals[4], totals[5])
+    gains_grad = jnp.stack([gain_grad_first, gain_grad_second], axis=1)
+    small = jnp.concatenate([gains_grad, router_grad], axis=1)
+    small = lax.psum_scatter(small, "shard", scatter_dimension=0, tiled=True)
+    small = lax.psum(small, "rep")
+    qkv_grad = spread_columns(qkv_grad, rep_count)
+    out_grad = spread_columns(out_grad, rep_count)
+    return (block_out, token_grad, small[:, :2].T, qkv_grad, out_grad, small[:, 2:], gate_up_grad, down_grad)
 
 
 def solution(mesh):

time: 5460 us -> 1990 us (0.36)
  waiting for transfers between devices: 3950 us -> 766 us
  local copies, waits for them, and re-layouts: 420 us -> 294 us
  blocking collectives: 202 us -> 88.9 us
    reduce_scatter x4 -> x7, waiting for transfers between devices: 2480 us -> 177 us  [the longest x2 114 us: spread_columns(): share = lax.psum_scatter(part, 'shard', scatter_dimension=0, tiled=True)]
    all_gather x4 -> x10, waiting for transfers between devices: 1040 us -> 325 us  [the longest x2 90.1 us: gather_columns(): part = lax.all_gather(own, 'shard', axis=0, tiled=True)]
    psum x1 -> x0, waiting for transfers between devices: 191 us -> none  [shards(): lax.psum(shares[1].astype(jnp.bfloat16), 'rep').astype(jnp.float32)]
    gather x4 -> x0, local copies, waits for them, and re-layouts: 144 us -> none  [the longest x1 44.7 us: shards(): picked = expert_out[slot_rows]]
    all_gather x2 -> x6, blocking collectives: 194 us -> 76.5 us  [the longest x1 21.9 us: shards(): w_router = lax.all_gather(router_weight, 'shard', axis=0, tiled=True)]
    ppermute x4, waiting for transfers between devices: 124 us -> 210 us  [partner(): return lax.ppermute(block, axis, route)]
    unnamed x13 -> x21, waiting for transfers between devices: 117 us -> 55.5 us
    dot_general x11 -> x12, matrix products: 259 us -> 255 us  [the longest x1 41.9 us: shards(): jnp.einsum('td,efd->etf', cot_all, w_down, preferred_element_type=jnp.flo...]
  transfers between devices with their start and end apart: 15 -> 23, of which waited for: 12 -> 17; matrix products, arithmetic and copies ran while one was open for 18% -> 51% of each run, Pallas kernels for 0% -> 0%
where the time goes in v1:
time: 1990 us; the launch traced here: 1970 us
  waiting for transfers between devices  766 us (38%)
  matrix products  548 us (28%)
  local copies, waits for them, and re-layouts  294 us (15%)
  other arithmetic  252 us (13%)
  blocking collectives  88.9 us (4%)
    ppermute x4, waiting for transfers between devices, partner(): return lax.ppermute(block, axis, route)  210 us
    reduce_scatter x2, waiting for transfers between devices, spread_columns(): share = lax.psum_scatter(part, 'shard', scatter_dimension=0, tiled=True)  114 us
    dot_general x16, matrix products, head_scores(): jnp.einsum('sgqd,skd->sgqk', queries, keys, preferred_element_type=jnp.fl...  104 us
    all_gather x2, waiting for transfers between devices, gather_columns(): part = lax.all_gather(own, 'shard', axis=0, tiled=True)  90.1 us
    reshape x2, local copies, waits for them, and re-layouts, shards(): path_grad = jnp.stack([key_grad, value_grad], axis=1).transpose(2, 3, 1,...  86.5 us
    convert_element_type x8, other arithmetic, head_backward(): score_grad = (probs * (prob_grad - inner)).astype(jnp.bfloat16)  79.8 us
    all_gather x2, waiting for transfers between devices, spread_experts(): return lax.all_gather(share, 'rep', axis=0, tiled=True).astype(jnp.float32)  65.7 us
    all_gather x1, waiting for transfers between devices, shards(): cot_all = lax.all_gather(cotangent, 'rep', axis=0, tiled=True)  57.8 us
  transfers between devices with their start and end apart: 23, of which 17 were waited for; matrix products, arithmetic and copies ran while one was open for 51% of the time, Pallas kernels for 0%

profile of v1, /device:TPU:9, one launch (start us, length us, event | category | flops | bytes accessed | tf_op | source)
XLA Modules:
  0.0 1971.9 jit_solution(907492801094239132)
XLA Ops:
  10.8 48.6 %all-gather.16.cloned.1.call-done = bf16[1536,640]{1,0:T(8,128)(2,1)} async-done(((bf16[192,640]{1,0:T(8,128)(2,1)}), bf16[1536,640]{1,0:T(8,128)(2,1)}) %all-gather.16.cloned.1.call-update) | async-done | bytes 1966096 | tf_op jit(solution)/shard_map/all_gather | solution.py:113
  59.5 41.6 %all-gather.18.cloned.1.call-done = bf16[1536,384]{1,0:T(8,128)(2,1)} async-done(((bf16[192,384]{1,0:T(8,128)(2,1)}), bf16[1536,384]{1,0:T(8,128)(2,1)}) %all-gather.18.cloned.1.call-update) | async-done | bytes 1179664 | tf_op jit(solution)/shard_map/all_gather | solution.py:113
  106.3 12.5 all-gather.2
  122.2 36.4 %all-gather.32.cloned.1.call-done = bf16[6144,640]{1,0:T(8,128)(2,1)} async-done(((bf16[1536,640]{1,0:T(8,128)(2,1)}), bf16[6144,640]{1,0:T(8,128)(2,1)}) %all-gather.32.cloned.1.call-update) | async-done | bytes 7864336 | tf_op jit(solution)/shard_map/all_gather | solution.py:114
  158.6 9.5 convolution_convert_fusion.3
  175.5 28.5 %collective-permute-done = bf16[5,128,1024]{2,1,0:T(8,128)(2,1)} collective-permute-done((bf16[5,128,1024]{2,1,0:T(8,128)(2,1)}, bf16[5,128,1024]{2,1,0:T(8,128)(2,1)}, u32[]{:S(2)}, u32[]{:S(2)}) %collective-permute-start) | collective-permute-done | bytes 1310752 | tf_op jit(solution)/shard_map/ppermute | solution.py:31
  228.2 89.0 %collective-permute-done.1 = bf16[10,128,1024]{2,1,0:T(8,128)(2,1)} collective-permute-done((bf16[10,128,1024]{2,1,0:T(8,128)(2,1)}, bf16[10,128,1024]{2,1,0:T(8,128)(2,1)}, u32[]{:S(2)}, u32[]{:S(2)}) %collective-permute-start.1) | collective-permute-done | bytes 2621472 | tf_op jit(solution)/shard_map/ppermute | solution.py:31
  317.2 7.2 maximum_select_fusion
  324.4 9.0 gather_fusion
  333.4 20.5 %copy.124 = bf16[50,128,1024]{1,0,2:T(8,128)(2,1)} copy(bf16[50,128,1024]{2,1,0:T(8,128)(2,1)} %gather_fusion) | data formatting | bytes 26214400 | tf_op jit(solution)/shard_map/gather | solution.py:207
  353.9 30.3 %reshape.627 = bf16[5,1280,2,8,64]{1,0,4,3,2:T(8,128)(2,1)} reshape(bf16[50,128,1024]{1,0,2:T(8,128)(2,1)} %copy.124) | data formatting | bytes 26214400 | tf_op jit(solution)/shard_map/reshape | solution.py:207
  384.2 16.5 slice_bitcast_fusion
  400.6 8.5 copy.127
  409.1 8.5 copy.128
  419.4 96.1 %while.28 = (s32[]{:T(128)}, bf16[8,5,3,128,64]{3,4,2,1,0:T(8,128)(2,1)}, f32[8,5,3,128,1]{3,2,1,4,0:T(4,128)}, bf16[8,5,3,128,64]{3,4,2,1,0:T(8,128)(2,1)}, bf1...) while((s32[]{:T(128)}, ...), condition=%wide.region_23.24_spmd.clone, body=%wide.region_20.23_spmd.clone.sunk | while | flops 659576960 | bytes 35134812 | solution.py:212
  531.0 21.9 %all-gather.3 = bf16[8,192,16]{1,2,0:T(8,128)(2,1)S(1)} all-gather(bf16[1,192,16]{1,2,0:T(8,128)(2,1)S(1)} %bitcast.341), channel_id=1, replica_groups=mesh['rep'=4,'shard'=8] {'shard'}, dimensions={0}, use_global_device_ids=true | all-gather | bytes 55296 | tf_op jit(solution)/shard_map/all_gather | solution.py:174
  555.4 13.8 all_gather.64
  569.3 17.0 all-gather.22.cloned.1.call-done
  586.3 41.5 %convolution_bitcast_fusion.1 = f32[4,2560,1024]{1,2,0:T(8,128)} fusion(bf16[4,1536,1024]{2,1,0:T(8,128)(2,1)} %all-gather.20.cloned.1.call-done, bf16[2560,1536]{1,0:T(8,128)(2,1)} %all-gather.22.cloned.1.call-done), kind=kOutput, calls=%fused_computation.64 | convolution fusion | flops 32212254720 | bytes 62390272 | tf_op jit(solution)/shard_map/td,edf->etf/dot_general | solution.py:230
  627.8 57.6 %all-gather.24.cloned.1.call-done = bf16[4,512,1536]{2,1,0:T(8,128)(2,1)} async-done(((bf16[4,64,1536]{2,1,0:T(8,128)(2,1)}), bf16[4,512,1536]{2,1,0:T(8,128)(2,1)}) %all-gather.24.cloned.1.call-update) | async-done | bytes 6291472 | tf_op jit(solution)/shard_map/all_gather | solution.py:180
  685.4 57.8 %all-gather.26.cloned.1.call-done = bf16[2560,1536]{1,0:T(8,128)(2,1)} async-done(((bf16[640,1536]{1,0:T(8,128)(2,1)}), bf16[2560,1536]{1,0:T(8,128)(2,1)}) %all-gather.26.cloned.1.call-update) | async-done | bytes 7864336 | tf_op jit(solution)/shard_map/all_gather | solution.py:183
  743.2 41.9 %multiply_convert_fusion.2 = (bf16[4,2560,512]{1,2,0:T(8,128)(2,1)}, bf16[4,2560,512]{1,2,0:T(8,128)(2,1)}, f32[4,2560]{1,0:T(4,128)}, f32[4,2560,512]{1,2,0:T(8,128)}) fusion(f32[4,2560,1024]{1,2,0:T(8,128)} %convolution_bitcast_fusion.1, f32[4,2560]{1,0:T(4,128)S(1)} %dynamic-slice_bitcast_fusion.1, ...), kind=kOutput, calls=%fused_computation.70 | convolution fusion | flops 16200488960 | bytes 98123776 | tf_op jit(solution)/shard_map/td,efd->etf/dot_general | solution.py:239
  785.1 40.9 %bitcast_convert_fusion = bf16[2560,1536]{1,0:T(8,128)(2,1)} fusion(bf16[4,1536,1024]{2,1,0:T(8,128)(2,1)} %all-gather.20.cloned.1.call-done, bf16[4,2560,512]{1,2,0:T(8,128)(2,1)} %get-tuple-element.321, bf16[4,2560,512]{1,2,0:T(8,128)(2,1)} %get-tuple-element.320), kind=kOutput, calls=%fused_computation.74 | convolution fusion | flops 32258129920 | bytes 41418752 | tf_op jit(solution)/shard_map/etf,edf->td/dot_general | solution.py:265
  826.1 25.2 %bitcast_convert_fusion.1 = bf16[2560,1536]{1,0:T(8,128)(2,1)} fusion(bf16[4,512,1536]{2,1,0:T(8,128)(2,1)} %all-gather.24.cloned.1.call-done, f32[4,2560,512]{1,2,0:T(8,128)} %get-tuple-element.323, f32[4,2560]{1,0:T(4,128)S(1)} %dynamic-slice_bitcast_fusion.1), kind=kOutput, calls=%fused_computation.75 | convolution fusion | flops 16120545280 | bytes 35168256 | tf_op jit(solution)/shard_map/etf,efd->td/dot_general | solution.py:236
  851.4 23.8 %fusion.64 = bf16[4,512,1536]{2,1,0:T(8,128)(2,1)} fusion(bf16[2560,1536]{1,0:T(8,128)(2,1)} %all-gather.26.cloned.1.call-done, f32[4,2560,512]{1,2,0:T(8,128)} %get-tuple-element.323, f32[4,2560]{1,0:T(4,128)S(1)} %dynamic-slice_bitcast_fusion.1), kind=kOutput, calls=%fused_computation.96 | convolution fusion | flops 16119758848 | bytes 35168256 | tf_op jit(solution)/shard_map/etf,td->efd/dot_general | solution.py:259
  875.3 40.0 %fusion.57 = bf16[4,1536,1024]{1,2,0:T(8,128)(2,1)} fusion(bf16[4,2560,512]{1,2,0:T(8,128)(2,1)} %get-tuple-element.321, bf16[4,2560,512]{1,2,0:T(8,128)(2,1)} %get-tuple-element.320, bf16[2560,1536]{1,0:T(8,128)(2,1)} %all-gather.22.cloned.1.call-done), kind=kOutput, calls=%fused_computation.79 | convolution fusion | flops 32260489216 | bytes 41418752 | tf_op jit(solution)/shard_map/td,etf->edf/dot_general | solution.py:260
  915.3 21.9 %copy.147 = bf16[4,1536,1024]{2,0,1:T(4,128)(2,1)} copy(bf16[4,1536,1024]{1,2,0:T(8,128)(2,1)} %fusion.57) | data formatting | bytes 25165824 | tf_op jit(solution)/shard_map/convert_element_type | solution.py:118
  944.9 8.1 multiply_reduce_fusion.1
  953.1 14.2 reduce-scatter.11.cloned.1.call-done
  1003.2 298.3 %while.29 = (s32[]{:T(128)}, bf16[8,5,3,128,64]{3,4,2,1,0:T(8,128)(2,1)S(1)}, f32[8,5,1280,64]{2,3,1,0:T(8,128)}, f32[8,5,1280,64]{2,3,1,0:T(8,128)}, bf16[8,5,3...) while((s32[]{:T(128)}, ...), condition=%wide.region_36.37_spmd.clone, body=%wide.region_34.36_spmd.clone.sunk | while | flops 1596455040 | bytes 136610768 | solution.py:292
  1007.2 9.7 multiply_reduce_fusion.5
  1016.9 10.0 multiply_convert_fusion.8
  1044.6 9.7 multiply_reduce_fusion.5
  1054.3 9.8 multiply_convert_fusion.8
  1081.6 9.7 multiply_reduce_fusion.5
  1091.3 9.8 multiply_convert_fusion.8
  1118.5 9.7 multiply_reduce_fusion.5
  1128.2 9.9 multiply_convert_fusion.8
  1156.1 9.7 multiply_reduce_fusion.5
  1165.7 10.0 multiply_convert_fusion.8
  1193.3 9.7 multiply_reduce_fusion.5
  1203.0 9.9 multiply_convert_fusion.8
  1230.6 9.7 multiply_reduce_fusion.5
  1240.2 10.5 multiply_convert_fusion.8
  1268.3 9.7 multiply_reduce_fusion.5
  1278.0 9.9 multiply_convert_fusion.8
  1301.6 19.9 %maximum_bitcast_fusion = f32[5,1280,2,8,64]{1,4,0,3,2:T(8,128)} fusion(f32[8,1,5,1280,64]{3,4,2,0,1:T(8,128)} %bitcast.315, f32[8,1,5,1280,64]{3,4,2,0,1:T(8,128)} %bitcast.314), kind=kLoop, calls=%fused_computation.63 | loop fusion | flops 6553600 | bytes 52428800 | tf_op jit(solution)/shard_map/transpose | solution.py:299
  1321.4 42.5 %copy.159 = f32[5,1280,2,8,64]{4,3,2,1,0:T(8,128)} copy(f32[5,1280,2,8,64]{1,4,0,3,2:T(8,128)} %maximum_bitcast_fusion) | data formatting | bytes 52428800 | tf_op jit(solution)/shard_map/reshape | solution.py:300
  1363.9 44.0 %reshape.680 = f32[50,128,1024]{2,1,0:T(8,128)} reshape(f32[5,1280,2,8,64]{4,3,2,1,0:T(8,128)} %copy.159) | data formatting | bytes 52428800 | tf_op jit(solution)/shard_map/reshape | solution.py:300
  1413.4 56.9 %scatter_fusion = f32[20,128,1024]{2,1,0:T(8,128)} fusion(f32[20,128,1024]{2,1,0:T(8,128)} %broadcast_in_dim.292, s32[50]{0:T(128)S(1)} %copy-done.34, f32[50,128,1024]{2,1,0:T(8,128)} %reshape.680), kind=kCustom, calls=%fused_computation.1 | custom fusion | flops 6553600 | bytes 78643400 | tf_op jit(solution)/shard_map/scatter-add | solution.py:303
  1475.8 67.5 %collective-permute-done.2 = bf16[10,128,1024]{2,1,0:T(8,128)(2,1)S(1)} collective-permute-done((bf16[10,128,1024]{2,1,0:T(8,128)(2,1)S(1)}, bf16[10,128,1024]{2,1,0:T(8,128)(2,1)S(1)}, u32[]{:S(2)}, u32[]{:S(2)}) %collective-permute-start.2) | collective-permute-done | bytes 2621472 | tf_op jit(solution)/shard_map/ppermute | solution.py:31
  1555.1 24.7 %collective-permute-done.3 = bf16[5,128,1024]{2,1,0:T(8,128)(2,1)S(1)} collective-permute-done((bf16[5,128,1024]{2,1,0:T(8,128)(2,1)S(1)}, bf16[5,128,1024]{2,1,0:T(8,128)(2,1)S(1)}, u32[]{:S(2)}, u32[]{:S(2)}) %collective-permute-start.3) | collective-permute-done | bytes 1310752 | tf_op jit(solution)/shard_map/ppermute | solution.py:31
  1584.2 10.9 convolution_convert_fusion.1
  1607.7 9.9 fusion.75
  1624.5 48.7 %reduce-scatter.15.cloned.1.call-done = bf16[1,1536,640]{2,1,0:T(8,128)(2,1)} async-done(((bf16[4,1536,640]{2,1,0:T(8,128)(2,1)}), bf16[1,1536,640]{2,1,0:T(8,128)(2,1)}) %reduce-scatter.15.cloned.1.call-update) | async-done | bytes 1966096 | tf_op jit(solution)/shard_map/reduce_scatter | solution.py:125
  1673.3 30.4 %all-gather.30.cloned.1.call-done = bf16[16,64,1536]{2,1,0:T(8,128)(2,1)} async-done(((bf16[4,64,1536]{2,1,0:T(8,128)(2,1)}), bf16[16,64,1536]{2,1,0:T(8,128)(2,1)}) %all-gather.30.cloned.1.call-update) | async-done | bytes 3145744 | tf_op jit(solution)/shard_map/all_gather | solution.py:119
  1714.3 53.5 %reduce-scatter.25.cloned.1.call-done = f32[192,18]{1,0:T(8,128)} async-done(((f32[1536,18]{1,0:T(8,128)}), f32[192,18]{1,0:T(8,128)}) %reduce-scatter.25.cloned.1.call-update) | async-done | bytes 13840
  1768.8 12.4 psum.7
  1782.4 35.3 %all-gather.28.cloned.1.call-done = bf16[16,192,1024]{2,1,0:T(8,128)(2,1)} async-done(((bf16[4,192,1024]{2,1,0:T(8,128)(2,1)}), bf16[16,192,1024]{2,1,0:T(8,128)(2,1)}) %all-gather.28.cloned.1.call-update) | async-done | bytes 6291472 | tf_op jit(solution)/shard_map/all_gather | solution.py:119
  1817.7 9.3 convert_element_type.131
  1827.0 55.6 %reduce-scatter.21.cloned.1.call-done = bf16[192,384]{1,0:T(8,128)(2,1)} async-done(((bf16[1536,384]{1,0:T(8,128)(2,1)}), bf16[192,384]{1,0:T(8,128)(2,1)}) %reduce-scatter.21.cloned.1.call-update) | async-done | bytes 147472 | tf_op jit(solution)/shard_map/reduce_scatter | solution.py:126
  1882.6 10.1 all_gather.69
  1893.8 58.2 %reduce-scatter.17.cloned.1.call-done = bf16[192,640]{1,0:T(8,128)(2,1)} async-done(((bf16[1536,640]{1,0:T(8,128)(2,1)}), bf16[192,640]{1,0:T(8,128)(2,1)}) %reduce-scatter.17.cloned.1.call-update) | async-done | bytes 245776 | tf_op jit(solution)/shard_map/reduce_scatter | solution.py:126
  1952.0 11.5 all_gather.68
  (405 shorter events, 404.6 us)
Async XLA Ops:
  7.2 522.1 %copy-start = (bf16[16,64,1536]{2,1,0:T(8,128)(2,1)S(1)}, bf16[16,64,1536]{2,1,0:T(8,128)(2,1)}, u32[]{:S(2)}) copy-start(bf16[16,64,1536]{2,1,0:T(8,128)(2,1)} %param.21) | copy-start | bytes 9437188
  7.2 96.7 %copy-start.47 = (s32[160]{0:T(256)S(1)}, s32[160]{0:T(256)}, u32[]{:S(2)}) copy-start(s32[160]{0:T(256)} %param.23) | copy-start | bytes 1924
  7.2 99.1 %copy-start.46 = (bf16[2,192]{1,0:T(2,128)(2,1)S(1)}, bf16[2,192]{1,0:T(2,128)(2,1)}, u32[]{:S(2)}) copy-start(bf16[2,192]{1,0:T(2,128)(2,1)} %param.16) | copy-start | bytes 2308
  7.2 52.2 %all-gather.16.cloned.1.call-start = ((), (), s32[]{:S(2)}) async-start(), calls=%async_computation.8 | async-start | bytes 2211840 | tf_op jit(solution)/shard_map/all_gather | solution.py:113
  9.1 91.9 %all-gather.18.cloned.1.call-start = ((), (), s32[]{:S(2)}) async-start(), calls=%async_computation.9 | async-start | bytes 1327104 | tf_op jit(solution)/shard_map/all_gather | solution.py:113
  10.8 147.8 %all-gather.32.cloned.1.call-start = ((), (), s32[]{:S(2)}) async-start(), calls=%async_computation.23 | async-start | bytes 9830400 | tf_op jit(solution)/shard_map/all_gather | solution.py:114
  59.4 149.7 %all-gather.34.cloned.1.call-start = ((), (), s32[]{:S(2)}) async-start(), calls=%async_computation.24 | async-start | bytes 5898240 | tf_op jit(solution)/shard_map/all_gather | solution.py:114
  101.0 468.3 %all-gather.20.cloned.1.call-start = ((), (), s32[]{:S(2)}) async-start(), calls=%async_computation.10 | async-start | bytes 14155776 | tf_op jit(solution)/shard_map/all_gather | solution.py:177
  103.8 482.5 %all-gather.22.cloned.1.call-start = ((), (), s32[]{:S(2)}) async-start(), calls=%async_computation.11 | async-start | bytes 9830400 | tf_op jit(solution)/shard_map/all_gather | solution.py:227
  119.5 48.5 %copy-start.38 = (f32[1536]{0:T(1024)}, f32[1536]{0:T(1024)S(1)}, u32[]{:S(2)}) copy-start(f32[1536]{0:T(1024)S(1)} %get-tuple-element.256) | copy-start | bytes 18436
  122.2 45.9 %copy-start.42 = (f32[640]{0:T(1024)}, f32[640]{0:T(1024)S(1)}, u32[]{:S(2)}) copy-start(f32[640]{0:T(1024)S(1)} %get-tuple-element.328) | copy-start | bytes 7684
  173.5 30.5 %collective-permute-start = (bf16[5,128,1024]{2,1,0:T(8,128)(2,1)}, bf16[5,128,1024]{2,1,0:T(8,128)(2,1)}, u32[]{:S(2)}, u32[]{:S(2)}) collective-permute-start(bf16[5,128,1024]{2,1,0:T(8,128)(2,1)} %bitcast.323), channel_id=1, source_target_pairs={{0,1},{1,0},{2,3},{3,2},{4,5},{5,4},{6,7},{7,6},{8,9},{9,8},{10,11... | collective-permute-start | bytes 3932168 | tf_op jit(solution)/shard_map/ppermute | solution.py:31
  207.9 109.2 %collective-permute-start.1 = (bf16[10,128,1024]{2,1,0:T(8,128)(2,1)}, bf16[10,128,1024]{2,1,0:T(8,128)(2,1)}, u32[]{:S(2)}, u32[]{:S(2)}) collective-permute-start(bf16[10,128,1024]{2,1,0:T(8,128)(2,1)} %maximum_select_fusion.1), channel_id=1, source_target_pairs={{0,2},{2,0},{1,3},{3,1},{4,6},{6,4},{5,7},{7,5},{8,10},{10,8},{9,1... | collective-permute-start | bytes 7864328 | tf_op jit(solution)/shard_map/ppermute | solution.py:31
  515.5 10.1 copy-start.5
  515.5 10.1 copy-start.20
  519.0 8.5 copy-start.28
  529.1 26.0 %copy-start.30 = (s32[640,8]{0,1:T(8,128)S(1)}, s32[640,8]{0,1:T(8,128)}, u32[]{:S(2)}) copy-start(s32[640,8]{0,1:T(8,128)} %param.22) | copy-start | bytes 61444
  529.2 156.2 %all-gather.24.cloned.1.call-start = ((), (), s32[]{:S(2)}) async-start(), calls=%async_computation.12 | async-start | bytes 7077888 | tf_op jit(solution)/shard_map/all_gather | solution.py:180
  530.2 213.0 %all-gather.26.cloned.1.call-start = ((), (), s32[]{:S(2)}) async-start(), calls=%async_computation.14 | async-start | bytes 9830400 | tf_op jit(solution)/shard_map/all_gather | solution.py:183
  531.0 413.9 %reduce-scatter.13.cloned.1.call-start = ((), (), s32[]{:S(2)}) async-start(), calls=%async_computation.15 | async-start | bytes 9830400 | tf_op jit(solution)/shard_map/reduce_scatter | solution.py:268
  555.4 72.4 %copy-start.22 = (f32[640,16]{0,1:T(8,128)}, f32[640,16]{0,1:T(8,128)S(1)}, u32[]{:S(2)}) copy-start(f32[640,16]{0,1:T(8,128)S(1)} %select_reduce_fusion) | copy-start | bytes 122884
  826.0 141.2 %reduce-scatter.11.cloned.1.call-start = ((), (), s32[]{:S(2)}) async-start(), calls=%async_computation.13 | async-start | bytes 9830400 | tf_op jit(solution)/shard_map/reduce_scatter | solution.py:237
  851.4 750.9 %reduce-scatter.23.cloned.1.call-start = ((), (), s32[]{:S(2)}) async-start(), calls=%async_computation.21 | async-start | bytes 7077888 | tf_op jit(solution)/shard_map/reduce_scatter | solution.py:118
  875.3 745.0 %all-reduce.3.cloned.1.call-start = ((), (), s32[]{:S(2)}) async-start(), calls=%async_computation.26 | async-start | bytes 25165824
  937.3 7.6 copy-start.27
  937.3 7.6 copy-start.29
  937.3 7.6 copy-start.32
  937.3 686.7 %reduce-scatter.19.cloned.1.call-start = ((), (), s32[]{:S(2)}) async-start(), calls=%async_computation.18 | async-start | bytes 5898240 | tf_op jit(solution)/shard_map/reduce_scatter | solution.py:125
  944.8 8.3 copy-start.25
  944.8 8.2 copy-start.36
  944.8 22.4 %copy-start.12 = (bf16[640,1536]{1,0:T(8,128)(2,1)S(1)}, bf16[640,1536]{1,0:T(8,128)(2,1)}, u32[]{:S(2)}) copy-start(bf16[640,1536]{1,0:T(8,128)(2,1)} %param.25) | copy-start | bytes 5898244
  944.8 22.4 %copy-start.44 = (f32[640]{0:T(1024)S(1)}, f32[640]{0:T(1024)}, u32[]{:S(2)}) copy-start(f32[640]{0:T(1024)} %get-tuple-element.329) | copy-start | bytes 7684
  1002.3 670.9 %reduce-scatter.15.cloned.1.call-start = ((), (), s32[]{:S(2)}) async-start(), calls=%async_computation.16 | async-start | bytes 9830400 | tf_op jit(solution)/shard_map/reduce_scatter | solution.py:125
  1006.1 10.8 copy-start.2
  1026.9 10.9 slice-start
  1043.5 10.8 copy-start.2
  1064.1 10.8 slice-start
  1080.5 10.8 copy-start.2
  1101.1 10.7 slice-start
  1117.4 10.8 copy-start.2
  1138.2 11.2 slice-start
  1154.9 10.8 copy-start.2
  1175.7 10.9 slice-start
  1192.2 10.8 copy-start.2
  1212.9 10.9 slice-start
  1229.4 10.8 copy-start.2
  1250.8 10.7 slice-start
  1267.1 10.8 copy-start.2
  1287.9 10.8 slice-start
  1301.5 19.9 %copy-start.13 = (bf16[8,5,3,128,64]{3,4,2,1,0:T(8,128)(2,1)}, bf16[8,5,3,128,64]{3,4,2,1,0:T(8,128)(2,1)S(1)}, u32[]{:S(2)}) copy-start(bf16[8,5,3,128,64]{3,4,2,1,0:T(8,128)(2,1)S(1)} %get-tuple-element.102) | copy-start | bytes 5898244
  1474.8 68.6 %collective-permute-start.2 = (bf16[10,128,1024]{2,1,0:T(8,128)(2,1)S(1)}, bf16[10,128,1024]{2,1,0:T(8,128)(2,1)S(1)}, u32[]{:S(2)}, u32[]{:S(2)}) collective-permute-start(bf16[10,128,1024]{2,1,0:T(8,128)(2,1)S(1)} %select_convert_fusion), channel_id=1, source_target_pairs={{0,2},{2,0},{1,3},{3,1},{4,6},{6,4},{5,7},{7,5},{8,10},{10,8},{9,1... | collective-permute-start | bytes 7864328 | tf_op jit(solution)/shard_map/ppermute | solution.py:31
  1549.4 30.4 %collective-permute-start.3 = (bf16[5,128,1024]{2,1,0:T(8,128)(2,1)S(1)}, bf16[5,128,1024]{2,1,0:T(8,128)(2,1)S(1)}, u32[]{:S(2)}, u32[]{:S(2)}) collective-permute-start(bf16[5,128,1024]{2,1,0:T(8,128)(2,1)S(1)} %select_convert_fusion.1), channel_id=1, source_target_pairs={{0,1},{1,0},{2,3},{3,2},{4,5},{5,4},{6,7},{7,6},{8,9},{9,8},{10,11... | collective-permute-start | bytes 3932168 | tf_op jit(solution)/shard_map/ppermute | solution.py:31
  1555.1 29.1 %copy-start.9 = (bf16[640,1536]{1,0:T(8,128)(2,1)S(1)}, bf16[640,1536]{1,0:T(8,128)(2,1)}, u32[]{:S(2)}) copy-start(bf16[640,1536]{1,0:T(8,128)(2,1)} %param.15) | copy-start | bytes 5898244
  1555.1 29.1 %copy-start.39 = (f32[1536]{0:T(1024)S(1)}, f32[1536]{0:T(1024)}, u32[]{:S(2)}) copy-start(f32[1536]{0:T(1024)} %copy-done.38) | copy-start | bytes 18436
  1555.1 29.1 %copy-start.43 = (f32[640]{0:T(1024)S(1)}, f32[640]{0:T(1024)}, u32[]{:S(2)}) copy-start(f32[640]{0:T(1024)} %copy-done.42) | copy-start | bytes 7684
  1602.2 101.5 %all-gather.30.cloned.1.call-start = ((), (), s32[]{:S(2)}) async-start(), calls=%async_computation.22 | async-start | bytes 3932160 | tf_op jit(solution)/shard_map/all_gather | solution.py:119
  1602.7 165.1 %reduce-scatter.25.cloned.1.call-start = ((), (), s32[]{:S(2)}) async-start(), calls=%async_computation.25 | async-start | bytes 884736
  1607.7 11.2 copy-start.48
  1618.9 198.8 %all-gather.28.cloned.1.call-start = ((), (), s32[]{:S(2)}) async-start(), calls=%async_computation.20 | async-start | bytes 7864320 | tf_op jit(solution)/shard_map/all_gather | solution.py:119
  1623.9 258.7 %reduce-scatter.21.cloned.1.call-start = ((), (), s32[]{:S(2)}) async-start(), calls=%async_computation.19 | async-start | bytes 1327104 | tf_op jit(solution)/shard_map/reduce_scatter | solution.py:126
  1624.5 327.5 %reduce-scatter.17.cloned.1.call-start = ((), (), s32[]{:S(2)}) async-start(), calls=%async_computation.17 | async-start | bytes 2211840 | tf_op jit(solution)/shard_map/reduce_scatter | solution.py:126
  1673.2 36.0 %copy-start.11 = (bf16[640,1536]{1,0:T(8,128)(2,1)S(1)}, bf16[640,1536]{1,0:T(8,128)(2,1)}, u32[]{:S(2)}) copy-start(bf16[640,1536]{1,0:T(8,128)(2,1)} %param.15) | copy-start | bytes 5898244
  1673.3 36.0 %copy-start.41 = (f32[640]{0:T(1024)S(1)}, f32[640]{0:T(1024)}, u32[]{:S(2)}) copy-start(f32[640]{0:T(1024)} %get-tuple-element.327) | copy-start | bytes 7684
  1817.7 147.2 %copy-start.1 = (bf16[16,64,1536]{2,1,0:T(8,128)(2,1)S(1)}, bf16[16,64,1536]{2,1,0:T(8,128)(2,1)}, u32[]{:S(2)}) copy-start(bf16[16,64,1536]{2,1,0:T(8,128)(2,1)} %param.21) | copy-start | bytes 9437188
  (31 other events, 112.9 us)
Sparse Core Ops, SparseCore 0:
  10.8 48.5 all-gather.15
  62.1 38.8 all-gather.17
  102.6 55.9 all-gather.31
  160.0 37.4 all-gather.33
  200.1 223.7 all-gather.19
  529.3 56.9 all-gather.21
  589.1 96.3 all-gather.23
  687.0 56.1 all-gather.25
  826.2 68.5 reduce-scatter.12
  897.3 69.8 reduce-scatter.10
  971.4 117.1 reduce-scatter.22
  1092.5 405.1 all-reduce.2
  1500.4 50.9 reduce-scatter.18
  1602.3 70.8 reduce-scatter.14
  1674.7 28.9 all-gather.29
  1707.8 60.0 reduce-scatter.24
  1769.9 47.8 all-gather.27
  1821.0 61.5 reduce-scatter.20
  1886.0 65.9 reduce-scatter.16

commit v2 on v1

--- a/solution.py
+++ b/solution.py
@@ -1,4 +1,8 @@
+import functools
+
 import jax
+import jax.experimental.pallas as pl
+import jax.experimental.pallas.tpu as pltpu
 import jax.numpy as jnp
 from jax import lax
 from jax.sharding import PartitionSpec as P
@@ -18,7 +22,438 @@
 
 
 EPS = 1e-06
-MASK_VALUE = -1e30
+
+
+PAIRS = KVH // 2
+LANES = 2 * HD
+NEG=-1e30
+def low_half(): return lax.broadcasted_iota(jnp.int32,(SEG,LANES),1)<HD
+def stack_heads(ref, row, pair, factor=None):
+    low=low_half()
+    t=[ref[pl.ds(row,SEG), pl.ds(pl.multiple_of((3*pair+i)*LANES,LANES),LANES)].astype(jnp.float32) for i in range(3)]
+    if factor is not None: t=[x*factor for x in t]
+    z=jnp.zeros_like(t[0])
+    r0=pltpu.roll(t[0],HD,1); r2=pltpu.roll(t[2],HD,1)
+    parts=[jnp.where(low,t[0],z),jnp.where(low,r0,z),jnp.where(low,t[1],z),
+           jnp.where(low,z,t[1]),jnp.where(low,z,r2),jnp.where(low,z,t[2])]
+    return jnp.concatenate(parts,axis=0)
+def unstack_heads(rows):
+    low=low_half()
+    a=[rows[i*SEG:(i+1)*SEG] for i in range(6)]
+    return [jnp.where(low,a[0],pltpu.roll(a[1],HD,1)), jnp.where(low,a[2],a[3]), jnp.where(low,pltpu.roll(a[4],HD,1),a[5])]
+def kv_path(kv_ref, slots, seg, depth, col):
+    return jnp.concatenate([kv_ref[slots[seg,lev],:,pl.ds(pl.multiple_of(col,LANES),LANES)] for lev in range(depth)],axis=0)
+NT=(((1,),(1,)),((),())); NN=(((1,),(0,)),((),())); TN=(((0,),(0,)),((),()))
+def dot(a,b,dims): return lax.dot_general(a,b,dims,preferred_element_type=jnp.float32)
+def causal_bias(width):
+    key=lax.broadcasted_iota(jnp.int32,(SEG,width),0); qry=lax.broadcasted_iota(jnp.int32,(SEG,width),1)%SEG
+    return jnp.where(key<=qry,0.0,NEG)
+def fwd_step(depth, slots, bias, q_ref, kv_ref, o_ref, lse_ref, s_scr, p_scr, i, c):
+    width=6*SEG
+    seg=i//PAIRS; pair=i%PAIRS
+    row=pl.multiple_of(seg*SEG,SEG)
+    q6=stack_heads(q_ref,row,pair,HD**-0.5).astype(jnp.bfloat16)
+    top=jnp.full((8,width),NEG,jnp.float32)
+    for lev in range(depth):
+        k=kv_ref[slots[seg,lev],:,pl.ds(pl.multiple_of(pair*LANES,LANES),LANES)]
+        s=dot(k,q6,NT)
+        s=s+(causal_bias(width) if lev==0 else bias[seg,lev])
+        s_scr[lev*SEG:(lev+1)*SEG,:]=s
+        top=jnp.maximum(top,jnp.max(s.reshape(SEG//8,8,width),axis=0))
+    top=jnp.max(top,axis=0,keepdims=True)
+    tot=jnp.zeros((8,width),jnp.float32)
+    acc=jnp.zeros((LANES,width),jnp.float32)
+    for lev in range(depth):
+        p=jnp.exp(s_scr[lev*SEG:(lev+1)*SEG,:]-top)
+        tot=tot+jnp.sum(p.reshape(SEG//8,8,width),axis=0)
+        p_scr[lev*SEG:(lev+1)*SEG,:]=p.astype(jnp.bfloat16)
+    v=kv_path(kv_ref,slots,seg,depth,KVH*HD+pair*LANES)
+    acc=dot(v,p_scr[...],TN)
+    tot=jnp.sum(tot,axis=0,keepdims=True)
+    lse_ref[i]=jnp.broadcast_to(top+jnp.log(tot),(8,width))
+    o6=(acc/tot).T
+    for j,t in enumerate(unstack_heads(o6)):
+        o_ref[pl.ds(row,SEG),pl.ds(pl.multiple_of((3*pair+j)*LANES,LANES),LANES)]=t.astype(o_ref.dtype)
+    return c
+def bwd_kernel(depth, slots, bias, inv, q_ref, kv_ref, o_ref, do_ref, lse_ref, dq_ref, dkv_ref, path, p_scr, d_scr):
+    width=6*SEG
+    segs=q_ref.shape[0]//SEG
+    path[:,depth]=jnp.zeros((segs,)+path.shape[2:],path.dtype)
+    def step(i,c):
+        seg=i//PAIRS; pair=i%PAIRS
+        row=pl.multiple_of(seg*SEG,SEG)
+        q6=stack_heads(q_ref,row,pair,HD**-0.5).astype(jnp.bfloat16)
+        do6f=stack_heads(do_ref,row,pair)
+        do6=do6f.astype(jnp.bfloat16)
+        prod=do6f*stack_heads(o_ref,row,pair)
+        hi=prod.astype(jnp.bfloat16); lo=(prod-hi.astype(jnp.float32)).astype(jnp.bfloat16)
+        ones=jnp.ones((8,LANES),jnp.bfloat16)
+        delta=(dot(ones,hi,NT)+dot(ones,lo,NT))[:1]
+        lse=lse_ref[i][:1]
+        kcol=pl.multiple_of(pair*LANES,LANES); vcol=pl.multiple_of(KVH*HD+pair*LANES,LANES)
+        for lev in range(depth):
+            k=kv_ref[slots[seg,lev],:,pl.ds(kcol,LANES)]
+            v=kv_ref[slots[seg,lev],:,pl.ds(vcol,LANES)]
+            s=dot(k,q6,NT)
+            s=s+(causal_bias(width) if lev==0 else bias[seg,lev])
+            p=jnp.exp(s-lse)
+            dp=dot(v,do6,NT)
+            ds=(p*(dp-delta)).astype(jnp.bfloat16)
+            p_scr[lev*SEG:(lev+1)*SEG,:]=p.astype(jnp.bfloat16)
+            d_scr[lev*SEG:(lev+1)*SEG,:]=ds
+        dv=dot(p_scr[...],do6,NN)
+        dk=dot(d_scr[...],q6,NN)
+        for lev in range(depth):
+            path[seg,lev,:,pl.ds(kcol,LANES)]=dk[lev*SEG:(lev+1)*SEG].astype(path.dtype)
+            path[seg,lev,:,pl.ds(vcol,LANES)]=dv[lev*SEG:(lev+1)*SEG].astype(path.dtype)
+        k=kv_path(kv_ref,slots,seg,depth,pair*LANES)
+        dq6=(dot(k,d_scr[...],TN)*(HD**-0.5)).T
+        for j,t in enumerate(unstack_heads(dq6)):
+            dq_ref[pl.ds(row,SEG),pl.ds(pl.multiple_of((3*pair+j)*LANES,LANES),LANES)]=t.astype(dq_ref.dtype)
+        return c
+    lax.fori_loop(0,segs*PAIRS,step,0)
+    def collect(slot,c):
+        for col in range(0,2*KVH*HD,256):
+            tot=path[0,inv[slot,0],:,col:col+256].astype(jnp.float32)
+            for seg in range(1,segs): tot=tot+path[seg,inv[slot,seg],:,col:col+256].astype(jnp.float32)
+            dkv_ref[slot,:,col:col+256]=tot.astype(dkv_ref.dtype)
+        return c
+    lax.fori_loop(0,dkv_ref.shape[0],collect,0)
+def attn_bwd(slots,bias,inv,q,kv,o,do,lse,depth):
+    T=q.shape[0]; segs=T//SEG
+    V=pl.BlockSpec(memory_space=pltpu.VMEM); S=pl.BlockSpec(memory_space=pltpu.SMEM)
+    return pl.pallas_call(functools.partial(bwd_kernel,depth),
+        out_shape=(jax.ShapeDtypeStruct(q.shape,jnp.bfloat16),jax.ShapeDtypeStruct(kv.shape,jnp.bfloat16)),
+        in_specs=[S,S,S,V,V,V,V,V],out_specs=(V,V),
+        scratch_shapes=[pltpu.VMEM((segs,depth+1,SEG,2*KVH*HD),jnp.bfloat16),pltpu.VMEM((depth*SEG,6*SEG),jnp.bfloat16),pltpu.VMEM((depth*SEG,6*SEG),jnp.bfloat16)],
+        compiler_params=pltpu.CompilerParams(vmem_limit_bytes=60*2**20))(slots,bias,inv,q,kv,o,do,lse)
+
+
+MESH = pl.DeviceIdType.MESH
+ANY = pl.BlockSpec(memory_space=pl.ANY)
+VMEM = pl.BlockSpec(memory_space=pltpu.VMEM)
+SMEM = pl.BlockSpec(memory_space=pltpu.SMEM)
+
+
+class Sends:
+    def __init__(self):
+        self.open = []
+
+    def start(self, cond, src, dst, send_sem, recv_sem, device):
+        copy = pltpu.make_async_remote_copy(
+            src_ref=src, dst_ref=dst, send_sem=send_sem, recv_sem=recv_sem, device_id=device, device_id_type=MESH
+        )
+        when(cond, copy.start)
+        self.open.append((cond, copy.wait_send))
+
+    def local(self, src, dst, sem):
+        copy = pltpu.make_async_copy(src, dst, sem)
+        copy.start()
+        self.open.append((None, copy.wait))
+
+    def drain(self):
+        for cond, wait in self.open:
+            when(cond, wait)
+        self.open = []
+
+
+def when(cond, body):
+    if cond is None:
+        body()
+    else:
+        pl.when(cond)(body)
+
+
+def received(cond, region, send_sem, recv_sem, device):
+    copy = pltpu.make_async_remote_copy(
+        src_ref=region, dst_ref=region, send_sem=send_sem, recv_sem=recv_sem, device_id=device, device_id_type=MESH
+    )
+    when(cond, copy.wait_recv)
+
+
+def line_place(shards):
+    me = lax.axis_index("shard")
+    return me, me // 2, shards // 2
+
+
+def greet(devices):
+    barrier = pltpu.get_barrier_semaphore()
+    count = 0
+    for cond, device in devices:
+        when(
+            cond,
+            lambda device=device: pl.semaphore_signal(barrier, inc=1, device_id=device, device_id_type=MESH),
+        )
+        count = count + (1 if cond is None else cond.astype(jnp.int32))
+    pl.semaphore_wait(barrier, count)
+
+
+def line_neighbours(shards):
+    me, spot, length = line_place(shards)
+    return [
+        (None, {"shard": me + 1 - 2 * (me % 2)}),
+        (spot > 0, {"shard": me - 2}),
+        (spot + 1 < length, {"shard": me + 2}),
+    ]
+
+
+class LineGather:
+    def __init__(self, shards, sources, region, up, down, pair, local_sem, arrived=None):
+        self.shards, self.sources, self.region = shards, sources, region
+        self.up, self.down, self.pair, self.local_sem = up, down, pair, local_sem
+        self.arrived = arrived or (lambda cond, block, index: None)
+        self.sends = Sends()
+        self.me, self.spot, self.length = line_place(shards)
+        self.twin = self.me + 1 - 2 * (self.me % 2)
+
+    def forward(self, cond, block, step, rising, falling, src=None):
+        place = step if rising else self.length - 1 + step
+        for n in range(len(self.sources)):
+            here = self.region(n, block)
+            out = here if src is None else src[n]
+            ways = []
+            if rising:
+                ways.append((both(cond, self.spot + 1 < self.length), self.up, step + 1, self.me + 2))
+            if falling:
+                ways.append((both(cond, self.spot > 0), self.down, step + 1, self.me - 2))
+            for where, sems, index, device in ways:
+                if index < self.length:
+                    self.sends.start(where, out, here, sems.at[0, index, n], sems.at[1, index, n], {"shard": device})
+            self.sends.start(
+                cond, out, here, self.pair.at[0, place, n], self.pair.at[1, place, n], {"shard": self.twin}
+            )
+
+    def begin(self):
+        for n, src in enumerate(self.sources):
+            self.sends.local(src, self.region(n, self.me), self.local_sem.at[n])
+        self.forward(None, self.me, 0, True, True, self.sources)
+
+    def finish_local(self):
+        for cond, wait in self.sends.open[: len(self.sources)]:
+            wait()
+        self.sends.open = self.sends.open[len(self.sources) :]
+
+    def step(self, step):
+        for sems, cond, block, rising in (
+            (self.up, self.spot - step >= 0, self.me - 2 * step, True),
+            (self.down, self.spot + step < self.length, self.me + 2 * step, False),
+        ):
+            for n in range(len(self.sources)):
+                received(cond, self.region(n, block), sems.at[0, step, n], sems.at[1, step, n], {"shard": self.twin})
+            self.forward(cond, block, step, rising, not rising)
+            self.arrived(cond, block, step if rising else self.length - 1 + step)
+
+    def pair_step(self, step):
+        turns = [(None, self.twin, 0)] if step == 0 else [
+            (self.spot - step >= 0, self.twin - 2 * step, step),
+            (self.spot + step < self.length, self.twin + 2 * step, self.length - 1 + step),
+        ]
+        for cond, block, place in turns:
+            for n in range(len(self.sources)):
+                received(
+                    cond, self.region(n, block), self.pair.at[0, place, n], self.pair.at[1, place, n], {"shard": self.twin}
+                )
+            self.arrived(cond, block, 2 * self.length - 1 + place)
+
+
+def both(first, second):
+    return second if first is None else jnp.logical_and(first, second)
+
+
+def line_sems(shards, arrays):
+    length = shards // 2
+    return [
+        pltpu.SemaphoreType.DMA((2, length, arrays)),
+        pltpu.SemaphoreType.DMA((2, length, arrays)),
+        pltpu.SemaphoreType.DMA((2, 2 * length - 1, arrays)),
+        pltpu.SemaphoreType.DMA((arrays,)),
+    ]
+
+
+class RepSpread:
+    def __init__(self, arrays, region, cross, core, relay):
+        self.arrays, self.region = arrays, region
+        self.cross, self.core, self.relay = cross, core, relay
+        rep = lax.axis_index("rep")
+        self.rep = rep
+        self.near = rep + 1 - 2 * (rep % 2)
+        self.far = lax.rem(rep + 2, 4)
+        self.diagonal = lax.rem(self.near + 2, 4)
+        self.sends = Sends()
+        self.blocks = []
+
+    def arrived(self, cond, block, index):
+        for n in self.arrays:
+            here = self.region(n, self.rep, block)
+            self.sends.start(
+                cond, here, here, self.cross.at[0, block, n], self.cross.at[1, block, n], {"rep": self.far}
+            )
+            self.sends.start(
+                cond, here, here, self.core.at[0, block, n], self.core.at[1, block, n], {"rep": self.near}
+            )
+        self.blocks.append((cond, block))
+
+    def pass_on(self):
+        for cond, block in self.blocks:
+            for n in self.arrays:
+                here = self.region(n, self.far, block)
+                received(cond, here, self.cross.at[0, block, n], self.cross.at[1, block, n], {"rep": self.far})
+                self.sends.start(
+                    cond, here, here, self.relay.at[0, block, n], self.relay.at[1, block, n], {"rep": self.near}
+                )
+        self.passed = getattr(self, "passed", []) + self.blocks
+        self.blocks = []
+
+    def end(self):
+        self.pass_on()
+        for cond, block in self.passed:
+            for n in self.arrays:
+                for sems, part in ((self.core, self.near), (self.relay, self.diagonal)):
+                    here = self.region(n, part, block)
+                    received(cond, here, sems.at[0, block, n], sems.at[1, block, n], {"rep": self.near})
+        self.sends.drain()
+
+
+def rep_neighbours():
+    rep = lax.axis_index("rep")
+    return [(None, {"rep": rep + 1 - 2 * (rep % 2)}), (None, {"rep": lax.rem(rep + 2, 4)})]
+
+
+def rep_sems(shards, arrays):
+    return [pltpu.SemaphoreType.DMA((2, shards, arrays)) for unused in range(3)]
+
+
+def weights_kernel(shards, qkv, out, small, qkv_all, out_all, small_all, up, down, pair, local_sem, cross, core, relay):
+    rep = lax.axis_index("rep")
+    greet(line_neighbours(shards) + rep_neighbours())
+    refs = (qkv_all, out_all, small_all)
+
+    def part(n, owner, block):
+        return refs[n].at[block] if n == 2 else refs[n].at[owner, block]
+
+    def columns(ref, width):
+        return ref.at[:, pl.ds(pl.multiple_of(rep * width, LANES), width)]
+
+    spread = RepSpread((0, 1), part, cross, core, relay)
+    sources = (columns(qkv, qkv_all.shape[-1]), columns(out, out_all.shape[-1]), small)
+    gather = LineGather(
+        shards, sources, lambda n, block: part(n, rep, block), up, down, pair, local_sem, spread.arrived
+    )
+    gather.begin()
+    gather.finish_local()
+    spread.arrived(None, gather.me, 0)
+    for step in range(gather.length):
+        if step:
+            gather.step(step)
+        spread.pass_on()
+        gather.pair_step(step)
+    spread.end()
+    gather.sends.drain()
+
+
+def gather_weights(qkv_weight, out_weight, small, shards, reps):
+    rows = qkv_weight.shape[0]
+    shapes = [
+        (reps, shards, rows, qkv_weight.shape[1] // reps),
+        (reps, shards, rows, out_weight.shape[1] // reps),
+        (shards,) + small.shape,
+    ]
+    return pl.pallas_call(
+        functools.partial(weights_kernel, shards),
+        out_shape=[jax.ShapeDtypeStruct(shape, jnp.bfloat16) for shape in shapes],
+        in_specs=[ANY] * 3,
+        out_specs=[ANY] * 3,
+        scratch_shapes=line_sems(shards, 3) + rep_sems(shards, 2),
+        compiler_params=pltpu.CompilerParams(collective_id=1, has_side_effects=True),
+    )(qkv_weight, out_weight, small)
+
+
+def attend_gather_kernel(
+    depth,
+    shards,
+    slots,
+    bias,
+    q_ref,
+    kv_ref,
+    gu_ref,
+    dn_ref,
+    o_ref,
+    lse_ref,
+    kv_all,
+    gu_all,
+    dn_all,
+    s_scr,
+    p_scr,
+    kv_sems,
+    up,
+    down,
+    pair,
+    local_sem,
+):
+    me = lax.axis_index("shard")
+    first = me // TREE_DEVS * TREE_DEVS
+    member = me % TREE_DEVS
+    seg_dev = kv_ref.shape[0]
+    others = [first + lax.rem(member + away, TREE_DEVS) for away in range(1, TREE_DEVS)]
+    greet(line_neighbours(shards) + [(None, {"shard": other}) for other in others])
+    sends = Sends()
+    own = kv_all.at[pl.ds(member * seg_dev, seg_dev)]
+    for away, other in enumerate(others):
+        sends.start(None, kv_ref, own, kv_sems.at[0, away], kv_sems.at[1, away], {"shard": other})
+    gather = LineGather(
+        shards,
+        (gu_ref, dn_ref),
+        lambda n, block: (gu_all, dn_all)[n].at[:, block],
+        up,
+        down,
+        pair,
+        local_sem,
+    )
+    gather.begin()
+    kv_all[pl.ds(member * seg_dev, seg_dev)] = kv_ref[...]
+    for away in range(TREE_DEVS - 1):
+        source = lax.rem(member + TREE_DEVS - 1 - away, TREE_DEVS)
+        block = kv_all.at[pl.ds(source * seg_dev, seg_dev)]
+        received(None, block, kv_sems.at[0, away], kv_sems.at[1, away], {"shard": first + source})
+    count = seg_dev * PAIRS
+    attend = functools.partial(fwd_step, depth, slots, bias, q_ref, kv_all, o_ref, lse_ref, s_scr, p_scr)
+    done = 0
+    for step in range(1, gather.length):
+        upto = count * step // (gather.length - 1)
+        lax.fori_loop(done, upto, attend, 0)
+        done = upto
+        gather.step(step)
+    for step in range(gather.length):
+        gather.pair_step(step)
+    gather.sends.drain()
+    sends.drain()
+
+
+def attend_gather(slots, bias, q, kv, gate_up, down, depth, shards):
+    tokens = q.shape[0]
+    count = tokens // SEG * PAIRS
+    experts, rows = gate_up.shape[:2]
+    return pl.pallas_call(
+        functools.partial(attend_gather_kernel, depth, shards),
+        out_shape=(
+            jax.ShapeDtypeStruct(q.shape, jnp.bfloat16),
+            jax.ShapeDtypeStruct((count, 8, 6 * SEG), jnp.float32),
+            jax.ShapeDtypeStruct((TREE_DEVS * kv.shape[0],) + kv.shape[1:], jnp.bfloat16),
+            jax.ShapeDtypeStruct((experts, shards, rows) + gate_up.shape[2:], jnp.bfloat16),
+            jax.ShapeDtypeStruct((experts, shards) + down.shape[1:], jnp.bfloat16),
+        ),
+        in_specs=[SMEM, SMEM, VMEM, VMEM, ANY, ANY],
+        out_specs=(VMEM, VMEM, VMEM, ANY, ANY),
+        scratch_shapes=[
+            pltpu.VMEM((depth * SEG, 6 * SEG), jnp.float32),
+            pltpu.VMEM((depth * SEG, 6 * SEG), jnp.bfloat16),
+            pltpu.SemaphoreType.DMA((2, TREE_DEVS - 1)),
+        ]
+        + line_sems(shards, 2),
+        compiler_params=pltpu.CompilerParams(
+            collective_id=2, has_side_effects=True, vmem_limit_bytes=48 * 2**20
+        ),
+    )(slots, bias, q, kv, gate_up, down)
 
 
 def partner(block, axis, stride):
@@ -71,47 +506,12 @@
     return (jnp.stack(slot_list, axis=1), jnp.stack(alive_list, axis=1))
 
 
-def head_scores(queries, keys, mask, scale):
-    scores = jnp.einsum("sgqd,skd->sgqk", queries, keys, preferred_element_type=jnp.float32) * scale
-    return jnp.where(mask[:, None], scores, MASK_VALUE)
-
-
-def head_forward(operands, mask, scale):
-    queries, keys, values = operands
-    scores = head_scores(queries, keys, mask, scale)
-    highest = jnp.max(scores, axis=-1, keepdims=True)
-    weights = jnp.exp(scores - highest)
-    totals = jnp.sum(weights, axis=-1, keepdims=True)
-    probs = (weights / totals).astype(jnp.bfloat16)
-    mixed = jnp.einsum("sgqk,skd->sgqd", probs, values, preferred_element_type=jnp.float32)
-    return (mixed.astype(jnp.bfloat16), highest + jnp.log(totals))
-
-
-def head_backward(operands, mask, scale):
-    queries, keys, values, upstream, log_totals = operands
-    scores = head_scores(queries, keys, mask, scale)
-    probs = jnp.exp(scores - log_totals)
-    value_grad = jnp.einsum(
-        "sgqk,sgqd->skd", probs.astype(jnp.bfloat16), upstream, preferred_element_type=jnp.float32
-    )
-    prob_grad = jnp.einsum("sgqd,skd->sgqk", upstream, values, preferred_element_type=jnp.float32)
-    inner = jnp.sum(probs * prob_grad, axis=-1, keepdims=True)
-    score_grad = (probs * (prob_grad - inner)).astype(jnp.bfloat16)
-    query_grad = (
-        jnp.einsum("sgqk,skd->sgqd", score_grad, keys, preferred_element_type=jnp.float32) * scale
-    )
-    key_grad = (
-        jnp.einsum("sgqk,sgqd->skd", score_grad, queries, preferred_element_type=jnp.float32)
-        * scale
-    )
-    return (query_grad.astype(jnp.bfloat16), key_grad, value_grad)
-
-
-def gather_columns(weight, rep_index, rep_count):
-    width = weight.shape[1] // rep_count
-    own = lax.dynamic_slice_in_dim(weight, rep_index * width, width, axis=1)
-    part = lax.all_gather(own, "shard", axis=0, tiled=True)
-    return lax.all_gather(part, "rep", axis=0)
+def path_levels(path_slots, path_alive, slot_count):
+    depth = path_slots.shape[1]
+    slots = jnp.arange(slot_count, dtype=jnp.int32)
+    hit = path_alive[None] & (path_slots[None] == slots[:, None, None])
+    levels = jnp.arange(depth, dtype=jnp.int32)
+    return depth - jnp.sum(jnp.where(hit, depth - levels, 0), axis=2)
 
 
 def spread_experts(grad):
@@ -147,11 +547,8 @@
     token_count = tokens.shape[0]
     seg_dev = token_count // SEG
     depth = TRUNK + 2
-    key_count = depth * SEG
     width_q = H * HD
     width_kv = KVH * HD
-    groups_per = H // KVH
-    scale = HD ** (-0.5)
     group_size = TREE_DEVS * seg_dev
     tree_count = group_size // TREE_SEGS
     member = shard_index % TREE_DEVS
@@ -160,26 +557,19 @@
     group_parents = lax.dynamic_slice_in_dim(parents, group * tree_count, tree_count)
     local_ids = lax.dynamic_slice_in_dim(group_ids, member * seg_dev, seg_dev)
     path_slots, path_alive = ancestor_slots(local_ids, group_ids, group_parents, depth)
-    key_level = jnp.arange(key_count, dtype=jnp.int32) // SEG
-    key_pos = jnp.arange(key_count, dtype=jnp.int32) % SEG
-    query_pos = jnp.arange(SEG, dtype=jnp.int32)
-    level_alive = jnp.repeat(path_alive, SEG, axis=1)
-    mask = level_alive[:, None, :] & (
-        (key_level[None, None, :] > 0) | (key_pos[None, None, :] <= query_pos[None, :, None])
-    )
     rep_count = lax.axis_size("rep")
     own_experts = E // rep_count
     first_expert = rep_index * own_experts
-    gains = lax.all_gather(norm_gains, "shard", axis=1, tiled=True)
-    w_router = lax.all_gather(router_weight, "shard", axis=0, tiled=True)
-    w_qkv = gather_columns(qkv_weight, rep_index, rep_count)
-    w_out = gather_columns(out_weight, rep_index, rep_count)
-    w_gate_up = lax.all_gather(
-        lax.dynamic_slice_in_dim(gate_up_weight, first_expert, own_experts), "shard", axis=1, tiled=True
-    )
-    w_down = lax.all_gather(
-        lax.dynamic_slice_in_dim(down_weight, first_expert, own_experts), "shard", axis=1, tiled=True
-    )
+    padding = jnp.zeros((norm_gains.shape[1], LANES - E - 2), jnp.bfloat16)
+    small = jnp.concatenate([router_weight, norm_gains.T, padding], axis=1)
+    w_qkv, w_out, small = gather_weights(qkv_weight, out_weight, small, shard_count, rep_count)
+    w_qkv = w_qkv.reshape(rep_count, D, -1)
+    w_out = w_out.reshape(rep_count, D, -1)
+    small = small.reshape(D, LANES)
+    w_router = small[:, :E]
+    gains = small[:, E : E + 2].T
+    gate_up_own = lax.dynamic_slice_in_dim(gate_up_weight, first_expert, own_experts)
+    down_own = lax.dynamic_slice_in_dim(down_weight, first_expert, own_experts)
     cot_all = lax.all_gather(cotangent, "rep", axis=0, tiled=True)
     gain_first = gains[0].astype(jnp.float32)
     gain_second = gains[1].astype(jnp.float32)
@@ -192,27 +582,12 @@
     own_kv = projected[:, width_q:].astype(jnp.bfloat16).reshape(seg_dev, SEG, 2 * width_kv)
     low_first = member % 2 == 0
     pair_first = member // 2 == 0
-    near_kv = partner(own_kv, "shard", 0)
-    pair_kv = jnp.where(
-        low_first,
-        jnp.concatenate([own_kv, near_kv], axis=0),
-        jnp.concatenate([near_kv, own_kv], axis=0),
-    )
-    far_kv = partner(pair_kv, "shard", 1)
-    group_kv = jnp.where(
-        pair_first,
-        jnp.concatenate([pair_kv, far_kv], axis=0),
-        jnp.concatenate([far_kv, pair_kv], axis=0),
-    )
-    chosen_kv = group_kv[path_slots].reshape(seg_dev, key_count, 2, KVH, HD)
-    head_kv = chosen_kv.transpose(3, 2, 0, 1, 4)
-    head_keys = head_kv[:, 0]
-    head_values = head_kv[:, 1]
-    head_queries = queries.reshape(seg_dev, SEG, KVH, groups_per, HD).transpose(2, 0, 3, 1, 4)
-    mixed, log_totals = lax.map(
-        lambda operands: head_forward(operands, mask, scale), (head_queries, head_keys, head_values)
-    )
-    attended = mixed.transpose(1, 3, 0, 2, 4).reshape(token_count, width_q)
+    bias = jnp.where(path_alive, 0.0, NEG).astype(jnp.float32)
+    attended, log_totals, group_kv, w_gate_up, w_down = attend_gather(
+        path_slots, bias, queries, own_kv, gate_up_own, down_own, depth, shard_count
+    )
+    w_gate_up = w_gate_up.reshape(own_experts, D, -1)
+    w_down = w_down.reshape(own_experts, FF, D)
     mixed_out = jnp.einsum("td,rdc->trc", attended, w_out, preferred_element_type=jnp.float32)
     residual = token_values + mixed_out.reshape(token_count, D)
     normed_second, scale_second = norm_rows(residual, gain_second)
@@ -286,25 +661,20 @@
         w_out,
         preferred_element_type=jnp.float32,
     ).astype(jnp.bfloat16)
-    head_upstream = attended_grad.reshape(seg_dev, SEG, KVH, groups_per, HD).transpose(
-        2, 0, 3, 1, 4
-    )
-    query_grad, key_grad, value_grad = lax.map(
-        lambda operands: head_backward(operands, mask, scale),
-        (head_queries, head_keys, head_values, head_upstream, log_totals),
-    )
-    query_grad = query_grad.transpose(1, 3, 0, 2, 4).reshape(token_count, width_q)
-    path_grad = (
-        jnp.stack([key_grad, value_grad], axis=1)
-        .transpose(2, 3, 1, 0, 4)
-        .reshape(seg_dev, depth, SEG, 2 * width_kv)
-    )
-    group_grad = (
-        jnp.zeros((group_size, SEG, 2 * width_kv), jnp.float32).at[path_slots].add(path_grad)
+    query_grad, group_grad = attn_bwd(
+        path_slots,
+        bias,
+        path_levels(path_slots, path_alive, group_size),
+        queries,
+        group_kv,
+        attended,
+        attended_grad,
+        log_totals,
+        depth,
     )
     pair_part = jnp.where(pair_first, group_grad[: 2 * seg_dev], group_grad[2 * seg_dev :])
     far_part = jnp.where(pair_first, group_grad[2 * seg_dev :], group_grad[: 2 * seg_dev])
-    pair_sum = pair_part + partner(far_part.astype(jnp.bfloat16), "shard", 1).astype(far_part.dtype)
+    pair_sum = pair_part.astype(jnp.float32) + partner(far_part, "shard", 1).astype(jnp.float32)
     own_part = jnp.where(low_first, pair_sum[:seg_dev], pair_sum[seg_dev:])
     near_part = jnp.where(low_first, pair_sum[seg_dev:], pair_sum[:seg_dev])
     own_grad = own_part + partner(near_part.astype(jnp.bfloat16), "shard", 0).astype(

time: 1990 us -> 1760 us (0.88)
  Pallas kernels: 0 us -> 427 us
  matrix products: 548 us -> 269 us
  local copies, waits for them, and re-layouts: 294 us -> 74.7 us
  other arithmetic: 252 us -> 51.9 us
  waiting for transfers between devices: 766 us -> 862 us
  blocking collectives: 88.9 us -> 47.7 us
    pallas_call x0 -> x3, Pallas kernels: none -> 427 us  [the longest x1 268 us: attend_gather(): pl.pallas_call(functools.partial(attend_gather_kernel, depth, shards), ou...]
    dot_general x56 -> x0, matrix products: 275 us -> none  [the longest x16 104 us: head_scores(): jnp.einsum('sgqd,skd->sgqk', queries, keys, preferred_element_type=jnp.fl...]
    unnamed x21 -> x15, waiting for transfers between devices: 55.5 us -> 325 us
    all_gather x6 -> x0, waiting for transfers between devices: 184 us -> none  [the longest x2 90.1 us: gather_columns(): part = lax.all_gather(own, 'shard', axis=0, tiled=True)]
    reshape x5 -> x2, local copies, waits for them, and re-layouts: 127 us -> 17.4 us  [the longest x1 10.6 us: shards(): w_qkv = w_qkv.reshape(rep_count, D, -1)]
    convert_element_type x9 -> x0, other arithmetic: 84.4 us -> none  [the longest x8 79.8 us: head_backward(): score_grad = (probs * (prob_grad - inner)).astype(jnp.bfloat16)]
    reduce_scatter x2, waiting for transfers between devices: 48.7 us -> 120 us  [spread_columns(): part = lax.psum_scatter(pieces, 'rep', scatter_dimension=0, tiled=True)[0]]
    scatter-add x1 -> x0, other arithmetic: 56.9 us -> none  [shards(): jnp.zeros((group_size, SEG, 2 * width_kv), jnp.float32).at[path_slots]]
  transfers between devices with their start and end apart: 23 -> 15, of which waited for: 17 -> 13; matrix products, arithmetic and copies ran while one was open for 51% -> 14% of each run, Pallas kernels for 0% -> 4%
where the time goes in v2:
time: 1760 us; the launch traced here: 1750 us
  waiting for transfers between devices  862 us (49%)
  Pallas kernels  427 us (24%)
  matrix products  269 us (15%)
  local copies, waits for them, and re-layouts  74.7 us (4%)
  other arithmetic  51.9 us (3%)
  blocking collectives  47.7 us (3%)
    unnamed x15, waiting for transfers between devices  325 us
    pallas_call x1, Pallas kernels, attend_gather(): pl.pallas_call(functools.partial(attend_gather_kernel, depth, shards), ou...  268 us
    ppermute x2, waiting for transfers between devices, partner(): return lax.ppermute(block, axis, route)  159 us
    reduce_scatter x2, waiting for transfers between devices, spread_columns(): part = lax.psum_scatter(pieces, 'rep', scatter_dimension=0, tiled=True)[0]  120 us
    reduce_scatter x2, waiting for transfers between devices, spread_columns(): share = lax.psum_scatter(part, 'shard', scatter_dimension=0, tiled=True)  114 us
    pallas_call x1, Pallas kernels, gather_weights(): pl.pallas_call(functools.partial(weights_kernel, shards), out_shape=[jax....  91.1 us
    pallas_call x1, Pallas kernels, attn_bwd(): pl.pallas_call(functools.partial(bwd_kernel, depth), out_shape=(jax.Shape...  68.3 us
    all_gather x2, waiting for transfers between devices, spread_experts(): return lax.all_gather(share, 'rep', axis=0, tiled=True).astype(jnp.float32)  66 us
  transfers between devices with their start and end apart: 15, of which 13 were waited for; matrix products, arithmetic and copies ran while one was open for 14% of the time, Pallas kernels for 4%

profile of v2, /device:TPU:9, one launch (start us, length us, event | category | flops | bytes accessed | tf_op | source)
XLA Modules:
  0.0 1748.9 jit_solution(4885640735725179742)
XLA Ops:
  7.3 1.0 copy.172
  9.9 91.1 %shard_map.170 = (bf16[4,8,192,640]{3,2,1,0:T(8,128)(2,1)}, bf16[4,8,192,384]{3,2,1,0:T(8,128)(2,1)}, bf16[8,192,128]{2,1,0:T(8,128)(2,1)}) custom-call(bf16[192,2560]{1,0:T(8,128)(2,1)} %qkv.1, bf16[192,1536]{1,0:T(8,128)(2,1)} %out.1, bf16[192,128]{1,0:T(8,128)(2,1)} %maximum_maximum_fusion.small), custom_call_target="tpu_custom_call" | custom-call | tf_op jit(solution)/shard_map/pallas_call | solution.py:361
  100.9 1.2 slice.64
  102.3 2.0 fusion.12
  104.9 10.6 copy.175
  115.6 8.3 convolution_convert_fusion.3
  123.9 1.4 slice.66.q_ref
  125.3 1.2 slice.67
  131.7 2.7 constant_dynamic-slice_fusion.1.gu_ref
  134.4 0.9 constant_dynamic-slice_fusion.dn_ref
  135.3 6.8 copy.176
  142.2 1.1 copy-done.4
  143.3 267.6 %shard_map.171 = (bf16[640,1536]{1,0:T(8,128)(2,1)S(1)}, f32[20,8,768]{2,1,0:T(8,128)S(1)}, bf16[20,128,1024]{2,1,0:T(8,128)(2,1)}, bf16[4,8,192,1024]{3,2,1,0:T(8,128)(2,1)}, bf16[4,8,64,1536]{3,2,1,0:T(8,128)(2,1)}) custom-call(s32[5,10]{1,0:T(8,128)S(1)} %stack.79.slots, f32[5,10]{1,0:T(8,128)S(1)} %broadcast_select_fusion.1.bias, ...), custom_call_target="tpu_custom_call" | custom-call | tf_op jit(solution)/shard_map/pallas_call | solution.py:436
  410.9 8.4 multiply_reduce_fusion.2
  420.0 3.8 multiply_convert_fusion.5
  426.8 7.0 all_gather.25
  433.7 48.1 %all-gather.6.cloned.1.call-done = bf16[2560,1536]{1,0:T(8,128)(2,1)} async-done(((bf16[640,1536]{1,0:T(8,128)(2,1)}), bf16[2560,1536]{1,0:T(8,128)(2,1)}) %all-gather.6.cloned.1.call-update) | async-done | bytes 7864336 | tf_op jit(solution)/shard_map/all_gather | solution.py:602
  481.8 41.5 %convolution_bitcast_fusion = f32[4,2560,1024]{1,2,0:T(8,128)} fusion(bf16[4,1536,1024]{2,1,0:T(8,128)(2,1)} %bitcast.170, bf16[2560,1536]{1,0:T(8,128)(2,1)} %all-gather.6.cloned.1.call-done), kind=kOutput, calls=%fused_computation | convolution fusion | flops 32212254720 | bytes 62390272 | tf_op jit(solution)/shard_map/td,edf->etf/dot_general | solution.py:605
  523.4 15.4 all-gather.8.cloned.1.call-done
  538.7 41.7 %multiply_convert_fusion.1 = (bf16[4,2560,512]{1,2,0:T(8,128)(2,1)}, bf16[4,2560,512]{1,2,0:T(8,128)(2,1)}, f32[4,2560]{1,0:T(4,128)}, f32[4,2560,512]{1,2,0:T(8,128)}) fusion(f32[4,2560,1024]{1,2,0:T(8,128)} %convolution_bitcast_fusion, f32[4,2560]{1,0:T(4,128)S(1)} %dynamic-slice_bitcast_fusion, bf16[4,512,1536]{2,1,0:T(8,128)(2,1)} %bitcast.172, ...), kind=kOutput, calls=%fused_computation.6 | convolution fusion | flops 16200488960 | bytes 98123776 | tf_op jit(solution)/shard_map/td,efd->etf/dot_general | solution.py:614
  580.5 41.2 %bitcast_convert_fusion = bf16[2560,1536]{1,0:T(8,128)(2,1)} fusion(bf16[4,1536,1024]{2,1,0:T(8,128)(2,1)} %bitcast.171, bf16[4,2560,512]{1,2,0:T(8,128)(2,1)} %get-tuple-element.72, bf16[4,2560,512]{1,2,0:T(8,128)(2,1)} %get-tuple-element.71), kind=kOutput, calls=%fused_computation.10 | convolution fusion | flops 32258129920 | bytes 41418752 | tf_op jit(solution)/shard_map/etf,edf->td/dot_general | solution.py:640
  621.7 25.2 %bitcast_convert_fusion.1 = bf16[2560,1536]{1,0:T(8,128)(2,1)} fusion(bf16[4,512,1536]{2,1,0:T(8,128)(2,1)} %bitcast.173, f32[4,2560,512]{1,2,0:T(8,128)} %get-tuple-element.74, f32[4,2560]{1,0:T(4,128)S(1)} %dynamic-slice_bitcast_fusion), kind=kOutput, calls=%fused_computation.11 | convolution fusion | flops 16120545280 | bytes 35168256 | tf_op jit(solution)/shard_map/etf,efd->td/dot_general | solution.py:611
  647.0 23.9 %fusion.9 = bf16[4,512,1536]{2,1,0:T(8,128)(2,1)} fusion(bf16[2560,1536]{1,0:T(8,128)(2,1)} %all-gather.8.cloned.1.call-done, f32[4,2560,512]{1,2,0:T(8,128)} %get-tuple-element.74, f32[4,2560]{1,0:T(4,128)S(1)} %dynamic-slice_bitcast_fusion), kind=kOutput, calls=%fused_computation.30 | convolution fusion | flops 16119758848 | bytes 35168256 | tf_op jit(solution)/shard_map/etf,td->efd/dot_general | solution.py:634
  671.0 39.8 %fusion.2 = bf16[4,1536,1024]{1,2,0:T(8,128)(2,1)} fusion(bf16[4,2560,512]{1,2,0:T(8,128)(2,1)} %get-tuple-element.72, bf16[4,2560,512]{1,2,0:T(8,128)(2,1)} %get-tuple-element.71, bf16[2560,1536]{1,0:T(8,128)(2,1)} %all-gather.6.cloned.1.call-done), kind=kOutput, calls=%fused_computation.15 | convolution fusion | flops 32260489216 | bytes 41418752 | tf_op jit(solution)/shard_map/td,etf->edf/dot_general | solution.py:635
  710.8 22.0 %copy.186 = bf16[4,1536,1024]{2,0,1:T(4,128)(2,1)} copy(bf16[4,1536,1024]{1,2,0:T(8,128)(2,1)} %fusion.2) | data formatting | bytes 25165824 | tf_op jit(solution)/shard_map/convert_element_type | solution.py:518
  733.5 6.7 all-gather
  740.4 7.6 multiply_reduce_fusion
  748.0 14.9 reduce-scatter.11.cloned.1.call-done
  762.9 6.9 fusion.51
  769.8 5.5 convolution_convert_fusion.2
  775.4 6.7 copy.185
  783.6 7.2 bitcast_convert_fusion.2.do_ref
  790.8 68.3 %shard_map.172 = (bf16[640,1536]{1,0:T(8,128)(2,1)}, bf16[20,128,1024]{2,1,0:T(8,128)(2,1)}) custom-call(s32[5,10]{1,0:T(8,128)} %copy-done.8, f32[5,10]{1,0:T(8,128)} %copy-done.9, s32[20,5]{1,0:T(8,128)} %broadcast_subtract_fusion.inv, bf16[640,1536]{1,0:T(8,128)(2,1)} %slice.66.q_ref, bf16[20,128,1024]{2,1,0:T(8,128)(2,1)} %get-tuple-element.24.kv_ref, ...), custom_call_target="tpu_custom_call" | custom-call | tf_op jit(solution)/shard_map/pallas_call | solution.py:125
  859.1 4.4 broadcast_select_fusion
  863.8 130.9 %collective-permute-done = bf16[10,128,1024]{2,1,0:T(8,128)(2,1)S(1)} collective-permute-done((bf16[10,128,1024]{2,1,0:T(8,128)(2,1)}, bf16[10,128,1024]{2,1,0:T(8,128)(2,1)S(1)}, u32[]{:S(2)}, u32[]{:S(2)}) %collective-permute-start) | collective-permute-done | bytes 2621472 | tf_op jit(solution)/shard_map/ppermute | solution.py:466
  994.6 4.3 convert_add_fusion.1
  999.3 1.2 collective-permute-start.1
  1000.5 28.4 %collective-permute-done.1 = bf16[5,128,1024]{2,1,0:T(8,128)(2,1)S(1)} collective-permute-done((bf16[5,128,1024]{2,1,0:T(8,128)(2,1)S(1)}, bf16[5,128,1024]{2,1,0:T(8,128)(2,1)S(1)}, u32[]{:S(2)}, u32[]{:S(2)}) %collective-permute-start.1) | collective-permute-done | bytes 1310752 | tf_op jit(solution)/shard_map/ppermute | solution.py:466
  1028.9 0.8 add_convert_fusion.1
  1029.8 7.1 convolution_convert_fusion.1
  1037.0 3.9 copy.208
  1042.4 0.9 fusion.36
  1043.3 1.8 pad_maximum_fusion.7
  1045.1 9.6 fusion.20
  1054.7 1.2 copy.191
  1057.2 269.5 %all-reduce.3.cloned.1.call-done = bf16[4,1536,1024]{2,0,1:T(4,128)(2,1)} async-done(((bf16[4,1536,1024]{2,0,1:T(4,128)(2,1)}), bf16[4,1536,1024]{2,0,1:T(4,128)(2,1)}) %all-reduce.3.cloned.1.call-update) | async-done | bytes 12582928
  1326.6 1.9 constant_dynamic-slice_fusion.3
  1328.6 1.6 copy.187
  1330.3 47.9 %reduce-scatter.19.cloned.1.call-done = bf16[1,1536,384]{2,1,0:T(8,128)(2,1)} async-done(((bf16[4,1536,384]{2,1,0:T(8,128)(2,1)}), bf16[1,1536,384]{2,1,0:T(8,128)(2,1)}) %reduce-scatter.19.cloned.1.call-update) | async-done | bytes 1179664 | tf_op jit(solution)/shard_map/reduce_scatter | solution.py:525
  1378.2 72.1 %reduce-scatter.15.cloned.1.call-done = bf16[1,1536,640]{2,1,0:T(8,128)(2,1)} async-done(((bf16[4,1536,640]{2,1,0:T(8,128)(2,1)}), bf16[1,1536,640]{2,1,0:T(8,128)(2,1)}) %reduce-scatter.15.cloned.1.call-update) | async-done | bytes 1966096 | tf_op jit(solution)/shard_map/reduce_scatter | solution.py:525
  1450.3 30.6 %all-gather.12.cloned.1.call-done = bf16[16,64,1536]{2,1,0:T(8,128)(2,1)} async-done(((bf16[4,64,1536]{2,1,0:T(8,128)(2,1)}), bf16[16,64,1536]{2,1,0:T(8,128)(2,1)}) %all-gather.12.cloned.1.call-update) | async-done | bytes 3145744 | tf_op jit(solution)/shard_map/all_gather | solution.py:519
  1480.9 5.6 convert_element_type.118
  1486.5 5.0 fusion.17
  1491.5 53.5 %reduce-scatter.25.cloned.1.call-done = f32[192,18]{1,0:T(8,128)} async-done(((f32[1536,18]{1,0:T(8,128)}), f32[192,18]{1,0:T(8,128)}) %reduce-scatter.25.cloned.1.call-update) | async-done | bytes 13840
  1545.1 1.0 copy.192
  1546.1 12.4 psum.7
  1559.7 35.4 %all-gather.10.cloned.1.call-done = bf16[16,192,1024]{2,1,0:T(8,128)(2,1)} async-done(((bf16[4,192,1024]{2,1,0:T(8,128)(2,1)}), bf16[16,192,1024]{2,1,0:T(8,128)(2,1)}) %all-gather.10.cloned.1.call-update) | async-done | bytes 6291472 | tf_op jit(solution)/shard_map/all_gather | solution.py:519
  1595.1 9.3 convert_element_type.116
  1604.4 55.5 %reduce-scatter.21.cloned.1.call-done = bf16[192,384]{1,0:T(8,128)(2,1)} async-done(((bf16[1536,384]{1,0:T(8,128)(2,1)}), bf16[192,384]{1,0:T(8,128)(2,1)}) %reduce-scatter.21.cloned.1.call-update) | async-done | bytes 147472 | tf_op jit(solution)/shard_map/reduce_scatter | solution.py:526
  1659.9 10.1 all_gather.29
  1670.0 1.1 convert_element_type.113
  1671.1 58.1 %reduce-scatter.17.cloned.1.call-done = bf16[192,640]{1,0:T(8,128)(2,1)} async-done(((bf16[1536,640]{1,0:T(8,128)(2,1)}), bf16[192,640]{1,0:T(8,128)(2,1)}) %reduce-scatter.17.cloned.1.call-update) | async-done | bytes 245776 | tf_op jit(solution)/shard_map/reduce_scatter | solution.py:526
  1729.3 11.5 all_gather.28
  1740.7 1.5 convert_element_type.111
  (185 shorter events, 17.9 us)
Async XLA Ops:
  7.2 127.2 %copy-start = (bf16[16,64,1536]{2,1,0:T(8,128)(2,1)S(1)}, bf16[16,64,1536]{2,1,0:T(8,128)(2,1)}, u32[]{:S(2)}) copy-start(bf16[16,64,1536]{2,1,0:T(8,128)(2,1)} %param.17) | copy-start | bytes 9437188
  7.2 474.7 %all-gather.6.cloned.1.call-start = ((), (), s32[]{:S(2)}) async-start(), calls=%async_computation.8 | async-start | bytes 9830400 | tf_op jit(solution)/shard_map/all_gather | solution.py:602
  102.3 13.2 copy-start.30
  102.3 317.6 %copy-start.24 = (f32[1536]{0:T(1024)}, f32[1536]{0:T(1024)S(1)}, u32[]{:S(2)}) copy-start(f32[1536]{0:T(1024)S(1)} %get-tuple-element.48) | copy-start | bytes 18436
  104.9 10.6 copy-start.33
  123.9 2.6 copy-start.38
  130.2 0.6 copy-start.36
  130.2 11.9 copy-start.9
  135.3 6.9 copy-start.2
  135.3 6.9 copy-start.3
  142.2 640.0 %copy-start.8 = (s32[5,10]{1,0:T(8,128)}, s32[5,10]{1,0:T(8,128)S(1)}, u32[]{:S(2)}) copy-start(s32[5,10]{1,0:T(8,128)S(1)} %stack.79.slots) | copy-start | bytes 604
  142.2 1.1 copy-start.4
  143.3 267.6 %copy-start.13 = (bf16[640,1536]{1,0:T(8,128)(2,1)S(1)}, bf16[640,1536]{1,0:T(8,128)(2,1)}, u32[]{:S(2)}) copy-start(bf16[640,1536]{1,0:T(8,128)(2,1)} %param.11) | copy-start | bytes 5898244
  410.9 8.4 copy-start.5
  410.9 8.4 copy-start.7
  419.9 3.9 copy-start.27
  420.0 4.7 copy-start.17
  423.8 1.5 copy-start.10
  423.8 2.2 copy-start.26
  423.8 114.9 %all-gather.8.cloned.1.call-start = ((), (), s32[]{:S(2)}) async-start(), calls=%async_computation.10 | async-start | bytes 9830400 | tf_op jit(solution)/shard_map/all_gather | solution.py:573
  424.6 315.8 %reduce-scatter.13.cloned.1.call-start = ((), (), s32[]{:S(2)}) async-start(), calls=%async_computation.11 | async-start | bytes 9830400 | tf_op jit(solution)/shard_map/reduce_scatter | solution.py:643
  426.1 0.6 copy-start.22
  621.7 141.2 %reduce-scatter.11.cloned.1.call-start = ((), (), s32[]{:S(2)}) async-start(), calls=%async_computation.9 | async-start | bytes 9830400 | tf_op jit(solution)/shard_map/reduce_scatter | solution.py:612
  647.0 394.0 %reduce-scatter.23.cloned.1.call-start = ((), (), s32[]{:S(2)}) async-start(), calls=%async_computation.17 | async-start | bytes 7077888 | tf_op jit(solution)/shard_map/reduce_scatter | solution.py:518
  670.9 655.7 %all-reduce.3.cloned.1.call-start = ((), (), s32[]{:S(2)}) async-start(), calls=%async_computation.20 | async-start | bytes 25165824
  732.8 0.8 copy-start.29
  732.8 7.5 copy-start.23
  732.8 7.6 copy-start.18
  732.8 7.6 copy-start.25
  732.8 7.6 copy-start.28
  732.8 645.3 %reduce-scatter.19.cloned.1.call-start = ((), (), s32[]{:S(2)}) async-start(), calls=%async_computation.14 | async-start | bytes 5898240 | tf_op jit(solution)/shard_map/reduce_scatter | solution.py:525
  740.3 22.6 %copy-start.35 = (f32[640]{0:T(1024)S(1)}, f32[640]{0:T(1024)}, u32[]{:S(2)}) copy-start(f32[640]{0:T(1024)} %get-tuple-element.78) | copy-start | bytes 7684
  762.9 6.9 copy-start.6
  769.8 5.5 copy-start.20
  782.0 0.7 copy-start.37
  782.0 1.6 copy-start.21
  782.1 668.2 %reduce-scatter.15.cloned.1.call-start = ((), (), s32[]{:S(2)}) async-start(), calls=%async_computation.12 | async-start | bytes 9830400 | tf_op jit(solution)/shard_map/reduce_scatter | solution.py:525
  863.5 131.1 %collective-permute-start = (bf16[10,128,1024]{2,1,0:T(8,128)(2,1)}, bf16[10,128,1024]{2,1,0:T(8,128)(2,1)S(1)}, u32[]{:S(2)}, u32[]{:S(2)}) collective-permute-start(bf16[10,128,1024]{2,1,0:T(8,128)(2,1)} %broadcast_select_fusion), channel_id=1, source_target_pairs={{0,2},{2,0},{1,3},{3,1},{4,6},{6,4},{5,7},{7,5},{8,10},{10,8},{9,1... | collective-permute-start | bytes 7864328 | tf_op jit(solution)/shard_map/ppermute | solution.py:466
  999.2 30.6 %copy-start.14 = (bf16[640,1536]{1,0:T(8,128)(2,1)S(1)}, bf16[640,1536]{1,0:T(8,128)(2,1)}, u32[]{:S(2)}) copy-start(bf16[640,1536]{1,0:T(8,128)(2,1)} %param.11) | copy-start | bytes 5898244
  999.2 30.6 %copy-start.19 = (bf16[640,1536]{1,0:T(8,128)(2,1)S(1)}, bf16[640,1536]{1,0:T(8,128)(2,1)}, u32[]{:S(2)}) copy-start(bf16[640,1536]{1,0:T(8,128)(2,1)} %get-tuple-element.26) | copy-start | bytes 5898244
  999.2 30.6 %copy-start.31 = (f32[1536]{0:T(1024)S(1)}, f32[1536]{0:T(1024)}, u32[]{:S(2)}) copy-start(f32[1536]{0:T(1024)} %copy-done.30) | copy-start | bytes 18436
  999.2 30.6 %copy-start.34 = (f32[640]{0:T(1024)S(1)}, f32[640]{0:T(1024)}, u32[]{:S(2)}) copy-start(f32[640]{0:T(1024)} %copy-done.33) | copy-start | bytes 7684
  999.3 29.7 %collective-permute-start.1 = (bf16[5,128,1024]{2,1,0:T(8,128)(2,1)S(1)}, bf16[5,128,1024]{2,1,0:T(8,128)(2,1)S(1)}, u32[]{:S(2)}, u32[]{:S(2)}) collective-permute-start(bf16[5,128,1024]{2,1,0:T(8,128)(2,1)S(1)} %select_convert_fusion), channel_id=1, source_target_pairs={{0,1},{1,0},{2,3},{3,2},{4,5},{5,4},{6,7},{7,6},{8,9},{9,8},{10,11... | collective-permute-start | bytes 3932168 | tf_op jit(solution)/shard_map/ppermute | solution.py:466
  1040.9 1.5 copy-start.11
  1040.9 440.0 %all-gather.12.cloned.1.call-start = ((), (), s32[]{:S(2)}) async-start(), calls=%async_computation.18 | async-start | bytes 3932160 | tf_op jit(solution)/shard_map/all_gather | solution.py:519
  1041.6 503.5 %reduce-scatter.25.cloned.1.call-start = ((), (), s32[]{:S(2)}) async-start(), calls=%async_computation.19 | async-start | bytes 884736
  1042.4 2.7 copy-start.15
  1045.1 10.9 copy-start.39
  1055.9 539.2 %all-gather.10.cloned.1.call-start = ((), (), s32[]{:S(2)}) async-start(), calls=%async_computation.16 | async-start | bytes 7864320 | tf_op jit(solution)/shard_map/all_gather | solution.py:519
  1330.2 329.6 %reduce-scatter.21.cloned.1.call-start = ((), (), s32[]{:S(2)}) async-start(), calls=%async_computation.15 | async-start | bytes 1327104 | tf_op jit(solution)/shard_map/reduce_scatter | solution.py:526
  1378.2 351.1 %reduce-scatter.17.cloned.1.call-start = ((), (), s32[]{:S(2)}) async-start(), calls=%async_computation.13 | async-start | bytes 2211840 | tf_op jit(solution)/shard_map/reduce_scatter | solution.py:526
  1450.3 36.2 %copy-start.16 = (bf16[640,1536]{1,0:T(8,128)(2,1)S(1)}, bf16[640,1536]{1,0:T(8,128)(2,1)}, u32[]{:S(2)}) copy-start(bf16[640,1536]{1,0:T(8,128)(2,1)} %param.11) | copy-start | bytes 5898244
  1450.3 36.2 %copy-start.32 = (f32[640]{0:T(1024)S(1)}, f32[640]{0:T(1024)}, u32[]{:S(2)}) copy-start(f32[640]{0:T(1024)} %get-tuple-element.76) | copy-start | bytes 7684
  1480.9 5.6 copy-start.12
  1595.1 147.2 %copy-start.1 = (bf16[16,64,1536]{2,1,0:T(8,128)(2,1)S(1)}, bf16[16,64,1536]{2,1,0:T(8,128)(2,1)}, u32[]{:S(2)}) copy-start(bf16[16,64,1536]{2,1,0:T(8,128)(2,1)} %param.17) | copy-start | bytes 9437188
Sparse Core Ops, SparseCore 0:
  423.9 57.8 all-gather.5
  483.4 55.3 all-gather.7
  621.8 68.5 reduce-scatter.12
  693.0 69.8 reduce-scatter.10
  766.9 132.1 reduce-scatter.22
  903.1 423.5 all-reduce.2
  1329.3 48.7 reduce-scatter.18
  1381.2 68.9 reduce-scatter.14
  1451.9 28.9 all-gather.11
  1485.0 60.0 reduce-scatter.24
  1547.2 47.7 all-gather.9
  1598.3 61.4 reduce-scatter.20
  1663.3 65.8 reduce-scatter.16

commit v3 on v2

--- a/solution.py
+++ b/solution.py
@@ -75,60 +75,45 @@
     for j,t in enumerate(unstack_heads(o6)):
         o_ref[pl.ds(row,SEG),pl.ds(pl.multiple_of((3*pair+j)*LANES,LANES),LANES)]=t.astype(o_ref.dtype)
     return c
-def bwd_kernel(depth, slots, bias, inv, q_ref, kv_ref, o_ref, do_ref, lse_ref, dq_ref, dkv_ref, path, p_scr, d_scr):
+def bwd_step(depth, slots, bias, q_ref, kv_ref, o_ref, do_ref, lse_ref, dq_ref, path, p_scr, d_scr, i, c):
     width=6*SEG
-    segs=q_ref.shape[0]//SEG
-    path[:,depth]=jnp.zeros((segs,)+path.shape[2:],path.dtype)
-    def step(i,c):
-        seg=i//PAIRS; pair=i%PAIRS
-        row=pl.multiple_of(seg*SEG,SEG)
-        q6=stack_heads(q_ref,row,pair,HD**-0.5).astype(jnp.bfloat16)
-        do6f=stack_heads(do_ref,row,pair)
-        do6=do6f.astype(jnp.bfloat16)
-        prod=do6f*stack_heads(o_ref,row,pair)
-        hi=prod.astype(jnp.bfloat16); lo=(prod-hi.astype(jnp.float32)).astype(jnp.bfloat16)
-        ones=jnp.ones((8,LANES),jnp.bfloat16)
-        delta=(dot(ones,hi,NT)+dot(ones,lo,NT))[:1]
-        lse=lse_ref[i][:1]
-        kcol=pl.multiple_of(pair*LANES,LANES); vcol=pl.multiple_of(KVH*HD+pair*LANES,LANES)
-        for lev in range(depth):
-            k=kv_ref[slots[seg,lev],:,pl.ds(kcol,LANES)]
-            v=kv_ref[slots[seg,lev],:,pl.ds(vcol,LANES)]
-            s=dot(k,q6,NT)
-            s=s+(causal_bias(width) if lev==0 else bias[seg,lev])
-            p=jnp.exp(s-lse)
-            dp=dot(v,do6,NT)
-            ds=(p*(dp-delta)).astype(jnp.bfloat16)
-            p_scr[lev*SEG:(lev+1)*SEG,:]=p.astype(jnp.bfloat16)
-            d_scr[lev*SEG:(lev+1)*SEG,:]=ds
-        dv=dot(p_scr[...],do6,NN)
-        dk=dot(d_scr[...],q6,NN)
-        for lev in range(depth):
-            path[seg,lev,:,pl.ds(kcol,LANES)]=dk[lev*SEG:(lev+1)*SEG].astype(path.dtype)
-            path[seg,lev,:,pl.ds(vcol,LANES)]=dv[lev*SEG:(lev+1)*SEG].astype(path.dtype)
-        k=kv_path(kv_ref,slots,seg,depth,pair*LANES)
-        dq6=(dot(k,d_scr[...],TN)*(HD**-0.5)).T
-        for j,t in enumerate(unstack_heads(dq6)):
-            dq_ref[pl.ds(row,SEG),pl.ds(pl.multiple_of((3*pair+j)*LANES,LANES),LANES)]=t.astype(dq_ref.dtype)
-        return c
-    lax.fori_loop(0,segs*PAIRS,step,0)
-    def collect(slot,c):
-        for col in range(0,2*KVH*HD,256):
-            tot=path[0,inv[slot,0],:,col:col+256].astype(jnp.float32)
-            for seg in range(1,segs): tot=tot+path[seg,inv[slot,seg],:,col:col+256].astype(jnp.float32)
-            dkv_ref[slot,:,col:col+256]=tot.astype(dkv_ref.dtype)
-        return c
-    lax.fori_loop(0,dkv_ref.shape[0],collect,0)
-def attn_bwd(slots,bias,inv,q,kv,o,do,lse,depth):
-    T=q.shape[0]; segs=T//SEG
-    V=pl.BlockSpec(memory_space=pltpu.VMEM); S=pl.BlockSpec(memory_space=pltpu.SMEM)
-    return pl.pallas_call(functools.partial(bwd_kernel,depth),
-        out_shape=(jax.ShapeDtypeStruct(q.shape,jnp.bfloat16),jax.ShapeDtypeStruct(kv.shape,jnp.bfloat16)),
-        in_specs=[S,S,S,V,V,V,V,V],out_specs=(V,V),
-        scratch_shapes=[pltpu.VMEM((segs,depth+1,SEG,2*KVH*HD),jnp.bfloat16),pltpu.VMEM((depth*SEG,6*SEG),jnp.bfloat16),pltpu.VMEM((depth*SEG,6*SEG),jnp.bfloat16)],
-        compiler_params=pltpu.CompilerParams(vmem_limit_bytes=60*2**20))(slots,bias,inv,q,kv,o,do,lse)
-
-
+    seg=i//PAIRS; pair=i%PAIRS
+    row=pl.multiple_of(seg*SEG,SEG)
+    q6=stack_heads(q_ref,row,pair,HD**-0.5).astype(jnp.bfloat16)
+    do6f=stack_heads(do_ref,row,pair)
+    do6=do6f.astype(jnp.bfloat16)
+    prod=do6f*stack_heads(o_ref,row,pair)
+    hi=prod.astype(jnp.bfloat16); lo=(prod-hi.astype(jnp.float32)).astype(jnp.bfloat16)
+    ones=jnp.ones((8,LANES),jnp.bfloat16)
+    delta=(dot(ones,hi,NT)+dot(ones,lo,NT))[:1]
+    lse=lse_ref[i][:1]
+    kcol=pl.multiple_of(pair*LANES,LANES); vcol=pl.multiple_of(KVH*HD+pair*LANES,LANES)
+    for lev in range(depth):
+        k=kv_ref[slots[seg,lev],:,pl.ds(kcol,LANES)]
+        v=kv_ref[slots[seg,lev],:,pl.ds(vcol,LANES)]
+        s=dot(k,q6,NT)
+        s=s+(causal_bias(width) if lev==0 else bias[seg,lev])
+        p=jnp.exp(s-lse)
+        dp=dot(v,do6,NT)
+        ds=(p*(dp-delta)).astype(jnp.bfloat16)
+        p_scr[lev*SEG:(lev+1)*SEG,:]=p.astype(jnp.bfloat16)
+        d_scr[lev*SEG:(lev+1)*SEG,:]=ds
+    dv=dot(p_scr[...],do6,NN)
+    dk=dot(d_scr[...],q6,NN)
+    for lev in range(depth):
+        path[seg,lev,:,pl.ds(kcol,LANES)]=dk[lev*SEG:(lev+1)*SEG].astype(path.dtype)
+        path[seg,lev,:,pl.ds(vcol,LANES)]=dv[lev*SEG:(lev+1)*SEG].astype(path.dtype)
+    k=kv_path(kv_ref,slots,seg,depth,pair*LANES)
+    dq6=(dot(k,d_scr[...],TN)*(HD**-0.5)).T
+    for j,t in enumerate(unstack_heads(dq6)):
+        dq_ref[pl.ds(row,SEG),pl.ds(pl.multiple_of((3*pair+j)*LANES,LANES),LANES)]=t.astype(dq_ref.dtype)
+    return c
+def bwd_collect(inv, path, group, slot, c):
+    for col in range(0,2*KVH*HD,256):
+        tot=path[0,inv[slot,0],:,col:col+256].astype(jnp.float32)
+        for seg in range(1,path.shape[0]): tot=tot+path[seg,inv[slot,seg],:,col:col+256].astype(jnp.float32)
+        group[slot,:,col:col+256]=tot.astype(group.dtype)
+    return c
 MESH = pl.DeviceIdType.MESH
 ANY = pl.BlockSpec(memory_space=pl.ANY)
 VMEM = pl.BlockSpec(memory_space=pltpu.VMEM)
@@ -281,15 +266,18 @@
         self.diagonal = lax.rem(self.near + 2, 4)
         self.sends = Sends()
         self.blocks = []
+        self.passed = []
+        self.sources = None
 
     def arrived(self, cond, block, index):
         for n in self.arrays:
             here = self.region(n, self.rep, block)
+            src = here if self.sources is None else self.sources[n]
             self.sends.start(
-                cond, here, here, self.cross.at[0, block, n], self.cross.at[1, block, n], {"rep": self.far}
+                cond, src, here, self.cross.at[0, block, n], self.cross.at[1, block, n], {"rep": self.far}
             )
             self.sends.start(
-                cond, here, here, self.core.at[0, block, n], self.core.at[1, block, n], {"rep": self.near}
+                cond, src, here, self.core.at[0, block, n], self.core.at[1, block, n], {"rep": self.near}
             )
         self.blocks.append((cond, block))
 
@@ -301,7 +289,7 @@
                 self.sends.start(
                     cond, here, here, self.relay.at[0, block, n], self.relay.at[1, block, n], {"rep": self.near}
                 )
-        self.passed = getattr(self, "passed", []) + self.blocks
+        self.passed = self.passed + self.blocks
         self.blocks = []
 
     def end(self):
@@ -456,14 +444,407 @@
     )(slots, bias, q, kv, gate_up, down)
 
 
-def partner(block, axis, stride):
-    count = lax.axis_size(axis)
-    route = []
-    for low in range(count):
-        high = low | 1 << stride
-        if high != low and high < count:
-            route += [(low, high), (high, low)]
-    return lax.ppermute(block, axis, route)
+class LineScatter:
+    def __init__(self, shards, arrays, local, pair_buf, line_buf, temp, stages, outs, pair, line, loads, ready=None):
+        self.shards, self.arrays, self.local = shards, arrays, local
+        self.pair_buf, self.line_buf, self.temp = pair_buf, line_buf, temp
+        self.stages, self.outs = stages, outs
+        self.pair, self.line, self.loads = pair, line, loads
+        self.ready = ready or (lambda block: None)
+        self.sends = Sends()
+        self.me, self.spot, self.length = line_place(shards)
+        self.side = self.me % 2
+        self.twin = self.me + 1 - 2 * self.side
+
+    def add(self, n, sources, target):
+        stage, out = self.stages[n], self.outs[n]
+        copies = []
+        for k, (cond, ref) in enumerate(sources):
+            copy = pltpu.make_async_copy(ref, stage.at[k], self.loads.at[k])
+            copies.append((cond, copy))
+            when(cond, copy.start)
+        outer, rows, width = out.shape
+        chunk = 32 if rows % 32 == 0 else rows
+        pieces = rows // chunk
+
+        def clear(k):
+            def one(i, c):
+                row = pl.multiple_of(i % pieces * chunk, chunk)
+                stage[k, i // pieces, pl.ds(row, chunk)] = jnp.zeros((chunk, width), stage.dtype)
+                return c
+
+            lax.fori_loop(0, outer * pieces, one, 0)
+
+        for k, (cond, copy) in enumerate(copies):
+            when(cond, copy.wait)
+            if cond is not None:
+                pl.when(jnp.logical_not(cond))(functools.partial(clear, k))
+
+        def one(i, c):
+            row = pl.multiple_of(i % pieces * chunk, chunk)
+            total = stage[0, i // pieces, pl.ds(row, chunk)].astype(jnp.float32)
+            for k in range(1, len(sources)):
+                total = total + stage[k, i // pieces, pl.ds(row, chunk)].astype(jnp.float32)
+            out[i // pieces, pl.ds(row, chunk)] = total.astype(out.dtype)
+            return c
+
+        lax.fori_loop(0, outer * pieces, one, 0)
+        store = pltpu.make_async_copy(out, target, self.loads.at[self.loads.shape[0] - 1])
+        store.start()
+        store.wait()
+
+    def begin(self):
+        order = []
+        for step in range(self.length):
+            for target in (self.length - 1 - step, step):
+                if target not in order:
+                    order.append(target)
+        for target in order:
+            block = 2 * target + 1 - self.side
+            self.ready(block)
+            for n in range(self.arrays):
+                sources = self.local(n, block)
+                src = sources[0]
+                if len(sources) > 1:
+                    src = self.temp[n].at[target]
+                    self.add(n, [(None, ref) for ref in sources], src)
+                self.sends.start(
+                    None,
+                    src,
+                    self.pair_buf[n].at[target],
+                    self.pair.at[0, target, n],
+                    self.pair.at[1, target, n],
+                    {"shard": self.twin},
+                )
+
+    def got_pair(self, target, n):
+        received(
+            None,
+            self.pair_buf[n].at[target],
+            self.pair.at[0, target, n],
+            self.pair.at[1, target, n],
+            {"shard": self.twin},
+        )
+
+    def got_line(self, cond, slot, n, device):
+        received(cond, self.line_buf[n].at[slot], self.line.at[0, slot, n], self.line.at[1, slot, n], {"shard": device})
+
+    def step(self, step):
+        below, above = self.spot > 0, self.spot + 1 < self.length
+        turns = (
+            (self.length - 1 - step, True, below, self.me - 2, self.me + 2),
+            (step, False, above, self.me + 2, self.me - 2),
+        )
+        for target, rising, has, source, device in turns:
+            cond = self.spot < target if rising else self.spot > target
+            block = 2 * target + self.side
+            slot = target if rising else jnp.where(self.spot == target + 1, self.length, target)
+            for n in range(self.arrays):
+                copy = pltpu.make_async_remote_copy(
+                    src_ref=self.pair_buf[n].at[target],
+                    dst_ref=self.line_buf[n].at[slot],
+                    send_sem=self.line.at[0, slot, n],
+                    recv_sem=self.line.at[1, slot, n],
+                    device_id={"shard": device},
+                    device_id_type=MESH,
+                )
+
+                def body(n=n, copy=copy, target=target, has=has, source=source, block=block):
+                    self.got_pair(target, n)
+                    self.got_line(has, target, n, source)
+                    if n == 0:
+                        self.ready(block)
+                    sources = [(None, ref) for ref in self.local(n, block)]
+                    sources += [(None, self.pair_buf[n].at[target]), (has, self.line_buf[n].at[target])]
+                    self.add(n, sources, self.pair_buf[n].at[target])
+                    copy.start()
+
+                pl.when(cond)(body)
+                self.sends.open.append((cond, copy.wait_send))
+
+    def finish(self, targets):
+        below, above = self.spot > 0, self.spot + 1 < self.length
+        self.ready(self.me)
+        for n in range(self.arrays):
+            self.got_pair(self.spot, n)
+            self.got_line(below, self.spot, n, self.me - 2)
+            self.got_line(above, self.length, n, self.me + 2)
+            sources = [(None, ref) for ref in self.local(n, self.me)]
+            sources += [
+                (None, self.pair_buf[n].at[self.spot]),
+                (below, self.line_buf[n].at[self.spot]),
+                (above, self.line_buf[n].at[self.length]),
+            ]
+            self.add(n, sources, targets[n])
+
+
+def scatter_sems(shards, arrays, loads):
+    length = shards // 2
+    return [
+        pltpu.SemaphoreType.DMA((2, length, arrays)),
+        pltpu.SemaphoreType.DMA((2, length + 1, arrays)),
+        pltpu.SemaphoreType.DMA((loads + 1,)),
+    ]
+
+
+def scatter_buffers(shards, block):
+    length = shards // 2
+    return [
+        jax.ShapeDtypeStruct((length,) + block, jnp.bfloat16),
+        jax.ShapeDtypeStruct((length + 1,) + block, jnp.bfloat16),
+    ]
+
+
+def back_kernel(
+    depth,
+    shards,
+    slots,
+    bias,
+    inv,
+    q_ref,
+    kv_ref,
+    o_ref,
+    do_ref,
+    lse_ref,
+    gu_ref,
+    dn_ref,
+    dq_ref,
+    dkv_ref,
+    gu_out,
+    dn_out,
+    gu_pair,
+    gu_line,
+    dn_pair,
+    dn_line,
+    path,
+    p_scr,
+    d_scr,
+    group,
+    guest,
+    gu_stage,
+    dn_stage,
+    gu_sum,
+    dn_sum,
+    kv_sems,
+    pair,
+    line,
+    loads,
+):
+    me = lax.axis_index("shard")
+    first = me // TREE_DEVS * TREE_DEVS
+    member = me % TREE_DEVS
+    segs = q_ref.shape[0] // SEG
+    others = [first + lax.rem(member + away, TREE_DEVS) for away in range(1, TREE_DEVS)]
+    greet(line_neighbours(shards) + [(None, {"shard": other}) for other in others])
+    scatter = LineScatter(
+        shards,
+        2,
+        lambda n, block: [(gu_ref, dn_ref)[n].at[:, block]],
+        (gu_pair, dn_pair),
+        (gu_line, dn_line),
+        None,
+        (gu_stage, dn_stage),
+        (gu_sum, dn_sum),
+        pair,
+        line,
+        loads,
+    )
+    scatter.begin()
+    path[:, depth] = jnp.zeros((segs,) + path.shape[2:], path.dtype)
+    step = functools.partial(
+        bwd_step, depth, slots, bias, q_ref, kv_ref, o_ref, do_ref, lse_ref, dq_ref, path, p_scr, d_scr
+    )
+    lax.fori_loop(0, segs * PAIRS, step, 0)
+    lax.fori_loop(0, group.shape[0], functools.partial(bwd_collect, inv, path, group), 0)
+    sends = Sends()
+    for away, other in enumerate(others):
+        target = lax.rem(member + away + 1, TREE_DEVS)
+        sends.start(
+            None,
+            group.at[pl.ds(target * segs, segs)],
+            guest.at[away],
+            kv_sems.at[0, away],
+            kv_sems.at[1, away],
+            {"shard": other},
+        )
+    for turn in range(scatter.length):
+        scatter.step(turn)
+    for away in range(TREE_DEVS - 1):
+        source = first + lax.rem(member + TREE_DEVS - 1 - away, TREE_DEVS)
+        received(None, guest.at[away], kv_sems.at[0, away], kv_sems.at[1, away], {"shard": source})
+
+    def join(seg, c):
+        for col in range(0, 2 * KVH * HD, 256):
+            total = group[member * segs + seg, :, col : col + 256].astype(jnp.float32)
+            for away in range(TREE_DEVS - 1):
+                total = total + guest[away, seg, :, col : col + 256].astype(jnp.float32)
+            dkv_ref[seg, :, col : col + 256] = total.astype(dkv_ref.dtype)
+        return c
+
+    lax.fori_loop(0, segs, join, 0)
+    scatter.finish((gu_out, dn_out))
+    sends.drain()
+    scatter.sends.drain()
+
+
+def attend_back(slots, bias, inv, q, kv, o, do, lse, gate_up_grad, down_grad, depth, shards):
+    segs = q.shape[0] // SEG
+    own_kv = (segs,) + kv.shape[1:]
+    gu_block = (gate_up_grad.shape[0],) + gate_up_grad.shape[2:]
+    dn_block = (down_grad.shape[0],) + down_grad.shape[2:]
+    outs = [
+        jax.ShapeDtypeStruct(q.shape, jnp.bfloat16),
+        jax.ShapeDtypeStruct(own_kv, jnp.bfloat16),
+        jax.ShapeDtypeStruct(gu_block, jnp.bfloat16),
+        jax.ShapeDtypeStruct(dn_block, jnp.bfloat16),
+    ]
+    outs += scatter_buffers(shards, gu_block) + scatter_buffers(shards, dn_block)
+    return pl.pallas_call(
+        functools.partial(back_kernel, depth, shards),
+        out_shape=outs,
+        in_specs=[SMEM] * 3 + [VMEM] * 5 + [ANY] * 2,
+        out_specs=[VMEM] * 2 + [ANY] * 6,
+        scratch_shapes=[
+            pltpu.VMEM((segs, depth + 1, SEG, 2 * KVH * HD), jnp.bfloat16),
+            pltpu.VMEM((depth * SEG, 6 * SEG), jnp.bfloat16),
+            pltpu.VMEM((depth * SEG, 6 * SEG), jnp.bfloat16),
+            pltpu.VMEM(kv.shape, jnp.bfloat16),
+            pltpu.VMEM((TREE_DEVS - 1,) + own_kv, jnp.bfloat16),
+            pltpu.VMEM((4,) + gu_block, jnp.bfloat16),
+            pltpu.VMEM((4,) + dn_block, jnp.bfloat16),
+            pltpu.VMEM(gu_block, jnp.bfloat16),
+            pltpu.VMEM(dn_block, jnp.bfloat16),
+            pltpu.SemaphoreType.DMA((2, TREE_DEVS - 1)),
+        ]
+        + scatter_sems(shards, 2, 4),
+        compiler_params=pltpu.CompilerParams(
+            collective_id=3, has_side_effects=True, vmem_limit_bytes=60 * 2**20
+        ),
+    )(slots, bias, inv, q, kv, o, do, lse, gate_up_grad, down_grad)[:4]
+
+
+def finish_kernel(
+    shards,
+    grad_ref,
+    gu_ref,
+    dn_ref,
+    grad_out,
+    gu_out,
+    dn_out,
+    core_buf,
+    share_buf,
+    cross_buf,
+    pair_buf,
+    line_buf,
+    temp_buf,
+    stage,
+    total,
+    core_sems,
+    swap_sems,
+    own_sems,
+    cross,
+    core,
+    relay,
+    pair,
+    line,
+    loads,
+):
+    rep = lax.axis_index("rep")
+    near = rep + 1 - 2 * (rep % 2)
+    far = lax.rem(rep + 2, 4)
+    half = rep % 2
+    greet(line_neighbours(shards) + rep_neighbours())
+    sends = Sends()
+    length = shards // 2
+    order = []
+    for step in range(length):
+        for target in (length - 1 - step, step):
+            if target not in order:
+                order.append(target)
+    side = lax.axis_index("shard") % 2
+    for turn in (1 - side, side):
+        for target in order:
+            block = 2 * target + turn
+            sends.start(
+                None,
+                grad_ref.at[1 - half, block],
+                core_buf.at[block],
+                core_sems.at[0, block],
+                core_sems.at[1, block],
+                {"rep": near},
+            )
+    experts = (gu_out, dn_out)
+    for n, src in enumerate((gu_ref, dn_ref)):
+        sends.local(src, experts[n].at[rep], own_sems.at[n])
+    spread = RepSpread((0, 1), lambda n, part, block: experts[n].at[part], cross, core, relay)
+    spread.sources = (gu_ref, dn_ref)
+    spread.arrived(None, 0, 0)
+
+    def ready(block):
+        received(None, core_buf.at[block], core_sems.at[0, block], core_sems.at[1, block], {"rep": near})
+
+    scatter = LineScatter(
+        shards,
+        1,
+        lambda n, block: [grad_ref.at[half, block], core_buf.at[block]],
+        (pair_buf,),
+        (line_buf,),
+        (temp_buf,),
+        (stage,),
+        (total,),
+        pair,
+        line,
+        loads,
+        ready,
+    )
+    scatter.begin()
+    for turn in range(scatter.length):
+        scatter.step(turn)
+    scatter.finish((share_buf,))
+    sends.start(None, share_buf, cross_buf, swap_sems.at[0, 0], swap_sems.at[1, 0], {"rep": far})
+    spread.end()
+    received(None, cross_buf, swap_sems.at[0, 0], swap_sems.at[1, 0], {"rep": far})
+    scatter.add(0, [(None, share_buf), (None, cross_buf)], grad_out.at[half])
+    sends.start(None, grad_out.at[half], grad_out.at[half], swap_sems.at[0, 1], swap_sems.at[1, 1], {"rep": near})
+    received(None, grad_out.at[1 - half], swap_sems.at[0, 1], swap_sems.at[1, 1], {"rep": near})
+    sends.drain()
+    scatter.sends.drain()
+
+
+def finish_grads(grad, gate_up_share, down_share, reps):
+    halves, shards = grad.shape[:2]
+    block = grad.shape[2:]
+
+    def shape(*dims):
+        return jax.ShapeDtypeStruct(dims, jnp.bfloat16)
+
+    outs = [
+        shape(halves, *block),
+        shape(reps, *gate_up_share.shape),
+        shape(reps, *down_share.shape),
+        shape(shards, *block),
+        shape(*block),
+        shape(*block),
+    ]
+    outs += scatter_buffers(shards, block) + [shape(shards // 2, *block)]
+    return pl.pallas_call(
+        functools.partial(finish_kernel, shards),
+        out_shape=outs,
+        in_specs=[ANY] * 3,
+        out_specs=[ANY] * len(outs),
+        scratch_shapes=[
+            pltpu.VMEM((5,) + block, jnp.bfloat16),
+            pltpu.VMEM(block, jnp.bfloat16),
+            pltpu.SemaphoreType.DMA((2, shards)),
+            pltpu.SemaphoreType.DMA((2, 2)),
+            pltpu.SemaphoreType.DMA((2,)),
+        ]
+        + rep_sems(1, 2)
+        + scatter_sems(shards, 1, 5),
+        compiler_params=pltpu.CompilerParams(
+            collective_id=4, has_side_effects=True, vmem_limit_bytes=32 * 2**20
+        ),
+    )(grad, gate_up_share, down_share)[:3]
 
 
 def norm_rows(values, gain):
@@ -514,18 +895,8 @@
     return depth - jnp.sum(jnp.where(hit, depth - levels, 0), axis=2)
 
 
-def spread_experts(grad):
-    share = lax.psum_scatter(grad.astype(jnp.bfloat16), "shard", scatter_dimension=1, tiled=True)
-    return lax.all_gather(share, "rep", axis=0, tiled=True).astype(jnp.float32)
-
-
-def spread_columns(grad, rep_count):
-    rows, width = grad.shape
-    pieces = grad.astype(jnp.bfloat16).reshape(rows, rep_count, width // rep_count).transpose(1, 0, 2)
-    part = lax.psum_scatter(pieces, "rep", scatter_dimension=0, tiled=True)[0]
-    share = lax.psum_scatter(part, "shard", scatter_dimension=0, tiled=True)
-    whole = lax.all_gather(share, "rep", axis=1, tiled=True)
-    return whole.astype(jnp.float32)
+def w_total(width_q, width_kv):
+    return width_q + 2 * width_kv + D
 
 
 def shards(
@@ -580,8 +951,6 @@
     projected = projected.reshape(token_count, width_q + 2 * width_kv)
     queries = projected[:, :width_q].astype(jnp.bfloat16)
     own_kv = projected[:, width_q:].astype(jnp.bfloat16).reshape(seg_dev, SEG, 2 * width_kv)
-    low_first = member % 2 == 0
-    pair_first = member // 2 == 0
     bias = jnp.where(path_alive, 0.0, NEG).astype(jnp.float32)
     attended, log_totals, group_kv, w_gate_up, w_down = attend_gather(
         path_slots, bias, queries, own_kv, gate_up_own, down_own, depth, shard_count
@@ -635,8 +1004,6 @@
     gate_up_grad = jnp.einsum(
         "td,etf->edf", act_all, gate_up_grad_rows, preferred_element_type=jnp.float32
     )
-    down_grad = spread_experts(down_grad)
-    gate_up_grad = spread_experts(gate_up_grad)
     act_part = jnp.einsum(
         "etf,edf->td", gate_up_grad_rows, w_gate_up, preferred_element_type=jnp.float32
     )
@@ -661,7 +1028,7 @@
         w_out,
         preferred_element_type=jnp.float32,
     ).astype(jnp.bfloat16)
-    query_grad, group_grad = attn_bwd(
+    query_grad, own_grad, gate_up_share, down_share = attend_back(
         path_slots,
         bias,
         path_levels(path_slots, path_alive, group_size),
@@ -670,18 +1037,13 @@
         attended,
         attended_grad,
         log_totals,
+        gate_up_grad.astype(jnp.bfloat16).reshape(own_experts, shard_count, -1, 2 * FF),
+        down_grad.astype(jnp.bfloat16).reshape(own_experts, shard_count, -1, D),
         depth,
-    )
-    pair_part = jnp.where(pair_first, group_grad[: 2 * seg_dev], group_grad[2 * seg_dev :])
-    far_part = jnp.where(pair_first, group_grad[2 * seg_dev :], group_grad[: 2 * seg_dev])
-    pair_sum = pair_part.astype(jnp.float32) + partner(far_part, "shard", 1).astype(jnp.float32)
-    own_part = jnp.where(low_first, pair_sum[:seg_dev], pair_sum[seg_dev:])
-    near_part = jnp.where(low_first, pair_sum[seg_dev:], pair_sum[:seg_dev])
-    own_grad = own_part + partner(near_part.astype(jnp.bfloat16), "shard", 0).astype(
-        near_part.dtype
+        shard_count,
     )
     projected_grad = jnp.concatenate(
-        [query_grad, own_grad.reshape(token_count, 2 * width_kv).astype(jnp.bfloat16)], axis=1
+        [query_grad, own_grad.reshape(token_count, 2 * width_kv)], axis=1
     )
     qkv_grad = jnp.dot(act_first.T, projected_grad, preferred_element_type=jnp.float32)
     act_first_grad = jnp.einsum(
@@ -694,13 +1056,34 @@
         token_values, scale_first, gains[0].astype(jnp.float32), act_first_grad
     )
     token_grad = residual_grad + through_first
-    gains_grad = jnp.stack([gain_grad_first, gain_grad_second], axis=1)
-    small = jnp.concatenate([gains_grad, router_grad], axis=1)
-    small = lax.psum_scatter(small, "shard", scatter_dimension=0, tiled=True)
-    small = lax.psum(small, "rep")
-    qkv_grad = spread_columns(qkv_grad, rep_count)
-    out_grad = spread_columns(out_grad, rep_count)
-    return (block_out, token_grad, small[:, :2].T, qkv_grad, out_grad, small[:, 2:], gate_up_grad, down_grad)
+    width = 2 * LANES * -(-(w_total(width_q, width_kv) + E + 2) // (2 * LANES))
+    padding = jnp.zeros((D, width - w_total(width_q, width_kv) - E - 2), jnp.float32)
+    joined = jnp.concatenate(
+        [
+            qkv_grad,
+            out_grad,
+            gain_grad_first[:, None],
+            gain_grad_second[:, None],
+            router_grad,
+            padding,
+        ],
+        axis=1,
+    ).astype(jnp.bfloat16)
+    joined = joined.reshape(shard_count, 1, D // shard_count, 2, width // 2).transpose(3, 0, 1, 2, 4)
+    joined, gate_up_grad, down_grad = finish_grads(joined, gate_up_share, down_share, rep_count)
+    joined = joined.transpose(1, 2, 0, 3).reshape(D // shard_count, width).astype(jnp.float32)
+    at_out = width_q + 2 * width_kv
+    at_small = at_out + D
+    return (
+        block_out,
+        token_grad,
+        joined[:, at_small : at_small + 2].T,
+        joined[:, :at_out],
+        joined[:, at_out:at_small],
+        joined[:, at_small + 2 : at_small + 2 + E],
+        gate_up_grad.reshape((E,) + gate_up_grad.shape[2:]).astype(jnp.float32),
+        down_grad.reshape((E,) + down_grad.shape[2:]).astype(jnp.float32),
+    )
 
 
 def solution(mesh):

time: 1760 us -> 1370 us (0.78)
  waiting for transfers between devices: 862 us -> 80.2 us
  Pallas kernels: 427 us -> 841 us
  local copies, waits for them, and re-layouts: 74.7 us -> 111 us
  blocking collectives: 47.7 us -> 13.6 us
  other arithmetic: 51.9 us -> 33.4 us
    pallas_call x1 -> x2, Pallas kernels: 68.3 us -> 482 us  [the longest x1 325 us: attend_back(): pl.pallas_call(functools.partial(back_kernel, depth, shards), out_shape=o...]
    unnamed x15 -> x4, waiting for transfers between devices: 325 us -> 0.75 us
    reduce_scatter x5 -> x0, waiting for transfers between devices: 234 us -> none  [the longest x2 120 us: spread_columns(): part = lax.psum_scatter(pieces, 'rep', scatter_dimension=0, tiled=True)[0]]
    ppermute x2 -> x0, waiting for transfers between devices: 159 us -> none  [partner(): return lax.ppermute(block, axis, route)]
    all_gather x2 -> x0, waiting for transfers between devices: 66 us -> none  [spread_experts(): return lax.all_gather(share, 'rep', axis=0, tiled=True).astype(jnp.float32)]
    convert_element_type x1 -> x4, local copies, waits for them, and re-layouts: 22 us -> 50.7 us  [the longest x2 31.3 us: shards(): joined = jnp.concatenate([qkv_grad, out_grad, gain_grad_first[:, None], g...]
    all_gather x2 -> x0, blocking collectives: 21.6 us -> none  [spread_columns(): whole = lax.all_gather(share, 'rep', axis=1, tiled=True)]
    concatenate x0 -> x1, local copies, waits for them, and re-layouts: none -> 19.7 us  [shards(): jnp.concatenate([qkv_grad, out_grad, gain_grad_first[:, None], gain_grad_...]
  transfers between devices with their start and end apart: 15 -> 4, of which waited for: 13 -> 3; matrix products, arithmetic and copies ran while one was open for 14% -> 12% of each run, Pallas kernels for 4% -> 0%
where the time goes in v3:
time: 1370 us
  Pallas kernels  841 us (61%)
  matrix products  271 us (20%)
  local copies, waits for them, and re-layouts  111 us (8%)
  waiting for transfers between devices  80.2 us (6%)
  other arithmetic  33.4 us (2%)
  between operations  14.6 us (1%)
    pallas_call x1, Pallas kernels, attend_back(): pl.pallas_call(functools.partial(back_kernel, depth, shards), out_shape=o...  325 us
    pallas_call x1, Pallas kernels, attend_gather(): pl.pallas_call(functools.partial(attend_gather_kernel, depth, shards), ou...  268 us
    pallas_call x1, Pallas kernels, finish_grads(): pl.pallas_call(functools.partial(finish_kernel, shards), out_shape=outs,...  157 us
    pallas_call x1, Pallas kernels, gather_weights(): pl.pallas_call(functools.partial(weights_kernel, shards), out_shape=[jax....  91.1 us
    all_gather x1, waiting for transfers between devices, shards(): act_all = lax.all_gather(act_second, 'rep', axis=0, tiled=True)  48.1 us
    dot_general x1, matrix products, shards(): jnp.einsum('td,edf->etf', act_all, w_gate_up, preferred_element_type=jnp....  41.5 us
    dot_general x1, matrix products, shards(): jnp.einsum('etf,edf->td', gate_up_grad_rows, w_gate_up, preferred_element...  41.2 us
    dot_general x1, matrix products, shards(): jnp.einsum('td,efd->etf', cot_all, w_down, preferred_element_type=jnp.flo...  41.2 us
  transfers between devices with their start and end apart: 4, of which 3 were waited for; matrix products, arithmetic and copies ran while one was open for 12% of the time, Pallas kernels for 0%

profile of v3, /device:TPU:9, one launch (start us, length us, event | category | flops | bytes accessed | tf_op | source)
XLA Modules:
  0.0 1365.3 jit_solution(7709031015063045829)
XLA Ops:
  7.3 1.0 copy.190
  8.2 0.8 copy.191
  9.1 0.7 maximum_maximum_fusion.small
  9.9 91.1 %shard_map.170 = (bf16[4,8,192,640]{3,2,1,0:T(8,128)(2,1)}, bf16[4,8,192,384]{3,2,1,0:T(8,128)(2,1)}, bf16[8,192,128]{2,1,0:T(8,128)(2,1)}) custom-call(bf16[192,2560]{1,0:T(8,128)(2,1)} %qkv.1, bf16[192,1536]{1,0:T(8,128)(2,1)} %out.1, bf16[192,128]{1,0:T(8,128)(2,1)} %maximum_maximum_fusion.small), custom_call_target="tpu_custom_call" | custom-call | tf_op jit(solution)/shard_map/pallas_call | solution.py:349
  100.9 1.2 slice.52
  102.3 2.0 fusion.12
  104.3 0.6 multiply_multiply_fusion.1
  105.0 10.6 copy.193
  115.6 8.3 convolution_convert_fusion.3
  123.9 1.4 slice.54.q_ref
  125.3 1.2 slice.55
  126.7 0.7 fusion.42
  130.3 0.3 select_reduce_fusion.3
  131.7 2.7 constant_dynamic-slice_fusion.1.gu_ref
  134.4 0.9 constant_dynamic-slice_fusion.dn_ref
  135.3 6.8 copy.194
  142.2 1.1 copy-done.4
  143.3 267.6 %shard_map.171 = (bf16[640,1536]{1,0:T(8,128)(2,1)S(1)}, f32[20,8,768]{2,1,0:T(8,128)S(1)}, bf16[20,128,1024]{2,1,0:T(8,128)(2,1)}, bf16[4,8,192,1024]{3,2,1,0:T(8,128)(2,1)}, bf16[4,8,64,1536]{3,2,1,0:T(8,128)(2,1)}) custom-call(s32[5,10]{1,0:T(8,128)S(1)} %stack.73.slots, f32[5,10]{1,0:T(8,128)S(1)} %broadcast_select_fusion.bias, ...), custom_call_target="tpu_custom_call" | custom-call | tf_op jit(solution)/shard_map/pallas_call | solution.py:424
  410.9 8.4 multiply_reduce_fusion.2
  419.4 0.6 multiply_multiply_fusion.2
  420.0 3.8 multiply_convert_fusion.5
  423.9 0.7 all-gather.6.cloned.1.call-update
  424.6 0.7 copy-done.12
  425.3 0.6 fusion.29
  426.2 0.6 copy-done.26
  426.8 7.0 all_gather.13
  433.8 48.1 %all-gather.4.cloned.1.call-done = bf16[2560,1536]{1,0:T(8,128)(2,1)} async-done(((bf16[640,1536]{1,0:T(8,128)(2,1)}), bf16[2560,1536]{1,0:T(8,128)(2,1)}) %all-gather.4.cloned.1.call-update) | async-done | bytes 7864336 | tf_op jit(solution)/shard_map/all_gather | solution.py:971
  481.8 41.5 %convolution_bitcast_fusion = f32[4,2560,1024]{1,2,0:T(8,128)} fusion(bf16[4,1536,1024]{2,1,0:T(8,128)(2,1)} %bitcast.179, bf16[2560,1536]{1,0:T(8,128)(2,1)} %all-gather.4.cloned.1.call-done), kind=kOutput, calls=%fused_computation | convolution fusion | flops 32212254720 | bytes 62390272 | tf_op jit(solution)/shard_map/td,edf->etf/dot_general | solution.py:974
  523.4 15.4 %all-gather.6.cloned.1.call-done = bf16[2560,1536]{1,0:T(8,128)(2,1)} async-done(((bf16[640,1536]{1,0:T(8,128)(2,1)}), bf16[2560,1536]{1,0:T(8,128)(2,1)}) %all-gather.6.cloned.1.call-update) | async-done | bytes 7864336 | tf_op jit(solution)/shard_map/all_gather | solution.py:944
  538.7 41.2 %multiply_convert_fusion.1 = (bf16[4,2560,512]{1,2,0:T(8,128)(2,1)}, bf16[4,2560,512]{1,2,0:T(8,128)(2,1)}, f32[4,2560]{1,0:T(4,128)S(1)}, f32[4,2560,512]{1,2,0:T(8,128)}) fusion(f32[4,2560,1024]{1,2,0:T(8,128)} %convolution_bitcast_fusion, f32[4,2560]{1,0:T(4,128)S(1)} %dynamic-slice_bitcast_fusion, bf16[4,512,1536]{2,1,0:T(8,128)(2,1)} %bitcast.181, ...), kind=kOutput, calls=%fused_computation.6 | convolution fusion | flops 16200488960 | bytes 98123776 | tf_op jit(solution)/shard_map/td,efd->etf/dot_general | solution.py:983
  579.9 41.2 %bitcast_convert_fusion = bf16[2560,1536]{1,0:T(8,128)(2,1)} fusion(bf16[4,1536,1024]{2,1,0:T(8,128)(2,1)} %bitcast.180, bf16[4,2560,512]{1,2,0:T(8,128)(2,1)} %get-tuple-element.106, bf16[4,2560,512]{1,2,0:T(8,128)(2,1)} %get-tuple-element.105), kind=kOutput, calls=%fused_computation.10 | convolution fusion | flops 32258129920 | bytes 41418752 | tf_op jit(solution)/shard_map/etf,edf->td/dot_general | solution.py:1007
  621.2 25.2 %bitcast_convert_fusion.1 = bf16[2560,1536]{1,0:T(8,128)(2,1)} fusion(bf16[4,512,1536]{2,1,0:T(8,128)(2,1)} %bitcast.182, f32[4,2560,512]{1,2,0:T(8,128)} %get-tuple-element.108, f32[4,2560]{1,0:T(4,128)S(1)} %dynamic-slice_bitcast_fusion), kind=kOutput, calls=%fused_computation.11 | convolution fusion | flops 16120545280 | bytes 35168256 | tf_op jit(solution)/shard_map/etf,efd->td/dot_general | solution.py:980
  646.4 0.6 copy-done.40
  647.3 0.6 broadcast_subtract_fusion.inv
  647.9 6.6 all-gather
  654.6 0.9 convolution_convert_fusion.4
  655.5 0.9 copy.206
  656.4 40.1 %fusion.2 = bf16[4,1536,1024]{1,2,0:T(8,128)(2,1)} fusion(bf16[4,2560,512]{1,2,0:T(8,128)(2,1)} %get-tuple-element.106, bf16[4,2560,512]{1,2,0:T(8,128)(2,1)} %get-tuple-element.105, bf16[2560,1536]{1,0:T(8,128)(2,1)} %all-gather.4.cloned.1.call-done), kind=kOutput, calls=%fused_computation.16 | convolution fusion | flops 32260489216 | bytes 41418752 | tf_op jit(solution)/shard_map/td,etf->edf/dot_general | solution.py:1004
  696.6 16.9 %copy.201 = bf16[4,1536,1024]{2,1,0:T(8,128)(2,1)} copy(bf16[4,1536,1024]{1,2,0:T(8,128)(2,1)} %fusion.2) | data formatting | bytes 25165824 | tf_op jit(solution)/shard_map/convert_element_type | solution.py:1040
  713.4 25.2 %fusion.9 = bf16[4,512,1536]{2,1,0:T(8,128)(2,1)} fusion(bf16[2560,1536]{1,0:T(8,128)(2,1)} %all-gather.6.cloned.1.call-done, f32[4,2560,512]{1,2,0:T(8,128)} %get-tuple-element.108, f32[4,2560]{1,0:T(4,128)S(1)} %dynamic-slice_bitcast_fusion), kind=kOutput, calls=%fused_computation.31 | convolution fusion | flops 16119758848 | bytes 35168256 | tf_op jit(solution)/shard_map/etf,td->efd/dot_general | solution.py:1003
  738.7 7.6 multiply_reduce_fusion
  746.3 16.0 %reduce-scatter.3.cloned.1.call-done = bf16[640,1536]{1,0:T(8,128)(2,1)} async-done(((bf16[2560,1536]{1,0:T(8,128)(2,1)}), bf16[640,1536]{1,0:T(8,128)(2,1)}) %reduce-scatter.3.cloned.1.call-update) | async-done | bytes 1966096 | tf_op jit(solution)/shard_map/reduce_scatter | solution.py:981
  762.3 6.1 fusion.50
  768.5 7.5 bitcast_convert_fusion.3.do_ref
  775.9 325.1 %shard_map.172 = (bf16[640,1536]{1,0:T(8,128)(2,1)}, bf16[5,128,1024]{2,1,0:T(8,128)(2,1)}, bf16[4,192,1024]{2,1,0:T(8,128)(2,1)}, bf16[4,64,1536]{2,1,0:T(8,128...) custom-call(s32[5,10]{1,0:T(8,128)} %copy-done.10, ...), custom_call_target="tpu_custom_call" | custom-call | tf_op jit(solution)/shard_map/pallas_call | solution.py:702
  1101.1 10.8 convolution_convert_fusion.1
  1112.2 1.3 copy-done.6
  1113.5 5.5 convolution_convert_fusion.2
  1119.0 7.4 fusion.20
  1126.3 0.3 broadcast_in_dim.276
  1126.6 0.3 broadcast_in_dim.277
  1127.0 19.7 %concatenate.17 = bf16[1536,4352]{1,0:T(8,128)(2,1)} concatenate(bf16[1536,2560]{1,0:T(8,128)(2,1)} %convolution_convert_fusion.1, bf16[1536,1536]{1,0:T(8,128)(2,1)} %convolution_convert_fusion.2, bf16[1536,1]{1,0:T(8,128)(2,1)S(1)} %broadcast_in_dim.276, bf16[1536,1]{1,0:T(8,128)(2,1)S(1)} %broadcast_in_dim.277, bf16[1536,16]{1,0:T(8,128)(2,1)S(1)} %copy-done.24, ...), dimensions={1} | concatenate | bytes 26738688 | tf_op jit(solution)/shard_map/concatenate | solution.py:1061
  1146.6 18.7 %convert_element_type.103 = bf16[8,1,192,2,2176]{4,3,2,0,1:T(2,128)(2,1)} reshape(bf16[1536,4352]{1,0:T(8,128)(2,1)} %concatenate.17) | data formatting | bytes 26738688 | tf_op jit(solution)/shard_map/convert_element_type | solution.py:1071
  1165.3 12.5 copy.230
  1177.9 157.1 %shard_map.173 = (bf16[2,1,192,2176]{3,2,1,0:T(8,128)(2,1)S(1)}, bf16[4,4,192,1024]{3,2,1,0:T(8,128)(2,1)}, bf16[4,4,64,1536]{3,2,1,0:T(8,128)(2,1)S(1)}, bf16[8...) custom-call(bf16[2,8,1,192,2176]{4,3,2,1,0:T(8,128)(2,1)} %bitcast.1, ...), custom_call_target="tpu_custom_call" | custom-call | tf_op jit(solution)/shard_map/pallas_call | solution.py:830
  1335.3 2.6 copy.208
  1338.1 1.5 slice.61
  1339.6 1.1 slice.62
  1340.8 6.8 bitcast_convert_fusion.2
  1347.6 0.7 copy.210
  1348.3 0.7 copy.209
  1348.9 4.0 bitcast_convert_fusion.4
  1352.9 0.4 copy-done.17
  1353.3 5.2 fusion.17
  (164 shorter events, 6.1 us)
Async XLA Ops:
  7.2 127.2 %copy-start = (bf16[16,64,1536]{2,1,0:T(8,128)(2,1)S(1)}, bf16[16,64,1536]{2,1,0:T(8,128)(2,1)}, u32[]{:S(2)}) copy-start(bf16[16,64,1536]{2,1,0:T(8,128)(2,1)} %param.17) | copy-start | bytes 9437188
  7.2 474.7 %all-gather.4.cloned.1.call-start = ((), (), s32[]{:S(2)}) async-start(), calls=%async_computation.2 | async-start | bytes 9830400 | tf_op jit(solution)/shard_map/all_gather | solution.py:971
  102.3 13.2 copy-start.33
  102.3 317.6 %copy-start.28 = (f32[1536]{0:T(1024)}, f32[1536]{0:T(1024)S(1)}, u32[]{:S(2)}) copy-start(f32[1536]{0:T(1024)S(1)} %get-tuple-element.82) | copy-start | bytes 18436
  105.0 10.6 copy-start.36
  123.9 2.6 copy-start.41
  130.2 0.6 copy-start.39
  130.2 11.9 copy-start.11
  135.3 6.9 copy-start.2
  135.3 6.9 copy-start.3
  142.2 504.3 %copy-start.10 = (s32[5,10]{1,0:T(8,128)}, s32[5,10]{1,0:T(8,128)S(1)}, u32[]{:S(2)}) copy-start(s32[5,10]{1,0:T(8,128)S(1)} %stack.73.slots) | copy-start | bytes 604
  142.2 1.1 copy-start.4
  143.3 267.6 %copy-start.15 = (bf16[640,1536]{1,0:T(8,128)(2,1)S(1)}, bf16[640,1536]{1,0:T(8,128)(2,1)}, u32[]{:S(2)}) copy-start(bf16[640,1536]{1,0:T(8,128)(2,1)} %param.11) | copy-start | bytes 5898244
  410.9 8.4 copy-start.5
  410.9 8.4 copy-start.9
  420.0 3.9 copy-start.31
  420.0 4.7 copy-start.19
  423.8 1.5 copy-start.12
  423.8 2.2 copy-start.30
  423.8 114.9 %all-gather.6.cloned.1.call-start = ((), (), s32[]{:S(2)}) async-start(), calls=%async_computation.4 | async-start | bytes 9830400 | tf_op jit(solution)/shard_map/all_gather | solution.py:944
  424.6 314.0 %reduce-scatter.5.cloned.1.call-start = ((), (), s32[]{:S(2)}) async-start(), calls=%async_computation.5 | async-start | bytes 9830400 | tf_op jit(solution)/shard_map/reduce_scatter | solution.py:1010
  426.2 0.6 copy-start.26
  621.1 141.2 %reduce-scatter.3.cloned.1.call-start = ((), (), s32[]{:S(2)}) async-start(), calls=%async_computation.3 | async-start | bytes 9830400 | tf_op jit(solution)/shard_map/reduce_scatter | solution.py:981
  646.4 0.7 copy-start.40
  646.4 8.2 copy-start.27
  646.4 8.2 copy-start.13
  713.4 25.2 %copy-start.20 = (bf16[8,192,128]{2,1,0:T(8,128)(2,1)S(1)}, bf16[8,192,128]{2,1,0:T(8,128)(2,1)}, u32[]{:S(2)}) copy-start(bf16[8,192,128]{2,1,0:T(8,128)(2,1)} %get-tuple-element.23) | copy-start | bytes 1179652
  713.4 25.2 %copy-start.29 = (f32[1536]{0:T(1024)S(1)}, f32[1536]{0:T(1024)}, u32[]{:S(2)}) copy-start(f32[1536]{0:T(1024)} %copy-done.28) | copy-start | bytes 18436
  713.4 25.2 %copy-start.32 = (f32[640]{0:T(1024)S(1)}, f32[640]{0:T(1024)}, u32[]{:S(2)}) copy-start(f32[640]{0:T(1024)} %copy-done.31) | copy-start | bytes 7684
  738.6 23.7 %copy-start.18 = (bf16[640,1536]{1,0:T(8,128)(2,1)S(1)}, bf16[640,1536]{1,0:T(8,128)(2,1)}, u32[]{:S(2)}) copy-start(bf16[640,1536]{1,0:T(8,128)(2,1)} %param.21) | copy-start | bytes 5898244
  738.6 23.7 %copy-start.38 = (f32[640]{0:T(1024)S(1)}, f32[640]{0:T(1024)}, u32[]{:S(2)}) copy-start(f32[640]{0:T(1024)} %get-tuple-element.112) | copy-start | bytes 7684
  768.5 7.5 copy-start.21
  775.9 325.1 %copy-start.16 = (bf16[640,1536]{1,0:T(8,128)(2,1)S(1)}, bf16[640,1536]{1,0:T(8,128)(2,1)}, u32[]{:S(2)}) copy-start(bf16[640,1536]{1,0:T(8,128)(2,1)} %param.11) | copy-start | bytes 5898244
  775.9 325.1 %copy-start.34 = (f32[1536]{0:T(1024)S(1)}, f32[1536]{0:T(1024)}, u32[]{:S(2)}) copy-start(f32[1536]{0:T(1024)} %copy-done.33) | copy-start | bytes 18436
  775.9 325.1 %copy-start.37 = (f32[640]{0:T(1024)S(1)}, f32[640]{0:T(1024)}, u32[]{:S(2)}) copy-start(f32[640]{0:T(1024)} %copy-done.36) | copy-start | bytes 7684
  1101.1 10.8 copy-start.23
  1101.1 10.8 copy-start.25
  1101.1 11.1 copy-start.22
  1111.9 1.5 copy-start.6
  1111.9 7.1 slice-start
  1113.5 5.5 slice-start.1
  1119.0 8.0 copy-start.24
  1165.3 12.6 copy-start.7
  1165.3 12.6 copy-start.8
  1335.3 5.6 slice-start.2
  1337.9 3.0 slice-start.3
  1348.9 4.0 copy-start.14
  1348.9 4.4 copy-start.17
  1348.9 4.4 copy-start.35
  1352.9 5.6 copy-start.1
Sparse Core Ops, SparseCore 0:
  423.9 57.8 all-gather.3
  483.4 55.3 all-gather.5
  621.2 69.4 reduce-scatter.4
  693.3 68.9 reduce-scatter.2

commit v4 on v3

--- a/solution.py
+++ b/solution.py
@@ -120,6 +120,10 @@
 SMEM = pl.BlockSpec(memory_space=pltpu.SMEM)
 
 
+def work(flops, moved):
+    return pl.CostEstimate(flops=int(flops), bytes_accessed=int(moved), transcendentals=0)
+
+
 class Sends:
     def __init__(self):
         self.open = []
@@ -311,21 +315,29 @@
     return [pltpu.SemaphoreType.DMA((2, shards, arrays)) for unused in range(3)]
 
 
-def weights_kernel(shards, qkv, out, small, qkv_all, out_all, small_all, up, down, pair, local_sem, cross, core, relay):
+def part_columns(ref, part, width):
+    return ref.at[:, pl.ds(pl.multiple_of(part * width, LANES), width)]
+
+
+def weights_kernel(shards, qkv, small, qkv_all, small_all, up, down, pair, local_sem, cross, core, relay):
     rep = lax.axis_index("rep")
     greet(line_neighbours(shards) + rep_neighbours())
-    refs = (qkv_all, out_all, small_all)
+    width = qkv.shape[1] // lax.axis_size("rep")
 
     def part(n, owner, block):
-        return refs[n].at[block] if n == 2 else refs[n].at[owner, block]
-
-    def columns(ref, width):
-        return ref.at[:, pl.ds(pl.multiple_of(rep * width, LANES), width)]
-
-    spread = RepSpread((0, 1), part, cross, core, relay)
-    sources = (columns(qkv, qkv_all.shape[-1]), columns(out, out_all.shape[-1]), small)
+        return small_all.at[block] if n == 1 else part_columns(qkv_all.at[block], owner, width)
+
+    spread = RepSpread((0,), part, cross, core, relay)
+    spread.sources = None
     gather = LineGather(
-        shards, sources, lambda n, block: part(n, rep, block), up, down, pair, local_sem, spread.arrived
+        shards,
+        (part_columns(qkv, rep, width), small),
+        lambda n, block: part(n, rep, block),
+        up,
+        down,
+        pair,
+        local_sem,
+        spread.arrived,
     )
     gather.begin()
     gather.finish_local()
@@ -339,65 +351,94 @@
     gather.sends.drain()
 
 
-def gather_weights(qkv_weight, out_weight, small, shards, reps):
-    rows = qkv_weight.shape[0]
-    shapes = [
-        (reps, shards, rows, qkv_weight.shape[1] // reps),
-        (reps, shards, rows, out_weight.shape[1] // reps),
-        (shards,) + small.shape,
-    ]
+def gather_weights(qkv_weight, small, shards):
+    shapes = [(shards,) + qkv_weight.shape, (shards,) + small.shape]
     return pl.pallas_call(
         functools.partial(weights_kernel, shards),
         out_shape=[jax.ShapeDtypeStruct(shape, jnp.bfloat16) for shape in shapes],
-        in_specs=[ANY] * 3,
-        out_specs=[ANY] * 3,
-        scratch_shapes=line_sems(shards, 3) + rep_sems(shards, 2),
+        in_specs=[ANY] * 2,
+        out_specs=[ANY] * 2,
+        scratch_shapes=line_sems(shards, 2) + rep_sems(shards, 1),
+        cost_estimate=work(0, 2e8),
         compiler_params=pltpu.CompilerParams(collective_id=1, has_side_effects=True),
-    )(qkv_weight, out_weight, small)
+    )(qkv_weight, small)
 
 
 def attend_gather_kernel(
     depth,
     shards,
+    experts,
     slots,
     bias,
     q_ref,
     kv_ref,
     gu_ref,
     dn_ref,
+    out_ref,
+    cot_ref,
     o_ref,
     lse_ref,
     kv_all,
     gu_all,
     dn_all,
+    out_all,
+    cot_all,
     s_scr,
     p_scr,
     kv_sems,
+    cot_sem,
     up,
     down,
     pair,
     local_sem,
+    cross,
+    core,
+    relay,
+    cot_cross,
+    cot_core,
+    cot_relay,
 ):
     me = lax.axis_index("shard")
+    rep = lax.axis_index("rep")
     first = me // TREE_DEVS * TREE_DEVS
     member = me % TREE_DEVS
     seg_dev = kv_ref.shape[0]
     others = [first + lax.rem(member + away, TREE_DEVS) for away in range(1, TREE_DEVS)]
-    greet(line_neighbours(shards) + [(None, {"shard": other}) for other in others])
+    greet(line_neighbours(shards) + rep_neighbours() + [(None, {"shard": other}) for other in others])
     sends = Sends()
     own = kv_all.at[pl.ds(member * seg_dev, seg_dev)]
     for away, other in enumerate(others):
         sends.start(None, kv_ref, own, kv_sems.at[0, away], kv_sems.at[1, away], {"shard": other})
+    width = out_ref.shape[1] // lax.axis_size("rep")
+    own_experts = gu_ref.shape[0] // lax.axis_size("rep")
+
+    def part(n, owner, block):
+        if n == 2:
+            return part_columns(out_all.at[block], owner, width)
+        return (gu_all, dn_all)[n].at[:, block]
+
+    spread = RepSpread((2,), part, cross, core, relay)
     gather = LineGather(
         shards,
-        (gu_ref, dn_ref),
-        lambda n, block: (gu_all, dn_all)[n].at[:, block],
+        (
+            gu_ref.at[pl.ds(rep * own_experts, experts)],
+            dn_ref.at[pl.ds(rep * own_experts, experts)],
+            part_columns(out_ref, rep, width),
+        ),
+        lambda n, block: part(n, rep, block),
         up,
         down,
         pair,
         local_sem,
+        spread.arrived,
     )
     gather.begin()
+    sends.local(cot_ref, cot_all.at[rep], cot_sem)
+    cot_spread = RepSpread((0,), lambda n, owner, block: cot_all.at[owner], cot_cross, cot_core, cot_relay)
+    cot_spread.sources = (cot_ref,)
+    cot_spread.arrived(None, 0, 0)
+    gather.finish_local()
+    spread.arrived(None, me, 0)
     kv_all[pl.ds(member * seg_dev, seg_dev)] = kv_ref[...]
     for away in range(TREE_DEVS - 1):
         source = lax.rem(member + TREE_DEVS - 1 - away, TREE_DEVS)
@@ -411,37 +452,155 @@
         lax.fori_loop(done, upto, attend, 0)
         done = upto
         gather.step(step)
-    for step in range(gather.length):
-        gather.pair_step(step)
+        gather.pair_step(step - 1)
+        spread.pass_on()
+    cot_spread.end()
+    gather.pair_step(gather.length - 1)
+    spread.end()
     gather.sends.drain()
     sends.drain()
 
 
-def attend_gather(slots, bias, q, kv, gate_up, down, depth, shards):
+def attend_gather(slots, bias, q, kv, gate_up, down, out, cotangent, depth, shards, reps, experts):
     tokens = q.shape[0]
     count = tokens // SEG * PAIRS
-    experts, rows = gate_up.shape[:2]
+    shapes = [
+        q.shape,
+        (TREE_DEVS * kv.shape[0],) + kv.shape[1:],
+        (experts, shards) + gate_up.shape[1:],
+        (experts, shards) + down.shape[1:],
+        (shards,) + out.shape,
+        (reps,) + cotangent.shape,
+    ]
+    outs = [jax.ShapeDtypeStruct(shape, jnp.bfloat16) for shape in shapes]
     return pl.pallas_call(
-        functools.partial(attend_gather_kernel, depth, shards),
-        out_shape=(
-            jax.ShapeDtypeStruct(q.shape, jnp.bfloat16),
-            jax.ShapeDtypeStruct((count, 8, 6 * SEG), jnp.float32),
-            jax.ShapeDtypeStruct((TREE_DEVS * kv.shape[0],) + kv.shape[1:], jnp.bfloat16),
-            jax.ShapeDtypeStruct((experts, shards, rows) + gate_up.shape[2:], jnp.bfloat16),
-            jax.ShapeDtypeStruct((experts, shards) + down.shape[1:], jnp.bfloat16),
-        ),
-        in_specs=[SMEM, SMEM, VMEM, VMEM, ANY, ANY],
-        out_specs=(VMEM, VMEM, VMEM, ANY, ANY),
+        functools.partial(attend_gather_kernel, depth, shards, experts),
+        out_shape=outs[:1] + [jax.ShapeDtypeStruct((count, 8, 6 * SEG), jnp.float32)] + outs[1:],
+        in_specs=[SMEM, SMEM, VMEM, VMEM] + [ANY] * 4,
+        out_specs=[VMEM] * 3 + [ANY] * 4,
         scratch_shapes=[
             pltpu.VMEM((depth * SEG, 6 * SEG), jnp.float32),
             pltpu.VMEM((depth * SEG, 6 * SEG), jnp.bfloat16),
             pltpu.SemaphoreType.DMA((2, TREE_DEVS - 1)),
+            pltpu.SemaphoreType.DMA,
         ]
-        + line_sems(shards, 2),
+        + line_sems(shards, 3)
+        + rep_sems(shards, 3)
+        + rep_sems(1, 1),
+        cost_estimate=work(2e10, 7e8),
         compiler_params=pltpu.CompilerParams(
             collective_id=2, has_side_effects=True, vmem_limit_bytes=48 * 2**20
         ),
-    )(slots, bias, q, kv, gate_up, down)
+    )(slots, bias, q, kv, gate_up, down, out, cotangent)
+
+
+def share_kernel(chunks, rows_ref, gate_ref, rows_all, gate_all, own_sems, cross, core, relay):
+    rep = lax.axis_index("rep")
+    greet(rep_neighbours())
+    size = rows_ref.shape[0] // chunks
+
+    def piece(n, part, block):
+        return gate_all.at[part] if n == chunks else rows_all.at[part, pl.ds(n * size, size)]
+
+    spread = RepSpread(tuple(range(chunks + 1)), piece, cross, core, relay)
+    spread.sources = [rows_ref.at[pl.ds(n * size, size)] for n in range(chunks)] + [gate_ref]
+    spread.arrived(None, 0, 0)
+    for n in range(chunks + 1):
+        spread.sends.local(spread.sources[n], piece(n, rep, 0), own_sems.at[n])
+    spread.end()
+
+
+def share_rows(rows, gates, reps):
+    chunks = 4
+    return pl.pallas_call(
+        functools.partial(share_kernel, chunks),
+        out_shape=[
+            jax.ShapeDtypeStruct((reps,) + rows.shape, rows.dtype),
+            jax.ShapeDtypeStruct((reps,) + gates.shape, gates.dtype),
+        ],
+        in_specs=[ANY] * 2,
+        out_specs=[ANY] * 2,
+        scratch_shapes=[pltpu.SemaphoreType.DMA((chunks + 1,))] + rep_sems(1, chunks + 1),
+        cost_estimate=work(0, 1.6e8),
+        compiler_params=pltpu.CompilerParams(collective_id=6, has_side_effects=True),
+    )(rows, gates)
+
+
+def join_kernel(part, total, near_buf, cross_out, cross_buf, near_sems, cross_sems):
+    rep = lax.axis_index("rep")
+    near = rep + 1 - 2 * (rep % 2)
+    far = lax.rem(rep + 2, 4)
+    diagonal = lax.rem(near + 2, 4)
+    greet(rep_neighbours())
+    sends = Sends()
+    chunks = near_sems.shape[2]
+    size = total.shape[0] // chunks
+    for slot, owner in ((1, diagonal), (0, near)):
+        for c in range(chunks):
+            rows = pl.ds(c * size, size)
+            sends.start(
+                None,
+                part.at[owner, rows],
+                near_buf.at[slot, rows],
+                near_sems.at[0, slot, c],
+                near_sems.at[1, slot, c],
+                {"rep": near},
+            )
+
+    def got(slot, c):
+        here = near_buf.at[slot, pl.ds(c * size, size)]
+        received(None, here, near_sems.at[0, slot, c], near_sems.at[1, slot, c], {"rep": near})
+
+    step = 32 if size % 32 == 0 else size
+    for c in range(chunks):
+        got(1, c)
+
+        def first(i, carry, c=c):
+            rows = pl.ds(pl.multiple_of(c * size + i * step, step), step)
+            value = part[far, rows].astype(jnp.float32) + near_buf[1, rows].astype(jnp.float32)
+            cross_out[rows] = value.astype(cross_out.dtype)
+            return carry
+
+        lax.fori_loop(0, size // step, first, 0)
+        rows = pl.ds(c * size, size)
+        sends.start(
+            None, cross_out.at[rows], cross_buf.at[rows], cross_sems.at[0, c], cross_sems.at[1, c], {"rep": far}
+        )
+    for c in range(chunks):
+        got(0, c)
+        here = cross_buf.at[pl.ds(c * size, size)]
+        received(None, here, cross_sems.at[0, c], cross_sems.at[1, c], {"rep": far})
+
+        def second(i, carry, c=c):
+            rows = pl.ds(pl.multiple_of(c * size + i * step, step), step)
+            value = part[rep, rows].astype(jnp.float32) + near_buf[0, rows].astype(jnp.float32)
+            total[rows] = value + cross_buf[rows].astype(jnp.float32)
+            return carry
+
+        lax.fori_loop(0, size // step, second, 0)
+    sends.drain()
+
+
+def join_reps(part):
+    block = part.shape[1:]
+    chunks = 4
+    return pl.pallas_call(
+        join_kernel,
+        out_shape=jax.ShapeDtypeStruct(block, jnp.float32),
+        in_specs=[VMEM],
+        out_specs=VMEM,
+        scratch_shapes=[
+            pltpu.VMEM((2,) + block, jnp.bfloat16),
+            pltpu.VMEM(block, jnp.bfloat16),
+            pltpu.VMEM(block, jnp.bfloat16),
+            pltpu.SemaphoreType.DMA((2, 2, chunks)),
+            pltpu.SemaphoreType.DMA((2, chunks)),
+        ],
+        cost_estimate=work(0, 1.6e8),
+        compiler_params=pltpu.CompilerParams(
+            collective_id=5, has_side_effects=True, vmem_limit_bytes=40 * 2**20
+        ),
+    )(part)
 
 
 class LineScatter:
@@ -654,7 +813,10 @@
     step = functools.partial(
         bwd_step, depth, slots, bias, q_ref, kv_ref, o_ref, do_ref, lse_ref, dq_ref, path, p_scr, d_scr
     )
-    lax.fori_loop(0, segs * PAIRS, step, 0)
+    early = segs * PAIRS * 3 // 5
+    lax.fori_loop(0, early, step, 0)
+    scatter.step(0)
+    lax.fori_loop(early, segs * PAIRS, step, 0)
     lax.fori_loop(0, group.shape[0], functools.partial(bwd_collect, inv, path, group), 0)
     sends = Sends()
     for away, other in enumerate(others):
@@ -667,7 +829,7 @@
             kv_sems.at[1, away],
             {"shard": other},
         )
-    for turn in range(scatter.length):
+    for turn in range(1, scatter.length):
         scatter.step(turn)
     for away in range(TREE_DEVS - 1):
         source = first + lax.rem(member + TREE_DEVS - 1 - away, TREE_DEVS)
@@ -717,38 +879,34 @@
             pltpu.SemaphoreType.DMA((2, TREE_DEVS - 1)),
         ]
         + scatter_sems(shards, 2, 4),
+        cost_estimate=work(5e10, 7e8),
         compiler_params=pltpu.CompilerParams(
             collective_id=3, has_side_effects=True, vmem_limit_bytes=60 * 2**20
         ),
     )(slots, bias, inv, q, kv, o, do, lse, gate_up_grad, down_grad)[:4]
 
 
-def finish_kernel(
-    shards,
-    grad_ref,
-    gu_ref,
-    dn_ref,
-    grad_out,
-    gu_out,
-    dn_out,
-    core_buf,
-    share_buf,
-    cross_buf,
-    pair_buf,
-    line_buf,
-    temp_buf,
-    stage,
-    total,
-    core_sems,
-    swap_sems,
-    own_sems,
-    cross,
-    core,
-    relay,
-    pair,
-    line,
-    loads,
-):
+def finish_kernel(shards, arrays, pieces, *refs):
+    refs = list(refs)
+
+    def take(count):
+        taken = refs[:count]
+        del refs[:count]
+        return taken
+
+    grads = take(arrays)
+    shares = take(pieces)
+    outs = take(arrays)
+    expert_outs = take(2)
+    core_bufs = take(arrays)
+    share_bufs = take(arrays)
+    cross_bufs = take(arrays)
+    temps = take(arrays)
+    pair_bufs = take(arrays)
+    line_bufs = take(arrays)
+    stages = take(arrays)
+    totals = take(arrays)
+    core_sems, swap_sems, own_sems, cross, core, relay, pair, line, loads = refs
     rep = lax.axis_index("rep")
     near = rep + 1 - 2 * (rep % 2)
     far = lax.rem(rep + 2, 4)
@@ -762,36 +920,52 @@
             if target not in order:
                 order.append(target)
     side = lax.axis_index("shard") % 2
+
+    def columns(n, ref, which):
+        width = totals[n].shape[-1]
+        if width == ref.shape[-1]:
+            return ref
+        return ref.at[:, :, pl.ds(pl.multiple_of(which * width, LANES), width)]
+
     for turn in (1 - side, side):
         for target in order:
             block = 2 * target + turn
-            sends.start(
-                None,
-                grad_ref.at[1 - half, block],
-                core_buf.at[block],
-                core_sems.at[0, block],
-                core_sems.at[1, block],
-                {"rep": near},
+            for n in range(arrays):
+                sends.start(
+                    None,
+                    columns(n, grads[n].at[block], 1 - half),
+                    core_bufs[n].at[block],
+                    core_sems.at[0, block, n],
+                    core_sems.at[1, block, n],
+                    {"rep": near},
+                )
+    experts = pieces // 2
+    size = shares[0].shape[0]
+
+    def place(n, part, block):
+        return expert_outs[n // experts].at[part, pl.ds(n % experts * size, size)]
+
+    for n in range(pieces):
+        sends.local(shares[n], place(n, rep, 0), own_sems.at[n])
+    spread = RepSpread(tuple(range(pieces)), place, cross, core, relay)
+    spread.sources = shares
+    spread.arrived(None, 0, 0)
+
+    def ready(block):
+        for n in range(arrays):
+            received(
+                None, core_bufs[n].at[block], core_sems.at[0, block, n], core_sems.at[1, block, n], {"rep": near}
             )
-    experts = (gu_out, dn_out)
-    for n, src in enumerate((gu_ref, dn_ref)):
-        sends.local(src, experts[n].at[rep], own_sems.at[n])
-    spread = RepSpread((0, 1), lambda n, part, block: experts[n].at[part], cross, core, relay)
-    spread.sources = (gu_ref, dn_ref)
-    spread.arrived(None, 0, 0)
-
-    def ready(block):
-        received(None, core_buf.at[block], core_sems.at[0, block], core_sems.at[1, block], {"rep": near})
 
     scatter = LineScatter(
         shards,
-        1,
-        lambda n, block: [grad_ref.at[half, block], core_buf.at[block]],
-        (pair_buf,),
-        (line_buf,),
-        (temp_buf,),
-        (stage,),
-        (total,),
+        arrays,
+        lambda n, block: [columns(n, grads[n].at[block], half), core_bufs[n].at[block]],
+        pair_bufs,
+        line_bufs,
+        temps,
+        stages,
+        totals,
         pair,
         line,
         loads,
@@ -800,51 +974,61 @@
     scatter.begin()
     for turn in range(scatter.length):
         scatter.step(turn)
-    scatter.finish((share_buf,))
-    sends.start(None, share_buf, cross_buf, swap_sems.at[0, 0], swap_sems.at[1, 0], {"rep": far})
+    scatter.finish(share_bufs)
+    for n in range(arrays):
+        sends.start(
+            None, share_bufs[n], cross_bufs[n], swap_sems.at[0, 0, n], swap_sems.at[1, 0, n], {"rep": far}
+        )
     spread.end()
-    received(None, cross_buf, swap_sems.at[0, 0], swap_sems.at[1, 0], {"rep": far})
-    scatter.add(0, [(None, share_buf), (None, cross_buf)], grad_out.at[half])
-    sends.start(None, grad_out.at[half], grad_out.at[half], swap_sems.at[0, 1], swap_sems.at[1, 1], {"rep": near})
-    received(None, grad_out.at[1 - half], swap_sems.at[0, 1], swap_sems.at[1, 1], {"rep": near})
+    for n in range(arrays):
+        received(None, cross_bufs[n], swap_sems.at[0, 0, n], swap_sems.at[1, 0, n], {"rep": far})
+        mine = columns(n, outs[n], half)
+        scatter.add(n, [(None, share_bufs[n]), (None, cross_bufs[n])], mine)
+        if outs[n].shape != totals[n].shape:
+            sends.start(None, mine, mine, swap_sems.at[0, 1, n], swap_sems.at[1, 1, n], {"rep": near})
+    for n in range(arrays):
+        if outs[n].shape != totals[n].shape:
+            theirs = columns(n, outs[n], 1 - half)
+            received(None, theirs, swap_sems.at[0, 1, n], swap_sems.at[1, 1, n], {"rep": near})
     sends.drain()
     scatter.sends.drain()
 
 
-def finish_grads(grad, gate_up_share, down_share, reps):
-    halves, shards = grad.shape[:2]
-    block = grad.shape[2:]
-
-    def shape(*dims):
-        return jax.ShapeDtypeStruct(dims, jnp.bfloat16)
-
-    outs = [
-        shape(halves, *block),
-        shape(reps, *gate_up_share.shape),
-        shape(reps, *down_share.shape),
-        shape(shards, *block),
-        shape(*block),
-        shape(*block),
+def finish_grads(grads, halved, gate_up_shares, down_shares, reps):
+    shards = grads[0].shape[0]
+    arrays = len(grads)
+    parts = len(gate_up_shares)
+    wholes = [grad.shape[1:] for grad in grads]
+    blocks = [
+        whole[:-1] + (whole[-1] // 2 if halve else whole[-1],) for whole, halve in zip(wholes, halved)
     ]
-    outs += scatter_buffers(shards, block) + [shape(shards // 2, *block)]
+    experts = parts * gate_up_shares[0].shape[0]
+    shapes = list(wholes)
+    shapes += [(reps, experts) + gate_up_shares[0].shape[1:], (reps, experts) + down_shares[0].shape[1:]]
+    shapes += [(shards,) + block for block in blocks]
+    shapes += blocks + blocks
+    shapes += [(shards // 2,) + block for block in blocks]
+    shapes += [(shards // 2,) + block for block in blocks]
+    shapes += [(shards // 2 + 1,) + block for block in blocks]
     return pl.pallas_call(
-        functools.partial(finish_kernel, shards),
-        out_shape=outs,
-        in_specs=[ANY] * 3,
-        out_specs=[ANY] * len(outs),
-        scratch_shapes=[
-            pltpu.VMEM((5,) + block, jnp.bfloat16),
-            pltpu.VMEM(block, jnp.bfloat16),
-            pltpu.SemaphoreType.DMA((2, shards)),
-            pltpu.SemaphoreType.DMA((2, 2)),
-            pltpu.SemaphoreType.DMA((2,)),
+        functools.partial(finish_kernel, shards, arrays, 2 * parts),
+        out_shape=[jax.ShapeDtypeStruct(shape, jnp.bfloat16) for shape in shapes],
+        in_specs=[ANY] * (arrays + 2 * parts),
+        out_specs=[ANY] * len(shapes),
+        scratch_shapes=[pltpu.VMEM((5,) + block, jnp.bfloat16) for block in blocks]
+        + [pltpu.VMEM(block, jnp.bfloat16) for block in blocks]
+        + [
+            pltpu.SemaphoreType.DMA((2, shards, arrays)),
+            pltpu.SemaphoreType.DMA((2, 2, arrays)),
+            pltpu.SemaphoreType.DMA((2 * parts,)),
         ]
-        + rep_sems(1, 2)
-        + scatter_sems(shards, 1, 5),
+        + rep_sems(1, 2 * parts)
+        + scatter_sems(shards, arrays, 5),
+        cost_estimate=work(0, 4e8),
         compiler_params=pltpu.CompilerParams(
             collective_id=4, has_side_effects=True, vmem_limit_bytes=32 * 2**20
         ),
-    )(grad, gate_up_share, down_share)[:3]
+    )(*grads, *gate_up_shares, *down_shares)[: arrays + 2]
 
 
 def norm_rows(values, gain):
@@ -895,8 +1079,29 @@
     return depth - jnp.sum(jnp.where(hit, depth - levels, 0), axis=2)
 
 
-def w_total(width_q, width_kv):
-    return width_q + 2 * width_kv + D
+def row_pieces(grad, shards):
+    experts, rows, width = grad.shape
+    return grad.astype(jnp.bfloat16).reshape(experts, shards, rows // shards, width).transpose(1, 0, 2, 3)
+
+
+def expert_forward(rows, gates, w_gate_up, w_down, upstream):
+    gate_up = jnp.einsum("td,edf->etf", rows, w_gate_up, preferred_element_type=jnp.float32)
+    gate_part = gate_up[..., :FF]
+    up_part = gate_up[..., FF:]
+    sig_gate = jax.nn.sigmoid(gate_part)
+    hidden = gate_part * sig_gate * up_part
+    gated = (hidden * gates).astype(jnp.bfloat16)
+    mix_part = jnp.einsum("etf,efd->td", gated, w_down, preferred_element_type=jnp.float32)
+    raw_grad = jnp.einsum("td,efd->etf", upstream, w_down, preferred_element_type=jnp.float32)
+    gate_grad = jnp.sum(hidden * raw_grad, axis=-1)
+    hidden_grad = raw_grad * gates
+    gate_grad_part = hidden_grad * up_part * sig_gate * (1.0 + gate_part * (1.0 - sig_gate))
+    up_grad_part = hidden_grad * gate_part * sig_gate
+    row_grads = jnp.concatenate([gate_grad_part, up_grad_part], axis=-1).astype(jnp.bfloat16)
+    down_grad = jnp.einsum("etf,td->efd", gated, upstream, preferred_element_type=jnp.float32)
+    gate_up_grad = jnp.einsum("td,etf->edf", rows, row_grads, preferred_element_type=jnp.float32)
+    act_part = jnp.einsum("etf,edf->td", row_grads, w_gate_up, preferred_element_type=jnp.float32)
+    return (mix_part, gate_grad, act_part, gate_up_grad, down_grad)
 
 
 def shards(
@@ -933,32 +1138,49 @@
     first_expert = rep_index * own_experts
     padding = jnp.zeros((norm_gains.shape[1], LANES - E - 2), jnp.bfloat16)
     small = jnp.concatenate([router_weight, norm_gains.T, padding], axis=1)
-    w_qkv, w_out, small = gather_weights(qkv_weight, out_weight, small, shard_count, rep_count)
-    w_qkv = w_qkv.reshape(rep_count, D, -1)
-    w_out = w_out.reshape(rep_count, D, -1)
+    w_qkv, small = gather_weights(qkv_weight, small, shard_count)
+    w_qkv = w_qkv.reshape(D, -1)
     small = small.reshape(D, LANES)
     w_router = small[:, :E]
     gains = small[:, E : E + 2].T
-    gate_up_own = lax.dynamic_slice_in_dim(gate_up_weight, first_expert, own_experts)
-    down_own = lax.dynamic_slice_in_dim(down_weight, first_expert, own_experts)
-    cot_all = lax.all_gather(cotangent, "rep", axis=0, tiled=True)
+    half = own_experts // 2
     gain_first = gains[0].astype(jnp.float32)
     gain_second = gains[1].astype(jnp.float32)
     token_values = tokens.astype(jnp.float32)
     normed_first, scale_first = norm_rows(token_values, gain_first)
     act_first = normed_first.astype(jnp.bfloat16)
-    projected = jnp.einsum("td,rdc->trc", act_first, w_qkv, preferred_element_type=jnp.float32)
-    projected = projected.reshape(token_count, width_q + 2 * width_kv)
+    projected = jnp.dot(act_first, w_qkv, preferred_element_type=jnp.float32)
     queries = projected[:, :width_q].astype(jnp.bfloat16)
     own_kv = projected[:, width_q:].astype(jnp.bfloat16).reshape(seg_dev, SEG, 2 * width_kv)
     bias = jnp.where(path_alive, 0.0, NEG).astype(jnp.float32)
-    attended, log_totals, group_kv, w_gate_up, w_down = attend_gather(
-        path_slots, bias, queries, own_kv, gate_up_own, down_own, depth, shard_count
-    )
-    w_gate_up = w_gate_up.reshape(own_experts, D, -1)
-    w_down = w_down.reshape(own_experts, FF, D)
-    mixed_out = jnp.einsum("td,rdc->trc", attended, w_out, preferred_element_type=jnp.float32)
-    residual = token_values + mixed_out.reshape(token_count, D)
+    attended, log_totals, group_kv, w_gate_up, w_down, w_out, cot_all = attend_gather(
+        path_slots,
+        bias,
+        queries,
+        own_kv,
+        gate_up_weight,
+        down_weight,
+        out_weight,
+        cotangent,
+        depth,
+        shard_count,
+        rep_count,
+        half,
+    )
+    gate_up_late, down_late, attended = lax.optimization_barrier(
+        (
+            lax.dynamic_slice_in_dim(gate_up_weight, first_expert + half, half),
+            lax.dynamic_slice_in_dim(down_weight, first_expert + half, half),
+            attended,
+        )
+    )
+    w_gate_up_late = lax.all_gather(gate_up_late, "shard", axis=1, tiled=True)
+    w_down_late = lax.all_gather(down_late, "shard", axis=1, tiled=True)
+    w_gate_up = w_gate_up.reshape(half, D, -1)
+    w_down = w_down.reshape(half, FF, D)
+    w_out = w_out.reshape(H * HD, D)
+    cot_all = cot_all.reshape(-1, D)
+    residual = token_values + jnp.dot(attended, w_out, preferred_element_type=jnp.float32)
     normed_second, scale_second = norm_rows(residual, gain_second)
     act_second = normed_second.astype(jnp.bfloat16)
     logits = jnp.dot(act_second, w_router, preferred_element_type=jnp.float32)
@@ -968,20 +1190,25 @@
     gates = jax.nn.softmax(chosen, axis=-1)
     upstream = cotangent.astype(jnp.float32)
     gate_table = jnp.sum(jnp.where(picks, gates[:, :, None], 0.0), axis=1)
-    act_all = lax.all_gather(act_second, "rep", axis=0, tiled=True)
-    gate_all = lax.all_gather(gate_table, "rep", axis=0, tiled=True)
-    own_gate = lax.dynamic_slice_in_dim(gate_all, first_expert, own_experts, axis=1).T[:, :, None]
-    gate_up = jnp.einsum("td,edf->etf", act_all, w_gate_up, preferred_element_type=jnp.float32)
-    gate_part = gate_up[..., :FF]
-    up_part = gate_up[..., FF:]
-    sig_gate = jax.nn.sigmoid(gate_part)
-    hidden = gate_part * sig_gate * up_part
-    gated = (hidden * own_gate).astype(jnp.bfloat16)
-    mix_part = jnp.einsum("etf,efd->td", gated, w_down, preferred_element_type=jnp.float32)
-    mixture = lax.psum_scatter(mix_part.astype(jnp.bfloat16), "rep", scatter_dimension=0, tiled=True)
-    block_out = (residual + mixture.astype(jnp.float32)).astype(jnp.bfloat16)
-    raw_grad = jnp.einsum("td,efd->etf", cot_all, w_down, preferred_element_type=jnp.float32)
-    gate_grad_own = jnp.sum(hidden * raw_grad, axis=-1)
+    act_all, gate_all = share_rows(act_second, gate_table.T, rep_count)
+    act_all = act_all.reshape(-1, D)
+    own_gate = lax.dynamic_slice_in_dim(gate_all, first_expert, own_experts, axis=1)
+    own_gate = own_gate.transpose(1, 0, 2).reshape(own_experts, -1, 1)
+    first_half = expert_forward(act_all, own_gate[:half], w_gate_up, w_down, cot_all)
+    first_half = first_half[:3] + (
+        row_pieces(first_half[3], shard_count),
+        row_pieces(first_half[4], shard_count),
+    )
+    first_half, w_gate_up_late, w_down_late = lax.optimization_barrier(
+        (first_half, w_gate_up_late, w_down_late)
+    )
+    second_half = expert_forward(act_all, own_gate[half:], w_gate_up_late, w_down_late, cot_all)
+    mix_part = first_half[0] + second_half[0]
+    gate_grad_own = jnp.concatenate([first_half[1], second_half[1]], axis=0)
+    gate_up_early = lax.psum_scatter(first_half[3], "shard", scatter_dimension=0, tiled=False)
+    down_early = lax.psum_scatter(first_half[4], "shard", scatter_dimension=0, tiled=False)
+    down_grad = second_half[4]
+    gate_up_grad = second_half[3]
     gate_grad_all = lax.all_gather(gate_grad_own, "rep", axis=0, tiled=True)
     gate_grad_table = lax.dynamic_slice_in_dim(
         gate_grad_all, rep_index * token_count, token_count, axis=1
@@ -994,22 +1221,8 @@
         precision=lax.Precision.HIGHEST,
         preferred_element_type=jnp.float32,
     )
-    hidden_grad = raw_grad * own_gate
-    gate_grad_part = hidden_grad * up_part * sig_gate * (1.0 + gate_part * (1.0 - sig_gate))
-    up_grad_part = hidden_grad * gate_part * sig_gate
-    gate_up_grad_rows = jnp.concatenate([gate_grad_part, up_grad_part], axis=-1).astype(
-        jnp.bfloat16
-    )
-    down_grad = jnp.einsum("etf,td->efd", gated, cot_all, preferred_element_type=jnp.float32)
-    gate_up_grad = jnp.einsum(
-        "td,etf->edf", act_all, gate_up_grad_rows, preferred_element_type=jnp.float32
-    )
-    act_part = jnp.einsum(
-        "etf,edf->td", gate_up_grad_rows, w_gate_up, preferred_element_type=jnp.float32
-    )
-    act_second_grad = lax.psum_scatter(
-        act_part.astype(jnp.bfloat16), "rep", scatter_dimension=0, tiled=True
-    ).astype(jnp.float32)
+    act_part = (first_half[2] + second_half[2]).astype(jnp.bfloat16)
+    act_second_grad = join_reps(act_part.reshape(rep_count, token_count, D))
     act_second_grad = act_second_grad + jnp.dot(
         logit_grad,
         w_router.astype(jnp.float32).T,
@@ -1022,12 +1235,14 @@
     residual_grad = upstream + through_second
     branch_grad = residual_grad.astype(jnp.bfloat16)
     out_grad = jnp.dot(attended.T, branch_grad, preferred_element_type=jnp.float32)
-    attended_grad = jnp.einsum(
-        "trc,rdc->td",
-        branch_grad.reshape(token_count, rep_count, D // rep_count),
-        w_out,
-        preferred_element_type=jnp.float32,
+    attended_grad = lax.dot_general(
+        branch_grad, w_out, (((1,), (1,)), ((), ())), preferred_element_type=jnp.float32
     ).astype(jnp.bfloat16)
+    attended_grad, gate_up_early, down_early, mix_part = lax.optimization_barrier(
+        (attended_grad, gate_up_early, down_early, mix_part.astype(jnp.bfloat16))
+    )
+    mixture = lax.psum_scatter(mix_part, "rep", scatter_dimension=0, tiled=True)
+    block_out = (residual + mixture.astype(jnp.float32)).astype(jnp.bfloat16)
     query_grad, own_grad, gate_up_share, down_share = attend_back(
         path_slots,
         bias,
@@ -1037,8 +1252,8 @@
         attended,
         attended_grad,
         log_totals,
-        gate_up_grad.astype(jnp.bfloat16).reshape(own_experts, shard_count, -1, 2 * FF),
-        down_grad.astype(jnp.bfloat16).reshape(own_experts, shard_count, -1, D),
+        gate_up_grad.astype(jnp.bfloat16).reshape(half, shard_count, -1, 2 * FF),
+        down_grad.astype(jnp.bfloat16).reshape(half, shard_count, -1, D),
         depth,
         shard_count,
     )
@@ -1046,41 +1261,37 @@
         [query_grad, own_grad.reshape(token_count, 2 * width_kv)], axis=1
     )
     qkv_grad = jnp.dot(act_first.T, projected_grad, preferred_element_type=jnp.float32)
-    act_first_grad = jnp.einsum(
-        "trc,rdc->td",
-        projected_grad.reshape(token_count, rep_count, -1),
-        w_qkv,
-        preferred_element_type=jnp.float32,
+    act_first_grad = lax.dot_general(
+        projected_grad, w_qkv, (((1,), (1,)), ((), ())), preferred_element_type=jnp.float32
     )
     through_first, gain_grad_first = norm_back(
         token_values, scale_first, gains[0].astype(jnp.float32), act_first_grad
     )
     token_grad = residual_grad + through_first
-    width = 2 * LANES * -(-(w_total(width_q, width_kv) + E + 2) // (2 * LANES))
-    padding = jnp.zeros((D, width - w_total(width_q, width_kv) - E - 2), jnp.float32)
-    joined = jnp.concatenate(
+    small_grad = jnp.concatenate(
         [
-            qkv_grad,
-            out_grad,
             gain_grad_first[:, None],
             gain_grad_second[:, None],
             router_grad,
-            padding,
+            jnp.zeros((D, LANES - E - 2), jnp.float32),
         ],
         axis=1,
-    ).astype(jnp.bfloat16)
-    joined = joined.reshape(shard_count, 1, D // shard_count, 2, width // 2).transpose(3, 0, 1, 2, 4)
-    joined, gate_up_grad, down_grad = finish_grads(joined, gate_up_share, down_share, rep_count)
-    joined = joined.transpose(1, 2, 0, 3).reshape(D // shard_count, width).astype(jnp.float32)
-    at_out = width_q + 2 * width_kv
-    at_small = at_out + D
+    )
+    grads = [
+        grad.astype(jnp.bfloat16).reshape(shard_count, 1, D // shard_count, -1)
+        for grad in (qkv_grad, out_grad, small_grad)
+    ]
+    qkv_grad, out_grad, small_grad, gate_up_grad, down_grad = finish_grads(
+        grads, (True, True, False), (gate_up_early, gate_up_share), (down_early, down_share), rep_count
+    )
+    small_grad = small_grad[0].astype(jnp.float32)
     return (
         block_out,
         token_grad,
-        joined[:, at_small : at_small + 2].T,
-        joined[:, :at_out],
-        joined[:, at_out:at_small],
-        joined[:, at_small + 2 : at_small + 2 + E],
+        small_grad[:, :2].T,
+        qkv_grad[0].astype(jnp.float32),
+        out_grad[0].astype(jnp.float32),
+        small_grad[:, 2 : 2 + E],
         gate_up_grad.reshape((E,) + gate_up_grad.shape[2:]).astype(jnp.float32),
         down_grad.reshape((E,) + down_grad.shape[2:]).astype(jnp.float32),
     )

time: 1370 us -> 1170 us (0.85); the launches traced: 1370 us -> 1140 us
  Pallas kernels: 841 us -> 700 us
  local copies, waits for them, and re-layouts: 111 us -> 55.4 us
  waiting for transfers between devices: 80.2 us -> 33.7 us
  matrix products: 271 us -> 300 us
    pallas_call x1, Pallas kernels: 325 us -> 201 us  [attend_back(): pl.pallas_call(functools.partial(back_kernel, depth, shards), out_shape=o...]
    all_gather x2, waiting for transfers between devices: 63.5 us -> 0.01 us  [the longest x1 0.01 us: shards(): w_down_late = lax.all_gather(down_late, 'shard', axis=1, tiled=True)]
    convert_element_type x4 -> x2, local copies, waits for them, and re-layouts: 50.7 us -> 17.5 us  [the longest x1 8.8 us: shards(): gate_up_grad.astype(jnp.bfloat16).reshape(half, shard_count, -1, 2 * FF)]
    pallas_call x1, Pallas kernels: 91.1 us -> 60.7 us  [gather_weights(): pl.pallas_call(functools.partial(weights_kernel, shards), out_shape=[jax....]
    dot_general x10 -> x16, matrix products: 246 us -> 272 us  [the longest x2 47.5 us: expert_forward(): jnp.einsum('td,edf->etf', rows, w_gate_up, preferred_element_type=jnp.flo...]
    concatenate x1 -> x2, local copies, waits for them, and re-layouts: 19.7 us -> 1.41 us  [shards(): jnp.concatenate([gain_grad_first[:, None], gain_grad_second[:, None], rou...]
    reduce_scatter x2 -> x3, waiting for transfers between devices: 16 us -> 32.9 us  [the longest x1 32.9 us: shards(): lax.psum_scatter(first_half[3], 'shard', scatter_dimension=0, tiled=False)]
    pallas_call x2 -> x4, Pallas kernels: 425 us -> 439 us  [the longest x1 191 us: attend_gather(): pl.pallas_call(functools.partial(attend_gather_kernel, depth, shards, exp...]
  transfers between devices with their start and end apart: 4 -> 5, of which waited for: 3 -> 1; matrix products, arithmetic and copies ran while one was open for 12% -> 30% of each run, Pallas kernels for 0% -> 39%
where the time goes in v4:
time: 1170 us; the launch traced here: 1140 us
  Pallas kernels  700 us (60%)
  matrix products  300 us (26%)
  local copies, waits for them, and re-layouts  55.4 us (5%)
  other arithmetic  34.2 us (3%)
  waiting for transfers between devices  33.7 us (3%)
  between operations  15.1 us (1%)
    pallas_call x1, Pallas kernels, attend_back(): pl.pallas_call(functools.partial(back_kernel, depth, shards), out_shape=o...  201 us
    pallas_call x1, Pallas kernels, attend_gather(): pl.pallas_call(functools.partial(attend_gather_kernel, depth, shards, exp...  191 us
    pallas_call x1, Pallas kernels, finish_grads(): pl.pallas_call(functools.partial(finish_kernel, shards, arrays, 2 * parts...  137 us
    pallas_call x1, Pallas kernels, share_rows(): pl.pallas_call(functools.partial(share_kernel, chunks), out_shape=[jax.Sh...  63.2 us
    pallas_call x1, Pallas kernels, gather_weights(): pl.pallas_call(functools.partial(weights_kernel, shards), out_shape=[jax....  60.7 us
    pallas_call x1, Pallas kernels, join_reps(): pl.pallas_call(join_kernel, out_shape=jax.ShapeDtypeStruct(block, jnp.flo...  47.6 us
    dot_general x2, matrix products, expert_forward(): jnp.einsum('td,edf->etf', rows, w_gate_up, preferred_element_type=jnp.flo...  47.5 us
    dot_general x2, matrix products, expert_forward(): jnp.einsum('td,efd->etf', upstream, w_down, preferred_element_type=jnp.fl...  46.1 us
  transfers between devices with their start and end apart: 5, of which 1 were waited for; matrix products, arithmetic and copies ran while one was open for 30% of the time, Pallas kernels for 39%

profile of v4, /device:TPU:9, one launch (start us, length us, event | category | flops | bytes accessed | tf_op | source)
XLA Modules:
  0.0 1144.1 jit_solution(2570192354071505092)
XLA Ops:
  7.3 2.0 fusion.6
  9.9 0.8 copy.187
  10.7 0.8 copy.188
  11.6 0.7 maximum_maximum_fusion.1.small
  12.3 60.7 %shard_map.170 = (bf16[8,192,2560]{2,1,0:T(8,128)(2,1)}, bf16[8,192,128]{2,1,0:T(8,128)(2,1)}) custom-call(bf16[192,2560]{1,0:T(8,128)(2,1)} %qkv.1, bf16[192,128]{1,0:T(8,128)(2,1)} %maximum_maximum_fusion.1.small), custom_call_target="tpu_custom_call" | custom-call | bytes 200000000 | tf_op jit(solution)/shard_map/pallas_call | solution.py:356
  73.0 1.2 slice.62
  75.0 8.3 convolution_convert_fusion.2
  83.5 1.4 slice.64.q_ref
  89.2 1.8 constant_dynamic-slice_fusion.1
  91.0 2.1 constant_dynamic-slice_fusion.2
  93.2 191.3 %shard_map.171 = (bf16[640,1536]{1,0:T(8,128)(2,1)S(1)}, f32[20,8,768]{2,1,0:T(8,128)S(1)}, bf16[20,128,1024]{2,1,0:T(8,128)(2,1)}, bf16[2,8,192,1024]{3,2,1,0:T...) custom-call(s32[5,10]{1,0:T(8,128)S(1)} %stack.73.slots, ...), custom_call_target="tpu_custom_call" | custom-call | flops 20000000000 | bytes 700000000 | tf_op jit(solution)/shard_map/pallas_call | solution.py:476
  284.5 1.3 copy-done.14
  285.8 0.8 copy-done.16
  286.6 0.7 all-gather.4.cloned.1.call-update
  287.4 6.9 multiply_reduce_fusion.2
  294.9 1.2 copy-done.17
  297.3 0.7 select_reduce_fusion
  298.0 63.2 %shard_map.172 = (bf16[4,640,1536]{2,1,0:T(8,128)(2,1)}, f32[4,16,640]{2,1,0:T(8,128)}) custom-call(bf16[640,1536]{1,0:T(8,128)(2,1)} %copy-done.19, f32[16,640]{1,0:T(8,128)} %bitcast.170), custom_call_target="tpu_custom_call" | custom-call | bytes 160000000 | tf_op jit(solution)/shard_map/pallas_call | solution.py:515
  361.2 0.9 dynamic-slice_bitcast_fusion
  362.1 0.6 fusion.48
  362.7 23.9 %convolution_bitcast_fusion.3 = f32[2,2560,1024]{1,2,0:T(8,128)} fusion(bf16[2,1536,1024]{2,1,0:T(8,128)(2,1)} %bitcast.202, bf16[2560,1536,1]{1,0,2:T(8,128)(2,1)} %bitcast.194), kind=kOutput, calls=%fused_computation.26 | convolution fusion | flops 16106127360 | bytes 35127296 | tf_op jit(solution)/shard_map/td,edf->etf/dot_general | solution.py:1088
  386.7 23.2 %multiply_convert_fusion.4 = (bf16[2,2560,512]{1,2,0:T(8,128)(2,1)}, bf16[2,2560,512]{1,2,0:T(8,128)(2,1)}, f32[2,2560]{1,0:T(2,128)}, f32[2,2560,512]{1,2,0:T(8,128)}) fusion(f32[2,2560,1024]{1,2,0:T(8,128)} %convolution_bitcast_fusion.3, f32[2,2560]{1,0:T(2,128)S(1)} %bitcast.176, bf16[2,512,1536]{2,1,0:T(8,128)(2,1)S(1)} %bitcast.210, ...), kind=kOutput, calls=%fused_computation.21 | convolution fusion | flops 8100244480 | bytes 52994048 | tf_op jit(solution)/shard_map/td,efd->etf/dot_general | solution.py:1095
  409.9 13.4 %convolution_convert_fusion.4 = bf16[2,512,1536]{2,1,0:T(8,128)(2,1)S(1)} fusion(bf16[2560,1536,1]{1,0,2:T(8,128)(2,1)} %bitcast.199, f32[2,2560,512]{1,2,0:T(8,128)} %get-tuple-element.150, f32[2,2560]{1,0:T(2,128)S(1)} %bitcast.177), kind=kOutput, calls=%fused_computation.57 | convolution fusion | flops 8059879424 | bytes 21516288 | tf_op jit(solution)/shard_map/etf,td->efd/dot_general | solution.py:1101
  423.3 1.9 copy.217
  425.3 1.8 copy-done.50
  427.0 19.1 %convert_bitcast_fusion.1 = bf16[2,1536,1024]{1,2,0:T(8,128)(2,1)} fusion(bf16[2560,1536,1]{1,0,2:T(8,128)(2,1)S(1)} %bitcast.197, bf16[2,2560,512]{1,2,0:T(8,128)(2,1)} %get-tuple-element.146, bf16[2,2560,512]{1,2,0:T(8,128)(2,1)S(1)} %copy-done.50), kind=kOutput, calls=%fused_computation.39 | convolution fusion | flops 16130244608 | bytes 24641536 | tf_op jit(solution)/shard_map/td,etf->edf/dot_general | solution.py:1102
  446.1 8.7 copy.193
  454.8 6.6 copy.216
  461.4 15.4 %convolution_bitcast_fusion.1 = f32[2560,1536]{1,0:T(8,128)} fusion(bf16[2,512,1536]{2,1,0:T(8,128)(2,1)S(1)} %bitcast.211, f32[2,2560,512]{1,2,0:T(8,128)} %get-tuple-element.150, f32[2,2560]{1,0:T(2,128)S(1)} %bitcast.178), kind=kOutput, calls=%fused_computation.5 | convolution fusion | flops 8058306560 | bytes 29380608 | tf_op jit(solution)/shard_map/etf,efd->td/dot_general | solution.py:1094
  476.8 20.6 %convolution_bitcast_fusion = f32[2560,1536]{1,0:T(8,128)} fusion(bf16[2,1536,1024]{2,1,0:T(8,128)(2,1)S(1)} %bitcast.205, bf16[2,2560,512]{1,2,0:T(8,128)(2,1)} %get-tuple-element.146, bf16[2,2560,512]{1,2,0:T(8,128)(2,1)S(1)} %bitcast.216), kind=kOutput, calls=%fused_computation.4 | convolution fusion | flops 16127098880 | bytes 32505856 | tf_op jit(solution)/shard_map/etf,edf->td/dot_general | solution.py:1103
  498.4 23.5 %convolution_bitcast_fusion.2 = f32[2,2560,1024]{1,2,0:T(8,128)} fusion(bf16[2,1536,1024]{2,1,0:T(8,128)(2,1)} %all-gather.4.cloned.1.call-done, bf16[2560,1536,1]{1,0,2:T(8,128)(2,1)} %bitcast.195), kind=kOutput, calls=%fused_computation.25 | convolution fusion | flops 16106127360 | bytes 35127296 | tf_op jit(solution)/shard_map/td,edf->etf/dot_general | solution.py:1088
  522.0 22.8 %fusion.2 = (f32[2,2560]{1,0:T(2,128)S(1)}, f32[2,2560,512]{1,2,0:T(8,128)}, bf16[2,2560,512]{1,2,0:T(8,128)(2,1)}, bf16[2,2560,512]{1,2,0:T(8,128)(2,1)}) fusion(f32[2,2560,1024]{1,2,0:T(8,128)} %convolution_bitcast_fusion.2, f32[2,2560]{1,0:T(2,128)S(1)} %bitcast.173, bf16[2,512,1536]{2,1,0:T(8,128)(2,1)} %all-gather.6.cloned.1.call-done, ...), kind=kOutput, calls=%fused_computation.11 | convolution fusion | flops 8100244480 | bytes 52994048 | tf_op jit(solution)/shard_map/td,efd->etf/dot_general | solution.py:1095
  544.8 25.2 %fusion.1 = bf16[2560,1536]{1,0:T(8,128)(2,1)} fusion(f32[2560,1536]{1,0:T(8,128)} %convolution_bitcast_fusion, bf16[2,1536,1024]{2,1,0:T(8,128)(2,1)} %all-gather.4.cloned.1.call-done, bf16[2,2560,512]{1,2,0:T(8,128)(2,1)} %get-tuple-element.147, bf16[2,2560,512]{1,2,0:T(8,128)(2,1)} %get-tuple-element.148), kind=kOutput, calls=%fused_computation.3 | convolution fusion | flops 16134963200 | bytes 40370176 | tf_op jit(solution)/shard_map/etf,edf->td/dot_general | solution.py:1103
  570.0 3.2 copy-done.3
  573.3 47.6 %shard_map.173 = f32[640,1536]{1,0:T(8,128)S(1)} custom-call(bf16[4,640,1536]{2,1,0:T(8,128)(2,1)S(1)} %bitcast.155), custom_call_target="tpu_custom_call" | custom-call | bytes 160000000 | tf_op jit(solution)/shard_map/pallas_call | solution.py:587
  620.9 1.9 copy-done.2
  622.8 5.6 all-gather
  628.6 6.4 multiply_reduce_fusion
  635.1 1.0 subtract_add_fusion
  636.2 4.7 convolution_convert_fusion.5.do_ref
  640.9 17.0 %fusion = bf16[2560,1536]{1,0:T(8,128)(2,1)} fusion(f32[2560,1536]{1,0:T(8,128)} %convolution_bitcast_fusion.1, bf16[2,512,1536]{2,1,0:T(8,128)(2,1)S(1)} %copy-done.48, f32[2,2560,512]{1,2,0:T(8,128)} %get-tuple-element.133, f32[2,2560]{1,0:T(2,128)S(1)} %bitcast.174), kind=kOutput, calls=%fused_computation.1 | convolution fusion | flops 8066170880 | bytes 37244928 | tf_op jit(solution)/shard_map/etf,efd->td/dot_general | solution.py:1094
  657.8 32.9 %reduce-scatter.4.cloned.1.call-done = bf16[1,2,192,1024]{3,2,1,0:T(8,128)(2,1)} async-done(((bf16[8,2,192,1024]{3,2,1,0:T(8,128)(2,1)}), bf16[1,2,192,1024]{3,2,1,0:T(8,128)(2,1)}) %reduce-scatter.4.cloned.1.call-update) | async-done | bytes 786448 | tf_op jit(solution)/shard_map/reduce_scatter | solution.py:1208
  690.7 22.7 %convert_bitcast_fusion = bf16[2,1536,1024]{1,2,0:T(8,128)(2,1)} fusion(bf16[2560,1536,1]{1,0,2:T(8,128)(2,1)} %bitcast.196, bf16[2,2560,512]{1,2,0:T(8,128)(2,1)} %get-tuple-element.147, bf16[2,2560,512]{1,2,0:T(8,128)(2,1)} %get-tuple-element.148), kind=kOutput, calls=%fused_computation.38 | convolution fusion | flops 16130244608 | bytes 24641536 | tf_op jit(solution)/shard_map/td,etf->edf/dot_general | solution.py:1102
  713.4 8.8 copy.201
  722.2 2.4 convolution_convert_fusion.6
  724.9 0.7 concatenate.44
  725.6 7.7 convolution_convert_fusion.1
  733.3 14.6 %convolution_convert_fusion.3 = bf16[2,512,1536]{2,1,0:T(8,128)(2,1)} fusion(bf16[2560,1536,1]{1,0,2:T(8,128)(2,1)} %bitcast.201, f32[2,2560,512]{1,2,0:T(8,128)} %get-tuple-element.133, f32[2,2560]{1,0:T(2,128)S(1)} %bitcast.175), kind=kOutput, calls=%fused_computation.56 | convolution fusion | flops 8059879424 | bytes 21516288 | tf_op jit(solution)/shard_map/etf,td->efd/dot_general | solution.py:1101
  747.9 200.6 %shard_map.174 = (bf16[640,1536]{1,0:T(8,128)(2,1)}, bf16[5,128,1024]{2,1,0:T(8,128)(2,1)}, bf16[2,192,1024]{2,1,0:T(8,128)(2,1)}, bf16[2,64,1536]{2,1,0:T(8,128...) custom-call(s32[5,10]{1,0:T(8,128)} %copy-done.11, ...), custom_call_target="tpu_custom_call" | custom-call | flops 49999998976 | bytes 700000000 | tf_op jit(solution)/shard_map/pallas_call | solution.py:864
  948.5 10.4 fusion.14
  958.9 0.7 concatenate.43
  960.1 10.8 convolution_convert_fusion
  970.9 137.0 %shard_map.175 = (bf16[1,192,2560]{2,1,0:T(8,128)(2,1)S(1)}, bf16[1,192,1536]{2,1,0:T(8,128)(2,1)S(1)}, bf16[1,192,128]{2,1,0:T(8,128)(2,1)S(1)}, bf16[4,4,192,1...) custom-call(bf16[8,1,192,2560]{3,2,1,0:T(8,128)(2,1)} %bitcast.162, ...), custom_call_target="tpu_custom_call" | custom-call | bytes 400000000 | tf_op jit(solution)/shard_map/pallas_call | solution.py:1013
  1107.9 0.9 copy-done.4
  1108.8 0.8 copy-done.8
  1109.7 0.7 copy.206
  1110.4 0.7 copy.205
  1111.1 2.2 bitcast_convert_fusion.3
  1113.3 9.2 bitcast_convert_fusion
  1122.5 1.5 bitcast_convert_fusion.2
  1124.0 4.3 bitcast_convert_fusion.1
  1128.3 1.3 copy-done.23
  1129.6 2.9 fusion.11
  1132.5 4.6 add_convert_fusion
  (195 shorter events, 9.8 us)
Async XLA Ops:
  7.2 77.9 %copy-start = (s32[8,20]{1,0:T(8,128)S(1)}, s32[8,20]{1,0:T(8,128)}, u32[]{:S(2)}) copy-start(s32[8,20]{1,0:T(8,128)} %param.20) | copy-start | bytes 1924
  7.2 490.3 %all-gather.6.cloned.1.call-start = ((), (), s32[]{:S(2)}) async-start(), calls=%async_computation.4 | async-start | bytes 3538944 | tf_op jit(solution)/shard_map/all_gather | solution.py:1178
  9.9 64.6 %copy-start.39 = (f32[640]{0:T(1024)}, f32[640]{0:T(1024)S(1)}, u32[]{:S(2)}) copy-start(f32[640]{0:T(1024)S(1)} %get-tuple-element.154) | copy-start | bytes 7684
  11.6 61.4 %copy-start.44 = (bf16[128]{0:T(256)(128)(2,1)}, bf16[128]{0:T(256)(128)(2,1)S(1)}, u32[]{:S(2)}) copy-start(bf16[128]{0:T(256)(128)(2,1)S(1)} %pad.14.clone) | copy-start | bytes 772
  74.4 0.6 copy-start.34
  74.4 220.5 %copy-start.29 = (f32[1536]{0:T(1024)}, f32[1536]{0:T(1024)S(1)}, u32[]{:S(2)}) copy-start(f32[1536]{0:T(1024)S(1)} %get-tuple-element.120) | copy-start | bytes 18436
  83.3 1.6 copy-start.46
  83.3 9.8 copy-start.13
  88.5 4.6 copy-start.42
  88.5 196.0 %copy-start.12 = (f32[5,10]{1,0:T(8,128)}, f32[5,10]{1,0:T(8,128)S(1)}, u32[]{:S(2)}) copy-start(f32[5,10]{1,0:T(8,128)S(1)} %broadcast_select_fusion.bias) | copy-start | bytes 604
  93.1 404.4 %copy-start.11 = (s32[5,10]{1,0:T(8,128)}, s32[5,10]{1,0:T(8,128)S(1)}, u32[]{:S(2)}) copy-start(s32[5,10]{1,0:T(8,128)S(1)} %stack.73.slots) | copy-start | bytes 604
  284.5 1.3 copy-start.14
  285.8 0.8 copy-start.16
  286.6 210.8 %all-gather.4.cloned.1.call-start = ((), (), s32[]{:S(2)}) async-start(), calls=%async_computation.3 | async-start | bytes 7077888 | tf_op jit(solution)/shard_map/all_gather | solution.py:1177
  287.3 370.5 %reduce-scatter.6.cloned.1.call-start = ((), (), s32[]{:S(2)}) async-start(), calls=%async_computation.6 | async-start | bytes 3538944 | tf_op jit(solution)/shard_map/reduce_scatter | solution.py:1209
  294.2 1.9 copy-start.17
  294.3 2.3 copy-start.25
  294.3 2.9 copy-start.31
  294.9 1.6 copy-start.32
  296.5 1.4 copy-start.19
  362.7 23.9 %copy-start.49 = (bf16[2,8,64,1536]{3,2,1,0:T(8,128)(2,1)S(1)}, bf16[2,8,64,1536]{3,2,1,0:T(8,128)(2,1)}, u32[]{:S(2)}) copy-start(bf16[2,8,64,1536]{3,2,1,0:T(8,128)(2,1)} %get-tuple-element.50) | copy-start | bytes 9437188
  409.9 15.3 %copy-start.47 = (bf16[4,640,1536]{2,1,0:T(8,128)(2,1)S(1)}, bf16[4,640,1536]{2,1,0:T(8,128)(2,1)}, u32[]{:S(2)}) copy-start(bf16[4,640,1536]{2,1,0:T(8,128)(2,1)} %get-tuple-element.48) | copy-start | bytes 23592964
  423.3 3.7 copy-start.50
  454.8 22.0 %slice-start = ((s8[6291456]{0:T(1024)(128)(4,1)}), s8[4194304]{0:T(1024)(128)(4,1)S(1)}, s32[]{:S(2)}) async-start(s8[6291456]{0:T(1024)(128)(4,1)} %bitcast.203), calls=%async_computation.8 | async-start | bytes 8388608
  454.8 22.0 %slice-start.4 = ((s8[5242880]{0:T(1024)(128)(4,1)}), s8[4194304]{0:T(1024)(128)(4,1)S(1)}, s32[]{:S(2)}) async-start(s8[5242880]{0:T(1024)(128)(4,1)} %bitcast.215), calls=%async_computation.12 | async-start | bytes 8388608
  461.4 15.4 %slice-start.1 = ((s8[6291456]{0:T(1024)(128)(4,1)}), s8[2097152]{0:T(1024)(128)(4,1)S(1)}, s32[]{:S(2)}) async-start(s8[6291456]{0:T(1024)(128)(4,1)} %bitcast.203), calls=%async_computation.9 | async-start | bytes 4194304
  461.4 15.4 %slice-start.5 = ((s8[5242880]{0:T(1024)(128)(4,1)}), s8[1048576]{0:T(1024)(128)(4,1)S(1)}, s32[]{:S(2)}) async-start(s8[5242880]{0:T(1024)(128)(4,1)} %bitcast.215), calls=%async_computation.13 | async-start | bytes 2097152
  476.8 20.8 %copy-start.43 = (pred[5,10]{1,0:T(8,128)(4,1)S(1)}, pred[5,10]{1,0:T(8,128)(4,1)}, u32[]{:S(2)}) copy-start(pred[5,10]{1,0:T(8,128)(4,1)} %copy-done.42) | copy-start | bytes 154
  497.5 193.3 %reduce-scatter.4.cloned.1.call-start = ((), (), s32[]{:S(2)}) async-start(), calls=%async_computation.5 | async-start | bytes 7077888 | tf_op jit(solution)/shard_map/reduce_scatter | solution.py:1208
  498.4 23.6 %copy-start.36 = (f32[2,4,640]{2,0,1:T(2,128)S(1)}, f32[2,4,640]{2,0,1:T(2,128)}, u32[]{:S(2)}) copy-start(f32[2,4,640]{2,0,1:T(2,128)} %get-tuple-element.151) | copy-start | bytes 61444
  498.4 634.1 %reduce-scatter.8.cloned.1.call-start = ((), (), s32[]{:S(2)}) async-start(), calls=%async_computation.7 | async-start | bytes 9830400 | tf_op jit(solution)/shard_map/reduce_scatter | solution.py:1244
  570.0 3.2 copy-start.3
  573.3 49.5 %copy-start.37 = (f32[2,2560]{1,0:T(2,128)S(1)}, f32[2,2560]{1,0:T(2,128)}, u32[]{:S(2)}) copy-start(f32[2,2560]{1,0:T(2,128)} %get-tuple-element.57) | copy-start | bytes 61444
  573.3 55.2 %copy-start.28 = (f32[640,16]{0,1:T(8,128)S(1)}, f32[640,16]{0,1:T(8,128)}, u32[]{:S(2)}) copy-start(f32[640,16]{0,1:T(8,128)} %select_reduce_fusion) | copy-start | bytes 122884
  573.3 55.2 %copy-start.26 = (bf16[8,192,128]{2,1,0:T(8,128)(2,1)S(1)}, bf16[8,192,128]{2,1,0:T(8,128)(2,1)}, u32[]{:S(2)}) copy-start(bf16[8,192,128]{2,1,0:T(8,128)(2,1)} %get-tuple-element.42) | copy-start | bytes 1179652
  573.3 55.3 %copy-start.30 = (f32[1536]{0:T(1024)S(1)}, f32[1536]{0:T(1024)}, u32[]{:S(2)}) copy-start(f32[1536]{0:T(1024)} %copy-done.29) | copy-start | bytes 18436
  573.3 55.3 %copy-start.33 = (f32[640]{0:T(1024)S(1)}, f32[640]{0:T(1024)}, u32[]{:S(2)}) copy-start(f32[640]{0:T(1024)} %copy-done.32) | copy-start | bytes 7684
  620.9 1.9 copy-start.2
  628.5 6.5 copy-start.18
  628.5 6.5 copy-start.27
  628.6 6.5 copy-start.41
  628.6 7.5 slice-start.2
  635.1 1.1 slice-start.3
  636.1 4.7 copy-start.20
  636.2 4.7 copy-start.48
  713.4 12.2 %copy-start.15 = (bf16[640,1536]{1,0:T(8,128)(2,1)S(1)}, bf16[640,1536]{1,0:T(8,128)(2,1)}, u32[]{:S(2)}) copy-start(bf16[640,1536]{1,0:T(8,128)(2,1)} %copy-done.14) | copy-start | bytes 5898244
  747.9 200.6 %copy-start.22 = (bf16[640,1536]{1,0:T(8,128)(2,1)S(1)}, bf16[640,1536]{1,0:T(8,128)(2,1)}, u32[]{:S(2)}) copy-start(bf16[640,1536]{1,0:T(8,128)(2,1)} %param.11) | copy-start | bytes 5898244
  747.9 200.6 %copy-start.35 = (f32[1536]{0:T(1024)S(1)}, f32[1536]{0:T(1024)}, u32[]{:S(2)}) copy-start(f32[1536]{0:T(1024)} %copy-done.34) | copy-start | bytes 18436
  747.9 200.6 %copy-start.40 = (f32[640]{0:T(1024)S(1)}, f32[640]{0:T(1024)}, u32[]{:S(2)}) copy-start(f32[640]{0:T(1024)} %copy-done.39) | copy-start | bytes 7684
  948.5 11.1 copy-start.45
  960.0 10.8 copy-start.6
  960.0 10.8 copy-start.7
  960.0 10.8 copy-start.9
  960.1 10.8 copy-start.10
  1107.9 0.9 copy-start.4
  1108.8 0.8 copy-start.8
  1113.3 9.2 copy-start.5
  1122.5 5.8 copy-start.24
  1124.0 4.3 copy-start.21
  1124.0 5.5 copy-start.23
  1124.0 5.5 copy-start.38
  1129.6 7.6 copy-start.1
Sparse Core Ops, SparseCore 0:
  286.7 57.6 all-gather.5
  347.2 96.6 all-gather.3
  497.6 71.8 reduce-scatter.5
  573.5 117.1 reduce-scatter.3
  693.1 69.0 reduce-scatter.7

commit v5 on v4

--- a/solution.py
+++ b/solution.py
@@ -187,17 +187,18 @@
 
 
 class LineGather:
-    def __init__(self, shards, sources, region, up, down, pair, local_sem, arrived=None):
+    def __init__(self, shards, sources, region, up, down, pair, local_sem, arrived=None, order=None):
         self.shards, self.sources, self.region = shards, sources, region
         self.up, self.down, self.pair, self.local_sem = up, down, pair, local_sem
         self.arrived = arrived or (lambda cond, block, index: None)
+        self.order = order or tuple(range(len(sources)))
         self.sends = Sends()
         self.me, self.spot, self.length = line_place(shards)
         self.twin = self.me + 1 - 2 * (self.me % 2)
 
     def forward(self, cond, block, step, rising, falling, src=None):
         place = step if rising else self.length - 1 + step
-        for n in range(len(self.sources)):
+        for n in self.order:
             here = self.region(n, block)
             out = here if src is None else src[n]
             ways = []
@@ -400,15 +401,19 @@
 ):
     me = lax.axis_index("shard")
     rep = lax.axis_index("rep")
-    first = me // TREE_DEVS * TREE_DEVS
     member = me % TREE_DEVS
     seg_dev = kv_ref.shape[0]
-    others = [first + lax.rem(member + away, TREE_DEVS) for away in range(1, TREE_DEVS)]
-    greet(line_neighbours(shards) + rep_neighbours() + [(None, {"shard": other}) for other in others])
+    twin = me + 1 - 2 * (member % 2)
+    across = me + 2 - 4 * (member // 2)
+    greet(line_neighbours(shards) + rep_neighbours() + [(None, {"shard": across})])
     sends = Sends()
-    own = kv_all.at[pl.ds(member * seg_dev, seg_dev)]
-    for away, other in enumerate(others):
-        sends.start(None, kv_ref, own, kv_sems.at[0, away], kv_sems.at[1, away], {"shard": other})
+
+    def kv_block(owner):
+        return kv_all.at[pl.ds(owner % TREE_DEVS * seg_dev, seg_dev)]
+
+    own = kv_block(me)
+    sends.start(None, kv_ref, own, kv_sems.at[0, 0], kv_sems.at[1, 0], {"shard": twin})
+    sends.start(None, kv_ref, own, kv_sems.at[0, 1], kv_sems.at[1, 1], {"shard": across})
     width = out_ref.shape[1] // lax.axis_size("rep")
     own_experts = gu_ref.shape[0] // lax.axis_size("rep")
 
@@ -421,8 +426,8 @@
     gather = LineGather(
         shards,
         (
-            gu_ref.at[pl.ds(rep * own_experts, experts)],
-            dn_ref.at[pl.ds(rep * own_experts, experts)],
+            gu_ref.at[pl.ds(rep * own_experts + own_experts // 2 - experts, experts)],
+            dn_ref.at[pl.ds(rep * own_experts, own_experts // 2)],
             part_columns(out_ref, rep, width),
         ),
         lambda n, block: part(n, rep, block),
@@ -431,6 +436,7 @@
         pair,
         local_sem,
         spread.arrived,
+        (2, 0, 1),
     )
     gather.begin()
     sends.local(cot_ref, cot_all.at[rep], cot_sem)
@@ -440,20 +446,25 @@
     gather.finish_local()
     spread.arrived(None, me, 0)
     kv_all[pl.ds(member * seg_dev, seg_dev)] = kv_ref[...]
-    for away in range(TREE_DEVS - 1):
-        source = lax.rem(member + TREE_DEVS - 1 - away, TREE_DEVS)
-        block = kv_all.at[pl.ds(source * seg_dev, seg_dev)]
-        received(None, block, kv_sems.at[0, away], kv_sems.at[1, away], {"shard": first + source})
+    theirs = kv_block(twin)
+    received(None, theirs, kv_sems.at[0, 0], kv_sems.at[1, 0], {"shard": twin})
+    sends.start(None, theirs, theirs, kv_sems.at[0, 2], kv_sems.at[1, 2], {"shard": across})
+    gather.step(1)
+    gather.pair_step(0)
+    received(None, kv_block(across), kv_sems.at[0, 1], kv_sems.at[1, 1], {"shard": across})
+    diagonal = across + 1 - 2 * (member % 2)
+    received(None, kv_block(diagonal), kv_sems.at[0, 2], kv_sems.at[1, 2], {"shard": across})
     count = seg_dev * PAIRS
     attend = functools.partial(fwd_step, depth, slots, bias, q_ref, kv_all, o_ref, lse_ref, s_scr, p_scr)
     done = 0
-    for step in range(1, gather.length):
-        upto = count * step // (gather.length - 1)
+    for step in range(2, gather.length + 1):
+        upto = count * (step - 1) // (gather.length - 1)
         lax.fori_loop(done, upto, attend, 0)
         done = upto
-        gather.step(step)
-        gather.pair_step(step - 1)
-        spread.pass_on()
+        if step < gather.length:
+            gather.step(step)
+            gather.pair_step(step - 1)
+            spread.pass_on()
     cot_spread.end()
     gather.pair_step(gather.length - 1)
     spread.end()
@@ -468,7 +479,7 @@
         q.shape,
         (TREE_DEVS * kv.shape[0],) + kv.shape[1:],
         (experts, shards) + gate_up.shape[1:],
-        (experts, shards) + down.shape[1:],
+        (down.shape[0] // reps // 2, shards) + down.shape[1:],
         (shards,) + out.shape,
         (reps,) + cotangent.shape,
     ]
@@ -652,29 +663,32 @@
         store.start()
         store.wait()
 
-    def begin(self):
-        order = []
-        for step in range(self.length):
-            for target in (self.length - 1 - step, step):
-                if target not in order:
-                    order.append(target)
-        for target in order:
-            block = 2 * target + 1 - self.side
-            self.ready(block)
-            for n in range(self.arrays):
-                sources = self.local(n, block)
-                src = sources[0]
-                if len(sources) > 1:
-                    src = self.temp[n].at[target]
-                    self.add(n, [(None, ref) for ref in sources], src)
-                self.sends.start(
-                    None,
-                    src,
-                    self.pair_buf[n].at[target],
-                    self.pair.at[0, target, n],
-                    self.pair.at[1, target, n],
-                    {"shard": self.twin},
-                )
+    def pick(self, turn):
+        spot, last = self.spot, self.length - 1
+        low = jnp.where(turn < last - spot, last - turn, turn - last + spot)
+        high = jnp.where(turn < spot, turn, last - turn + spot)
+        return jnp.where(turn == last, spot, jnp.where(2 * spot < self.length, low, high))
+
+    def offer(self, turn):
+        if turn >= self.length:
+            return
+        target = self.pick(turn)
+        block = 2 * target + 1 - self.side
+        self.ready(block)
+        for n in range(self.arrays):
+            sources = self.local(n, block)
+            src = sources[0]
+            if len(sources) > 1:
+                src = self.temp[n].at[target]
+                self.add(n, [(None, ref) for ref in sources], src)
+            self.sends.start(
+                None,
+                src,
+                self.pair_buf[n].at[target],
+                self.pair.at[0, target, n],
+                self.pair.at[1, target, n],
+                {"shard": self.twin},
+            )
 
     def got_pair(self, target, n):
         received(
@@ -688,22 +702,22 @@
     def got_line(self, cond, slot, n, device):
         received(cond, self.line_buf[n].at[slot], self.line.at[0, slot, n], self.line.at[1, slot, n], {"shard": device})
 
-    def step(self, step):
+    def step(self, slot):
         below, above = self.spot > 0, self.spot + 1 < self.length
+        mirrored = self.length - 1 - self.spot
         turns = (
-            (self.length - 1 - step, True, below, self.me - 2, self.me + 2),
-            (step, False, above, self.me + 2, self.me - 2),
+            (self.spot <= slot, self.length - 1 - slot + self.spot, True, below, self.me - 2, self.me + 2),
+            (mirrored <= slot, slot - mirrored, False, above, self.me + 2, self.me - 2),
         )
-        for target, rising, has, source, device in turns:
-            cond = self.spot < target if rising else self.spot > target
+        for cond, target, rising, has, source, device in turns:
             block = 2 * target + self.side
-            slot = target if rising else jnp.where(self.spot == target + 1, self.length, target)
+            place = target if rising else jnp.where(self.spot == target + 1, self.length, target)
             for n in range(self.arrays):
                 copy = pltpu.make_async_remote_copy(
                     src_ref=self.pair_buf[n].at[target],
-                    dst_ref=self.line_buf[n].at[slot],
-                    send_sem=self.line.at[0, slot, n],
-                    recv_sem=self.line.at[1, slot, n],
+                    dst_ref=self.line_buf[n].at[place],
+                    send_sem=self.line.at[0, place, n],
+                    recv_sem=self.line.at[1, place, n],
                     device_id={"shard": device},
                     device_id_type=MESH,
                 )
@@ -780,6 +794,8 @@
     d_scr,
     group,
     guest,
+    passing,
+    landed,
     gu_stage,
     dn_stage,
     gu_sum,
@@ -790,11 +806,11 @@
     loads,
 ):
     me = lax.axis_index("shard")
-    first = me // TREE_DEVS * TREE_DEVS
     member = me % TREE_DEVS
     segs = q_ref.shape[0] // SEG
-    others = [first + lax.rem(member + away, TREE_DEVS) for away in range(1, TREE_DEVS)]
-    greet(line_neighbours(shards) + [(None, {"shard": other}) for other in others])
+    twin = me + 1 - 2 * (member % 2)
+    across = me + 2 - 4 * (member // 2)
+    greet(line_neighbours(shards) + [(None, {"shard": across})])
     scatter = LineScatter(
         shards,
         2,
@@ -808,42 +824,57 @@
         line,
         loads,
     )
-    scatter.begin()
+    scatter.offer(0)
     path[:, depth] = jnp.zeros((segs,) + path.shape[2:], path.dtype)
     step = functools.partial(
         bwd_step, depth, slots, bias, q_ref, kv_ref, o_ref, do_ref, lse_ref, dq_ref, path, p_scr, d_scr
     )
-    early = segs * PAIRS * 3 // 5
-    lax.fori_loop(0, early, step, 0)
+    count = segs * PAIRS
+    cuts = (0, count * 8 // 20, count * 14 // 20, count)
+    scatter.offer(1)
+    lax.fori_loop(cuts[0], cuts[1], step, 0)
     scatter.step(0)
-    lax.fori_loop(early, segs * PAIRS, step, 0)
+    scatter.offer(2)
+    lax.fori_loop(cuts[1], cuts[2], step, 0)
+    if scatter.length > 2:
+        scatter.step(1)
+    scatter.offer(3)
+    lax.fori_loop(cuts[2], cuts[3], step, 0)
     lax.fori_loop(0, group.shape[0], functools.partial(bwd_collect, inv, path, group), 0)
     sends = Sends()
-    for away, other in enumerate(others):
-        target = lax.rem(member + away + 1, TREE_DEVS)
+    side = member % 2
+    for turn, slot in ((0, 1 - side), (1, side)):
+        owner = (across - side + slot) % TREE_DEVS
         sends.start(
             None,
-            group.at[pl.ds(target * segs, segs)],
-            guest.at[away],
-            kv_sems.at[0, away],
-            kv_sems.at[1, away],
-            {"shard": other},
+            group.at[pl.ds(owner * segs, segs)],
+            guest.at[slot],
+            kv_sems.at[0, turn],
+            kv_sems.at[1, turn],
+            {"shard": across},
         )
-    for turn in range(1, scatter.length):
+
+    def join(mine, slot, extra, target):
+        def one(seg, c):
+            for col in range(0, 2 * KVH * HD, 256):
+                total = group[mine * segs + seg, :, col : col + 256].astype(jnp.float32)
+                total = total + guest[slot, seg, :, col : col + 256].astype(jnp.float32)
+                if extra is not None:
+                    total = total + extra[seg, :, col : col + 256].astype(jnp.float32)
+                target[seg, :, col : col + 256] = total.astype(target.dtype)
+            return c
+
+        lax.fori_loop(0, segs, one, 0)
+
+    received(None, guest.at[1 - side], kv_sems.at[0, 0], kv_sems.at[1, 0], {"shard": across})
+    join(twin % TREE_DEVS, 1 - side, None, passing)
+    sends.start(None, passing, landed, kv_sems.at[0, 2], kv_sems.at[1, 2], {"shard": twin})
+    for turn in range(2, scatter.length - 1):
+        scatter.offer(turn + 2)
         scatter.step(turn)
-    for away in range(TREE_DEVS - 1):
-        source = first + lax.rem(member + TREE_DEVS - 1 - away, TREE_DEVS)
-        received(None, guest.at[away], kv_sems.at[0, away], kv_sems.at[1, away], {"shard": source})
-
-    def join(seg, c):
-        for col in range(0, 2 * KVH * HD, 256):
-            total = group[member * segs + seg, :, col : col + 256].astype(jnp.float32)
-            for away in range(TREE_DEVS - 1):
-                total = total + guest[away, seg, :, col : col + 256].astype(jnp.float32)
-            dkv_ref[seg, :, col : col + 256] = total.astype(dkv_ref.dtype)
-        return c
-
-    lax.fori_loop(0, segs, join, 0)
+    received(None, guest.at[side], kv_sems.at[0, 1], kv_sems.at[1, 1], {"shard": across})
+    received(None, landed, kv_sems.at[0, 2], kv_sems.at[1, 2], {"shard": twin})
+    join(member, side, landed, dkv_ref)
     scatter.finish((gu_out, dn_out))
     sends.drain()
     scatter.sends.drain()
@@ -871,7 +902,9 @@
             pltpu.VMEM((depth * SEG, 6 * SEG), jnp.bfloat16),
             pltpu.VMEM((depth * SEG, 6 * SEG), jnp.bfloat16),
             pltpu.VMEM(kv.shape, jnp.bfloat16),
-            pltpu.VMEM((TREE_DEVS - 1,) + own_kv, jnp.bfloat16),
+            pltpu.VMEM((2,) + own_kv, jnp.bfloat16),
+            pltpu.VMEM(own_kv, jnp.bfloat16),
+            pltpu.VMEM(own_kv, jnp.bfloat16),
             pltpu.VMEM((4,) + gu_block, jnp.bfloat16),
             pltpu.VMEM((4,) + dn_block, jnp.bfloat16),
             pltpu.VMEM(gu_block, jnp.bfloat16),
@@ -914,11 +947,6 @@
     greet(line_neighbours(shards) + rep_neighbours())
     sends = Sends()
     length = shards // 2
-    order = []
-    for step in range(length):
-        for target in (length - 1 - step, step):
-            if target not in order:
-                order.append(target)
     side = lax.axis_index("shard") % 2
 
     def columns(n, ref, which):
@@ -927,18 +955,6 @@
             return ref
         return ref.at[:, :, pl.ds(pl.multiple_of(which * width, LANES), width)]
 
-    for turn in (1 - side, side):
-        for target in order:
-            block = 2 * target + turn
-            for n in range(arrays):
-                sends.start(
-                    None,
-                    columns(n, grads[n].at[block], 1 - half),
-                    core_bufs[n].at[block],
-                    core_sems.at[0, block, n],
-                    core_sems.at[1, block, n],
-                    {"rep": near},
-                )
     experts = pieces // 2
     size = shares[0].shape[0]
 
@@ -971,8 +987,22 @@
         loads,
         ready,
     )
-    scatter.begin()
-    for turn in range(scatter.length):
+    for turn in range(length):
+        for which in (1 - side, side):
+            block = 2 * scatter.pick(turn) + which
+            for n in range(arrays):
+                sends.start(
+                    None,
+                    columns(n, grads[n].at[block], 1 - half),
+                    core_bufs[n].at[block],
+                    core_sems.at[0, block, n],
+                    core_sems.at[1, block, n],
+                    {"rep": near},
+                )
+    scatter.offer(0)
+    scatter.offer(1)
+    for turn in range(scatter.length - 1):
+        scatter.offer(turn + 2)
         scatter.step(turn)
     scatter.finish(share_bufs)
     for n in range(arrays):
@@ -1085,9 +1115,9 @@
 
 
 def expert_forward(rows, gates, w_gate_up, w_down, upstream):
-    gate_up = jnp.einsum("td,edf->etf", rows, w_gate_up, preferred_element_type=jnp.float32)
-    gate_part = gate_up[..., :FF]
-    up_part = gate_up[..., FF:]
+    gate_up = jnp.einsum("td,edf->etf", rows, w_gate_up, preferred_element_type=jnp.bfloat16)
+    gate_part = gate_up[..., :FF].astype(jnp.float32)
+    up_part = gate_up[..., FF:].astype(jnp.float32)
     sig_gate = jax.nn.sigmoid(gate_part)
     hidden = gate_part * sig_gate * up_part
     gated = (hidden * gates).astype(jnp.bfloat16)
@@ -1136,6 +1166,7 @@
     rep_count = lax.axis_size("rep")
     own_experts = E // rep_count
     first_expert = rep_index * own_experts
+    half = own_experts // 2
     padding = jnp.zeros((norm_gains.shape[1], LANES - E - 2), jnp.bfloat16)
     small = jnp.concatenate([router_weight, norm_gains.T, padding], axis=1)
     w_qkv, small = gather_weights(qkv_weight, small, shard_count)
@@ -1143,7 +1174,6 @@
     small = small.reshape(D, LANES)
     w_router = small[:, :E]
     gains = small[:, E : E + 2].T
-    half = own_experts // 2
     gain_first = gains[0].astype(jnp.float32)
     gain_second = gains[1].astype(jnp.float32)
     token_values = tokens.astype(jnp.float32)
@@ -1151,6 +1181,10 @@
     act_first = normed_first.astype(jnp.bfloat16)
     projected = jnp.dot(act_first, w_qkv, preferred_element_type=jnp.float32)
     queries = projected[:, :width_q].astype(jnp.bfloat16)
+    w_gate_up_early = lax.all_gather(
+        lax.dynamic_slice_in_dim(gate_up_weight, first_expert, half - 1), "shard", axis=1, tiled=True
+    )
+    queries, w_gate_up_early = lax.optimization_barrier((queries, w_gate_up_early))
     own_kv = projected[:, width_q:].astype(jnp.bfloat16).reshape(seg_dev, SEG, 2 * width_kv)
     bias = jnp.where(path_alive, 0.0, NEG).astype(jnp.float32)
     attended, log_totals, group_kv, w_gate_up, w_down, w_out, cot_all = attend_gather(
@@ -1165,7 +1199,7 @@
         depth,
         shard_count,
         rep_count,
-        half,
+        1,
     )
     gate_up_late, down_late, attended = lax.optimization_barrier(
         (
@@ -1176,7 +1210,7 @@
     )
     w_gate_up_late = lax.all_gather(gate_up_late, "shard", axis=1, tiled=True)
     w_down_late = lax.all_gather(down_late, "shard", axis=1, tiled=True)
-    w_gate_up = w_gate_up.reshape(half, D, -1)
+    w_gate_up = jnp.concatenate([w_gate_up_early, w_gate_up.reshape(1, D, -1)], axis=0)
     w_down = w_down.reshape(half, FF, D)
     w_out = w_out.reshape(H * HD, D)
     cot_all = cot_all.reshape(-1, D)
@@ -1238,11 +1272,9 @@
     attended_grad = lax.dot_general(
         branch_grad, w_out, (((1,), (1,)), ((), ())), preferred_element_type=jnp.float32
     ).astype(jnp.bfloat16)
-    attended_grad, gate_up_early, down_early, mix_part = lax.optimization_barrier(
-        (attended_grad, gate_up_early, down_early, mix_part.astype(jnp.bfloat16))
-    )
-    mixture = lax.psum_scatter(mix_part, "rep", scatter_dimension=0, tiled=True)
-    block_out = (residual + mixture.astype(jnp.float32)).astype(jnp.bfloat16)
+    attended_grad, gate_up_early, down_early = lax.optimization_barrier(
+        (attended_grad, gate_up_early, down_early)
+    )
     query_grad, own_grad, gate_up_share, down_share = attend_back(
         path_slots,
         bias,
@@ -1257,6 +1289,9 @@
         depth,
         shard_count,
     )
+    mix_part, query_grad = lax.optimization_barrier((mix_part.astype(jnp.bfloat16), query_grad))
+    mixture = lax.psum_scatter(mix_part, "rep", scatter_dimension=0, tiled=True)
+    block_out = (residual + mixture.astype(jnp.float32)).astype(jnp.bfloat16)
     projected_grad = jnp.concatenate(
         [query_grad, own_grad.reshape(token_count, 2 * width_kv)], axis=1
     )

time: 1170 us -> 1060 us (0.906); the launches traced: 1140 us -> 1050 us
  Pallas kernels: 700 us -> 626 us
  waiting for transfers between devices: 33.7 us -> 6.5 us
    pallas_call x1, Pallas kernels: 191 us -> 160 us  [attend_gather(): pl.pallas_call(functools.partial(attend_gather_kernel, depth, shards, exp...]
    reduce_scatter x1, waiting for transfers between devices: 32.9 us -> 6.39 us  [shards(): lax.psum_scatter(first_half[3], 'shard', scatter_dimension=0, tiled=False)]
    pallas_call x1, Pallas kernels: 201 us -> 176 us  [attend_back(): pl.pallas_call(functools.partial(back_kernel, depth, shards), out_shape=o...]
    pallas_call x1, Pallas kernels: 137 us -> 119 us  [finish_grads(): pl.pallas_call(functools.partial(finish_kernel, shards, arrays, 2 * parts...]
  transfers between devices with their start and end apart: 5 -> 6, of which waited for: 1 -> 1; matrix products, arithmetic and copies ran while one was open for 30% -> 36% of each run, Pallas kernels for 39% -> 28%
where the time goes in v5:
time: 1060 us; the launch traced here: 1050 us
  Pallas kernels  626 us (59%)
  matrix products  292 us (28%)
  local copies, waits for them, and re-layouts  66.9 us (6%)
  other arithmetic  34.2 us (3%)
  between operations  15.5 us (1%)
    pallas_call x1, Pallas kernels, attend_back(): pl.pallas_call(functools.partial(back_kernel, depth, shards), out_shape=o...  176 us
    pallas_call x1, Pallas kernels, attend_gather(): pl.pallas_call(functools.partial(attend_gather_kernel, depth, shards, exp...  160 us
    pallas_call x1, Pallas kernels, finish_grads(): pl.pallas_call(functools.partial(finish_kernel, shards, arrays, 2 * parts...  119 us
    pallas_call x1, Pallas kernels, share_rows(): pl.pallas_call(functools.partial(share_kernel, chunks), out_shape=[jax.Sh...  63 us
    pallas_call x1, Pallas kernels, gather_weights(): pl.pallas_call(functools.partial(weights_kernel, shards), out_shape=[jax....  60.7 us
    pallas_call x1, Pallas kernels, join_reps(): pl.pallas_call(join_kernel, out_shape=jax.ShapeDtypeStruct(block, jnp.flo...  47.4 us
    dot_general x2, matrix products, expert_forward(): jnp.einsum('etf,edf->td', row_grads, w_gate_up, preferred_element_type=jn...  46.2 us
    dot_general x2, matrix products, expert_forward(): jnp.einsum('td,edf->etf', rows, w_gate_up, preferred_element_type=jnp.bfl...  45.6 us
  transfers between devices with their start and end apart: 6, of which 1 were waited for; matrix products, arithmetic and copies ran while one was open for 36% of the time, Pallas kernels for 28%

profile of v5, /device:TPU:9, one launch (start us, length us, event | category | flops | bytes accessed | tf_op | source)
XLA Modules:
  0.0 1048.0 jit_solution(461993862246686812)
XLA Ops:
  7.2 1.9 constant_dynamic-slice_fusion
  9.3 0.8 copy.195
  10.1 0.8 copy.196
  11.5 0.7 maximum_maximum_fusion.1.small
  12.2 60.7 %shard_map.170 = (bf16[8,192,2560]{2,1,0:T(8,128)(2,1)}, bf16[8,192,128]{2,1,0:T(8,128)(2,1)}) custom-call(bf16[192,2560]{1,0:T(8,128)(2,1)} %qkv.1, bf16[192,128]{1,0:T(8,128)(2,1)} %maximum_maximum_fusion.1.small), custom_call_target="tpu_custom_call" | custom-call | bytes 200000000 | tf_op jit(solution)/shard_map/pallas_call | solution.py:357
  72.9 1.2 slice.62
  74.3 2.0 fusion.24
  76.9 8.9 convolution_convert_fusion.2
  86.0 1.4 slice.64.q_ref
  91.8 2.1 constant_dynamic-slice_fusion.3
  93.9 1.8 constant_dynamic-slice_fusion.2
  95.7 159.9 %shard_map.171 = (bf16[640,1536]{1,0:T(8,128)(2,1)S(1)}, f32[20,8,768]{2,1,0:T(8,128)S(1)}, bf16[20,128,1024]{2,1,0:T(8,128)(2,1)}, bf16[1,8,192,1024]{3,2,1,0:T...) custom-call(s32[5,10]{1,0:T(8,128)S(1)} %stack.73.slots, ...), custom_call_target="tpu_custom_call" | custom-call | flops 20000000000 | bytes 700000000 | tf_op jit(solution)/shard_map/pallas_call | solution.py:487
  255.6 1.3 copy-done.14
  256.9 0.8 copy-done.17
  258.6 4.8 copy.198
  263.4 4.6 copy.199
  268.1 6.3 multiply_reduce_fusion.2
  275.0 1.4 copy-done.18
  278.3 63.0 %shard_map.172 = (bf16[4,640,1536]{2,1,0:T(8,128)(2,1)}, f32[4,16,640]{2,1,0:T(8,128)}) custom-call(bf16[640,1536]{1,0:T(8,128)(2,1)} %copy-done.20, f32[16,640]{1,0:T(8,128)} %bitcast.169), custom_call_target="tpu_custom_call" | custom-call | bytes 160000000 | tf_op jit(solution)/shard_map/pallas_call | solution.py:526
  341.4 0.9 dynamic-slice_bitcast_fusion
  343.4 22.8 %convolution_bitcast_fusion.3 = bf16[2,2560,1024]{1,2,0:T(8,128)(2,1)} fusion(bf16[2560,1536,1]{1,0,2:T(8,128)(2,1)} %bitcast.193, bf16[1,1536,1024]{1,2,0:T(8,128)(2,1)} %copy.199, bf16[1,1536,1024]{1,2,0:T(8,128)(2,1)} %copy.198), kind=kOutput, calls=%fused_computation.57 | convolution fusion | flops 16109273088 | bytes 24641536 | tf_op jit(solution)/shard_map/td,edf->etf/dot_general | solution.py:1118
  366.2 18.2 %fusion.4 = (bf16[2,2560,512]{1,2,0:T(8,128)(2,1)S(1)}, bf16[2,2560,512]{1,2,0:T(8,128)(2,1)}, f32[2,2560]{1,0:T(2,128)}) fusion(f32[2,2560]{1,0:T(2,128)S(1)} %bitcast.175, bf16[2,2560,1024]{1,2,0:T(8,128)(2,1)} %convolution_bitcast_fusion.3, bf16[2,512,1536]{2,1,0:T(8,128)(2,1)S(1)} %bitcast.207, bf16[2560,1536,1]{1,0,2:T(8,128)(2,1)} %bitcast.197), kind=kOutput, calls=%fused_computation.21 | convolution fusion | flops 8105487360 | bytes 32022528 | tf_op jit(solution)/shard_map/td,efd->etf/dot_general | solution.py:1125
  384.4 16.3 %convolution_convert_fusion.4 = bf16[2,512,1536]{2,1,0:T(8,128)(2,1)S(1)} fusion(bf16[2560,1536,1]{1,0,2:T(8,128)(2,1)} %bitcast.198, f32[2,2560]{1,0:T(2,128)S(1)} %bitcast.176, bf16[2,2560,1024]{1,2,0:T(8,128)(2,1)} %convolution_bitcast_fusion.3), kind=kOutput, calls=%fused_computation.80 | convolution fusion | flops 8078229504 | bytes 21516288 | tf_op jit(solution)/shard_map/etf,td->efd/dot_general | solution.py:1131
  400.7 1.9 copy.227
  402.6 18.9 %convert_bitcast_fusion.1 = bf16[2,1536,1024]{1,2,0:T(8,128)(2,1)} fusion(bf16[2560,1536,1]{1,0,2:T(8,128)(2,1)S(1)} %bitcast.196, bf16[2,2560,512]{1,2,0:T(8,128)(2,1)} %get-tuple-element.148, bf16[2,2560,512]{1,2,0:T(8,128)(2,1)S(1)} %get-tuple-element.147), kind=kOutput, calls=%fused_computation.62 | convolution fusion | flops 16130244608 | bytes 24641536 | tf_op jit(solution)/shard_map/td,etf->edf/dot_general | solution.py:1132
  421.5 8.7 copy.203
  430.2 7.1 copy.226
  437.3 1.4 copy-done.57
  438.7 20.8 %convolution_bitcast_fusion = f32[2560,1536]{1,0:T(8,128)} fusion(bf16[2,2560,512]{1,2,0:T(8,128)(2,1)} %get-tuple-element.148, bf16[2,2560,512]{1,2,0:T(8,128)(2,1)S(1)} %copy-done.57, bf16[1,1536,1024]{1,2,0:T(8,128)(2,1)S(1)} %copy-done.31, bf16[1,1536,1024]{1,2,0:T(8,128)(2,1)S(1)} %copy-done.30), kind=kOutput, calls=%fused_computation.16 | convolution fusion | flops 16130244608 | bytes 32505856 | tf_op jit(solution)/shard_map/etf,edf->td/dot_general | solution.py:1133
  459.5 15.5 %convolution_bitcast_fusion.1 = f32[2560,1536]{1,0:T(8,128)} fusion(bf16[2,512,1536]{2,1,0:T(8,128)(2,1)S(1)} %bitcast.208, f32[2,2560]{1,0:T(2,128)S(1)} %bitcast.177, bf16[2,2560,1024]{1,2,0:T(8,128)(2,1)} %convolution_bitcast_fusion.3), kind=kOutput, calls=%fused_computation.17 | convolution fusion | flops 8076656640 | bytes 29380608 | tf_op jit(solution)/shard_map/etf,efd->td/dot_general | solution.py:1124
  475.1 22.8 %convolution_bitcast_fusion.2 = bf16[2,2560,1024]{1,2,0:T(8,128)(2,1)} fusion(bf16[2,1536,1024]{2,1,0:T(8,128)(2,1)} %all-gather.7.cloned.1.call-done, bf16[2560,1536,1]{1,0,2:T(8,128)(2,1)} %bitcast.194), kind=kOutput, calls=%fused_computation.56 | convolution fusion | flops 16106127360 | bytes 24641536 | tf_op jit(solution)/shard_map/td,edf->etf/dot_general | solution.py:1118
  497.9 18.9 %fusion.7 = (bf16[2,2560,512]{1,2,0:T(8,128)(2,1)}, bf16[2,2560,512]{1,2,0:T(8,128)(2,1)}, f32[2,2560]{1,0:T(2,128)S(1)}) fusion(f32[2,2560]{1,0:T(2,128)S(1)} %bitcast.172, bf16[2,2560,1024]{1,2,0:T(8,128)(2,1)} %convolution_bitcast_fusion.2, bf16[2,512,1536]{2,1,0:T(8,128)(2,1)S(1)} %copy-done.51, bf16[2560,1536,1]{1,0,2:T(8,128)(2,1)} %bitcast.199), kind=kOutput, calls=%fused_computation.24 | convolution fusion | flops 8105487360 | bytes 32022528 | tf_op jit(solution)/shard_map/td,efd->etf/dot_general | solution.py:1125
  516.8 22.8 %convert_bitcast_fusion = bf16[2,1536,1024]{1,2,0:T(8,128)(2,1)} fusion(bf16[2560,1536,1]{1,0,2:T(8,128)(2,1)} %bitcast.195, bf16[2,2560,512]{1,2,0:T(8,128)(2,1)} %get-tuple-element.146, bf16[2,2560,512]{1,2,0:T(8,128)(2,1)} %get-tuple-element.145), kind=kOutput, calls=%fused_computation.61 | convolution fusion | flops 16130244608 | bytes 24641536 | tf_op jit(solution)/shard_map/td,etf->edf/dot_general | solution.py:1132
  539.6 8.7 copy.211
  548.4 25.4 %fusion = bf16[2560,1536]{1,0:T(8,128)(2,1)} fusion(f32[2560,1536]{1,0:T(8,128)} %convolution_bitcast_fusion, bf16[2,1536,1024]{2,1,0:T(8,128)(2,1)} %all-gather.7.cloned.1.call-done, bf16[2,2560,512]{1,2,0:T(8,128)(2,1)} %get-tuple-element.146, bf16[2,2560,512]{1,2,0:T(8,128)(2,1)} %get-tuple-element.145), kind=kOutput, calls=%fused_computation.9 | convolution fusion | flops 16134963200 | bytes 40370176 | tf_op jit(solution)/shard_map/etf,edf->td/dot_general | solution.py:1133
  573.8 3.2 copy-done.3
  577.1 47.4 %shard_map.173 = f32[640,1536]{1,0:T(8,128)S(1)} custom-call(bf16[4,640,1536]{2,1,0:T(8,128)(2,1)S(1)} %bitcast.153), custom_call_target="tpu_custom_call" | custom-call | bytes 160000000 | tf_op jit(solution)/shard_map/pallas_call | solution.py:598
  624.5 1.9 copy-done.2
  626.4 5.7 all-gather
  632.3 6.6 multiply_reduce_fusion
  639.0 1.0 subtract_add_fusion
  640.1 4.7 convolution_convert_fusion.5.do_ref
  644.8 13.5 %convolution_convert_fusion.3 = bf16[2,512,1536]{2,1,0:T(8,128)(2,1)} fusion(bf16[2560,1536,1]{1,0,2:T(8,128)(2,1)S(1)} %bitcast.202, f32[2,2560]{1,0:T(2,128)S(1)} %bitcast.173, bf16[2,2560,1024]{1,2,0:T(8,128)(2,1)} %convolution_bitcast_fusion.2), kind=kOutput, calls=%fused_computation.79 | convolution fusion | flops 8078229504 | bytes 21516288 | tf_op jit(solution)/shard_map/etf,td->efd/dot_general | solution.py:1131
  658.3 17.1 %fusion.1 = bf16[2560,1536]{1,0:T(8,128)(2,1)} fusion(f32[2560,1536]{1,0:T(8,128)} %convolution_bitcast_fusion.1, bf16[2,512,1536]{2,1,0:T(8,128)(2,1)S(1)} %copy-done.52, f32[2,2560]{1,0:T(2,128)S(1)} %bitcast.174, bf16[2,2560,1024]{1,2,0:T(8,128)(2,1)} %convolution_bitcast_fusion.2), kind=kOutput, calls=%fused_computation.11 | convolution fusion | flops 8084520960 | bytes 37244928 | tf_op jit(solution)/shard_map/etf,efd->td/dot_general | solution.py:1124
  675.4 6.4 reduce-scatter.4.cloned.1.call-done
  681.8 176.4 %shard_map.174 = (bf16[640,1536]{1,0:T(8,128)(2,1)}, bf16[5,128,1024]{2,1,0:T(8,128)(2,1)}, bf16[2,192,1024]{2,1,0:T(8,128)(2,1)}, bf16[2,64,1536]{2,1,0:T(8,128...) custom-call(s32[5,10]{1,0:T(8,128)} %copy-done.11, ...), custom_call_target="tpu_custom_call" | custom-call | flops 49999998976 | bytes 700000000 | tf_op jit(solution)/shard_map/pallas_call | solution.py:895
  858.3 2.6 convolution_convert_fusion.6
  861.1 0.7 concatenate.48
  861.9 8.0 convolution_convert_fusion.1
  870.0 9.9 fusion.32
  879.9 0.7 concatenate.47
  881.0 11.7 %convolution_convert_fusion = bf16[1536,2560]{1,0:T(8,128)(2,1)} fusion(bf16[640,1024]{1,0:T(8,128)(2,1)} %bitcast.210, bf16[640,1536]{1,0:T(8,128)(2,1)} %get-tuple-element.71, bf16[640,1536]{1,0:T(8,128)(2,1)S(1)} %copy-done.25, f32[1536]{0:T(1024)S(1)} %copy-done.40, f32[640]{0:T(1024)S(1)} %copy-done.45), kind=kOutput, calls=%fused_computation.18 | convolution fusion | flops 5047582720 | bytes 13115904 | tf_op jit(solution)/shard_map/dot_general | solution.py:1298
  892.7 118.7 %shard_map.175 = (bf16[1,192,2560]{2,1,0:T(8,128)(2,1)S(1)}, bf16[1,192,1536]{2,1,0:T(8,128)(2,1)S(1)}, bf16[1,192,128]{2,1,0:T(8,128)(2,1)S(1)}, bf16[4,4,192,1...) custom-call(bf16[8,1,192,2560]{3,2,1,0:T(8,128)(2,1)} %bitcast.160, ...), custom_call_target="tpu_custom_call" | custom-call | bytes 400000000 | tf_op jit(solution)/shard_map/pallas_call | solution.py:1043
  1011.4 0.9 copy-done.4
  1012.3 0.8 copy-done.8
  1013.3 0.7 copy.216
  1013.9 0.7 copy.215
  1014.6 2.2 bitcast_convert_fusion.3
  1016.8 9.2 bitcast_convert_fusion
  1026.0 1.5 bitcast_convert_fusion.2
  1027.5 4.3 bitcast_convert_fusion.1
  1031.8 1.3 copy-done.26
  1033.1 2.9 fusion.29
  1036.0 4.6 add_convert_fusion
  (210 shorter events, 11.5 us)
Async XLA Ops:
  7.2 80.4 %copy-start = (s32[8,20]{1,0:T(8,128)S(1)}, s32[8,20]{1,0:T(8,128)}, u32[]{:S(2)}) copy-start(s32[8,20]{1,0:T(8,128)} %param.20) | copy-start | bytes 1924
  7.2 69.7 %copy-start.23 = (bf16[640,1536]{1,0:T(8,128)(2,1)S(1)}, bf16[640,1536]{1,0:T(8,128)(2,1)}, u32[]{:S(2)}) copy-start(bf16[640,1536]{1,0:T(8,128)(2,1)} %param.11) | copy-start | bytes 5898244
  7.2 88.5 %all-gather.5.cloned.1.call-start = ((), (), s32[]{:S(2)}) async-start(), calls=%async_computation.3 | async-start | bytes 3538944 | tf_op jit(solution)/shard_map/all_gather | solution.py:1184
  9.2 465.9 %all-gather.9.cloned.1.call-start = ((), (), s32[]{:S(2)}) async-start(), calls=%async_computation.5 | async-start | bytes 3538944 | tf_op jit(solution)/shard_map/all_gather | solution.py:1212
  74.3 11.6 %copy-start.39 = (f32[1536]{0:T(1024)}, f32[1536]{0:T(1024)S(1)}, u32[]{:S(2)}) copy-start(f32[1536]{0:T(1024)S(1)} %get-tuple-element.127) | copy-start | bytes 18436
  74.3 200.7 %copy-start.34 = (f32[1536]{0:T(1024)}, f32[1536]{0:T(1024)S(1)}, u32[]{:S(2)}) copy-start(f32[1536]{0:T(1024)S(1)} %get-tuple-element.126) | copy-start | bytes 18436
  76.9 8.9 copy-start.44
  85.9 1.6 copy-start.49
  85.9 9.8 copy-start.13
  91.8 166.0 %copy-start.11 = (s32[5,10]{1,0:T(8,128)}, s32[5,10]{1,0:T(8,128)S(1)}, u32[]{:S(2)}) copy-start(s32[5,10]{1,0:T(8,128)S(1)} %stack.73.slots) | copy-start | bytes 604
  93.9 161.7 %copy-start.12 = (f32[5,10]{1,0:T(8,128)}, f32[5,10]{1,0:T(8,128)S(1)}, u32[]{:S(2)}) copy-start(f32[5,10]{1,0:T(8,128)S(1)} %broadcast_select_fusion.bias) | copy-start | bytes 604
  255.6 1.3 copy-start.14
  257.7 217.3 %all-gather.7.cloned.1.call-start = ((), (), s32[]{:S(2)}) async-start(), calls=%async_computation.4 | async-start | bytes 7077888 | tf_op jit(solution)/shard_map/all_gather | solution.py:1211
  258.6 9.5 copy-start.15
  274.4 2.1 copy-start.18
  274.4 2.4 copy-start.28
  274.4 3.1 copy-start.36
  275.0 66.3 %copy-start.37 = (f32[640]{0:T(1024)}, f32[640]{0:T(1024)S(1)}, u32[]{:S(2)}) copy-start(f32[640]{0:T(1024)S(1)} %get-tuple-element.156) | copy-start | bytes 7684
  276.9 1.4 copy-start.20
  342.9 332.5 %reduce-scatter.6.cloned.1.call-start = ((), (), s32[]{:S(2)}) async-start(), calls=%async_computation.7 | async-start | bytes 3538944 | tf_op jit(solution)/shard_map/reduce_scatter | solution.py:1243
  343.4 22.8 %copy-start.53 = (bf16[2,8,64,1536]{3,2,1,0:T(8,128)(2,1)S(1)}, bf16[2,8,64,1536]{3,2,1,0:T(8,128)(2,1)}, u32[]{:S(2)}) copy-start(bf16[2,8,64,1536]{3,2,1,0:T(8,128)(2,1)} %get-tuple-element.55) | copy-start | bytes 9437188
  384.4 18.2 %copy-start.56 = (bf16[2,2560,512]{1,2,0:T(8,128)(2,1)}, bf16[2,2560,512]{1,2,0:T(8,128)(2,1)S(1)}, u32[]{:S(2)}) copy-start(bf16[2,2560,512]{1,2,0:T(8,128)(2,1)S(1)} %get-tuple-element.147) | copy-start | bytes 15728644
  384.4 18.2 %copy-start.50 = (bf16[4,640,1536]{2,1,0:T(8,128)(2,1)S(1)}, bf16[4,640,1536]{2,1,0:T(8,128)(2,1)}, u32[]{:S(2)}) copy-start(bf16[4,640,1536]{2,1,0:T(8,128)(2,1)} %get-tuple-element.53) | copy-start | bytes 23592964
  430.2 7.1 copy-start.30
  430.2 7.1 copy-start.31
  430.2 8.5 copy-start.57
  475.1 22.9 %copy-start.41 = (f32[2,4,640]{2,0,1:T(2,128)S(1)}, f32[2,4,640]{2,0,1:T(2,128)}, u32[]{:S(2)}) copy-start(f32[2,4,640]{2,0,1:T(2,128)} %get-tuple-element.151) | copy-start | bytes 61444
  475.1 206.7 %reduce-scatter.4.cloned.1.call-start = ((), (), s32[]{:S(2)}) async-start(), calls=%async_computation.6 | async-start | bytes 7077888 | tf_op jit(solution)/shard_map/reduce_scatter | solution.py:1242
  475.1 22.8 %copy-start.51 = (bf16[2,512,1536]{2,1,0:T(8,128)(2,1)S(1)}, bf16[2,512,1536]{2,1,0:T(8,128)(2,1)}, u32[]{:S(2)}) copy-start(bf16[2,512,1536]{2,1,0:T(8,128)(2,1)} %all-gather.9.cloned.1.call-done) | copy-start | bytes 9437188
  548.3 487.7 %reduce-scatter.8.cloned.1.call-start = ((), (), s32[]{:S(2)}) async-start(), calls=%async_computation.8 | async-start | bytes 9830400 | tf_op jit(solution)/shard_map/reduce_scatter | solution.py:1293
  573.8 3.2 copy-start.3
  577.1 49.3 %copy-start.42 = (f32[2,2560]{1,0:T(2,128)S(1)}, f32[2,2560]{1,0:T(2,128)}, u32[]{:S(2)}) copy-start(f32[2,2560]{1,0:T(2,128)} %get-tuple-element.64) | copy-start | bytes 61444
  577.1 55.2 %copy-start.33 = (f32[640,16]{0,1:T(8,128)S(1)}, f32[640,16]{0,1:T(8,128)}, u32[]{:S(2)}) copy-start(f32[640,16]{0,1:T(8,128)} %select_reduce_fusion) | copy-start | bytes 122884
  577.1 55.2 %copy-start.29 = (bf16[8,192,128]{2,1,0:T(8,128)(2,1)S(1)}, bf16[8,192,128]{2,1,0:T(8,128)(2,1)}, u32[]{:S(2)}) copy-start(bf16[8,192,128]{2,1,0:T(8,128)(2,1)} %get-tuple-element.45) | copy-start | bytes 1179652
  577.1 55.2 %copy-start.35 = (f32[1536]{0:T(1024)S(1)}, f32[1536]{0:T(1024)}, u32[]{:S(2)}) copy-start(f32[1536]{0:T(1024)} %copy-done.34) | copy-start | bytes 18436
  577.1 55.2 %copy-start.38 = (f32[640]{0:T(1024)S(1)}, f32[640]{0:T(1024)}, u32[]{:S(2)}) copy-start(f32[640]{0:T(1024)} %copy-done.37) | copy-start | bytes 7684
  624.5 1.9 copy-start.2
  632.3 6.6 copy-start.19
  632.3 6.6 copy-start.32
  632.3 6.6 copy-start.46
  632.3 7.7 slice-start.2
  638.9 1.1 slice-start.3
  639.0 5.8 slice-start
  640.0 4.7 copy-start.21
  640.1 4.7 slice-start.1
  644.8 13.5 %copy-start.52 = (bf16[2,512,1536]{2,1,0:T(8,128)(2,1)S(1)}, bf16[2,512,1536]{2,1,0:T(8,128)(2,1)}, u32[]{:S(2)}) copy-start(bf16[2,512,1536]{2,1,0:T(8,128)(2,1)} %all-gather.9.cloned.1.call-done) | copy-start | bytes 9437188
  858.3 3.5 copy-start.16
  861.8 8.1 copy-start.24
  861.8 8.1 copy-start.40
  861.8 8.1 copy-start.45
  861.8 8.1 copy-start.54
  861.9 8.1 copy-start.55
  869.9 10.7 %copy-start.48 = (bf16[128]{0:T(256)(128)(2,1)S(1)}, bf16[128]{0:T(256)(128)(2,1)}, u32[]{:S(2)}) copy-start(bf16[128]{0:T(256)(128)(2,1)} %copy-done.47) | copy-start | bytes 772
  870.0 11.1 %copy-start.25 = (bf16[640,1536]{1,0:T(8,128)(2,1)S(1)}, bf16[640,1536]{1,0:T(8,128)(2,1)}, u32[]{:S(2)}) copy-start(bf16[640,1536]{1,0:T(8,128)(2,1)} %param.11) | copy-start | bytes 5898244
  881.0 11.7 %copy-start.6 = (bf16[1,2,192,1024]{3,2,1,0:T(8,128)(2,1)S(1)}, bf16[1,2,192,1024]{3,2,1,0:T(8,128)(2,1)}, u32[]{:S(2)}) copy-start(bf16[1,2,192,1024]{3,2,1,0:T(8,128)(2,1)} %reduce-scatter.4.cloned.1.call-done) | copy-start | bytes 2359300
  881.0 11.7 %copy-start.7 = (bf16[2,192,1024]{2,1,0:T(8,128)(2,1)S(1)}, bf16[2,192,1024]{2,1,0:T(8,128)(2,1)}, u32[]{:S(2)}) copy-start(bf16[2,192,1024]{2,1,0:T(8,128)(2,1)} %get-tuple-element.74.refs_4_) | copy-start | bytes 2359300
  881.0 11.7 %copy-start.9 = (bf16[1,2,64,1536]{3,2,1,0:T(8,128)(2,1)S(1)}, bf16[1,2,64,1536]{3,2,1,0:T(8,128)(2,1)}, u32[]{:S(2)}) copy-start(bf16[1,2,64,1536]{3,2,1,0:T(8,128)(2,1)} %reduce-scatter.6.cloned.1.call-done) | copy-start | bytes 1179652
  881.0 11.7 %copy-start.10 = (bf16[2,64,1536]{2,1,0:T(8,128)(2,1)S(1)}, bf16[2,64,1536]{2,1,0:T(8,128)(2,1)}, u32[]{:S(2)}) copy-start(bf16[2,64,1536]{2,1,0:T(8,128)(2,1)} %get-tuple-element.76.refs_6_) | copy-start | bytes 1179652
  1016.8 9.2 copy-start.5
  1026.0 5.8 copy-start.27
  1027.5 4.3 copy-start.22
  1027.5 5.5 copy-start.26
  1027.5 5.5 copy-start.43
  1033.1 7.6 copy-start.1
  (4 other events, 3.1 us)
Sparse Core Ops, SparseCore 0:
  10.8 67.6 all-gather.4
  257.8 71.5 all-gather.8
  343.0 108.8 all-gather.6
  475.2 86.0 reduce-scatter.5
  564.7 117.0 reduce-scatter.3
  858.4 96.7 reduce-scatter.7

commit v6 on v5

--- a/solution.py
+++ b/solution.py
@@ -5,6 +5,7 @@
 import jax.experimental.pallas.tpu as pltpu
 import jax.numpy as jnp
 from jax import lax
+from jax.experimental.layout import Layout, with_layout_constraint
 from jax.sharding import PartitionSpec as P
 
 D = 1536
@@ -218,11 +219,6 @@
             self.sends.local(src, self.region(n, self.me), self.local_sem.at[n])
         self.forward(None, self.me, 0, True, True, self.sources)
 
-    def finish_local(self):
-        for cond, wait in self.sends.open[: len(self.sources)]:
-            wait()
-        self.sends.open = self.sends.open[len(self.sources) :]
-
     def step(self, step):
         for sems, cond, block, rising in (
             (self.up, self.spot - step >= 0, self.me - 2 * step, True),
@@ -329,7 +325,6 @@
         return small_all.at[block] if n == 1 else part_columns(qkv_all.at[block], owner, width)
 
     spread = RepSpread((0,), part, cross, core, relay)
-    spread.sources = None
     gather = LineGather(
         shards,
         (part_columns(qkv, rep, width), small),
@@ -341,8 +336,9 @@
         spread.arrived,
     )
     gather.begin()
-    gather.finish_local()
+    spread.sources = {0: part_columns(qkv, rep, width)}
     spread.arrived(None, gather.me, 0)
+    spread.sources = None
     for step in range(gather.length):
         if step:
             gather.step(step)
@@ -377,6 +373,7 @@
     dn_ref,
     out_ref,
     cot_ref,
+    early_ref,
     o_ref,
     lse_ref,
     kv_all,
@@ -388,6 +385,7 @@
     p_scr,
     kv_sems,
     cot_sem,
+    early_sem,
     up,
     down,
     pair,
@@ -416,11 +414,12 @@
     sends.start(None, kv_ref, own, kv_sems.at[0, 1], kv_sems.at[1, 1], {"shard": across})
     width = out_ref.shape[1] // lax.axis_size("rep")
     own_experts = gu_ref.shape[0] // lax.axis_size("rep")
+    early = early_ref.shape[0]
 
     def part(n, owner, block):
         if n == 2:
             return part_columns(out_all.at[block], owner, width)
-        return (gu_all, dn_all)[n].at[:, block]
+        return dn_all.at[:, block] if n else gu_all.at[pl.ds(early, experts), block]
 
     spread = RepSpread((2,), part, cross, core, relay)
     gather = LineGather(
@@ -440,11 +439,13 @@
     )
     gather.begin()
     sends.local(cot_ref, cot_all.at[rep], cot_sem)
+    sends.local(early_ref, gu_all.at[pl.ds(0, early)], early_sem)
     cot_spread = RepSpread((0,), lambda n, owner, block: cot_all.at[owner], cot_cross, cot_core, cot_relay)
     cot_spread.sources = (cot_ref,)
     cot_spread.arrived(None, 0, 0)
-    gather.finish_local()
+    spread.sources = {2: part_columns(out_ref, rep, width)}
     spread.arrived(None, me, 0)
+    spread.sources = None
     kv_all[pl.ds(member * seg_dev, seg_dev)] = kv_ref[...]
     theirs = kv_block(twin)
     received(None, theirs, kv_sems.at[0, 0], kv_sems.at[1, 0], {"shard": twin})
@@ -472,13 +473,13 @@
     sends.drain()
 
 
-def attend_gather(slots, bias, q, kv, gate_up, down, out, cotangent, depth, shards, reps, experts):
+def attend_gather(slots, bias, q, kv, gate_up, down, out, cotangent, early, depth, shards, reps, experts):
     tokens = q.shape[0]
     count = tokens // SEG * PAIRS
     shapes = [
         q.shape,
         (TREE_DEVS * kv.shape[0],) + kv.shape[1:],
-        (experts, shards) + gate_up.shape[1:],
+        (early.shape[0] + experts, shards) + gate_up.shape[1:],
         (down.shape[0] // reps // 2, shards) + down.shape[1:],
         (shards,) + out.shape,
         (reps,) + cotangent.shape,
@@ -487,12 +488,13 @@
     return pl.pallas_call(
         functools.partial(attend_gather_kernel, depth, shards, experts),
         out_shape=outs[:1] + [jax.ShapeDtypeStruct((count, 8, 6 * SEG), jnp.float32)] + outs[1:],
-        in_specs=[SMEM, SMEM, VMEM, VMEM] + [ANY] * 4,
+        in_specs=[SMEM, SMEM, VMEM, VMEM] + [ANY] * 3 + [VMEM] * 2,
         out_specs=[VMEM] * 3 + [ANY] * 4,
         scratch_shapes=[
             pltpu.VMEM((depth * SEG, 6 * SEG), jnp.float32),
             pltpu.VMEM((depth * SEG, 6 * SEG), jnp.bfloat16),
             pltpu.SemaphoreType.DMA((2, TREE_DEVS - 1)),
+            pltpu.SemaphoreType.DMA,
             pltpu.SemaphoreType.DMA,
         ]
         + line_sems(shards, 3)
@@ -502,7 +504,7 @@
         compiler_params=pltpu.CompilerParams(
             collective_id=2, has_side_effects=True, vmem_limit_bytes=48 * 2**20
         ),
-    )(slots, bias, q, kv, gate_up, down, out, cotangent)
+    )(slots, bias, q, kv, gate_up, down, out, cotangent, early)
 
 
 def share_kernel(chunks, rows_ref, gate_ref, rows_all, gate_all, own_sems, cross, core, relay):
@@ -529,11 +531,13 @@
             jax.ShapeDtypeStruct((reps,) + rows.shape, rows.dtype),
             jax.ShapeDtypeStruct((reps,) + gates.shape, gates.dtype),
         ],
-        in_specs=[ANY] * 2,
-        out_specs=[ANY] * 2,
+        in_specs=[VMEM] * 2,
+        out_specs=[VMEM] * 2,
         scratch_shapes=[pltpu.SemaphoreType.DMA((chunks + 1,))] + rep_sems(1, chunks + 1),
         cost_estimate=work(0, 1.6e8),
-        compiler_params=pltpu.CompilerParams(collective_id=6, has_side_effects=True),
+        compiler_params=pltpu.CompilerParams(
+            collective_id=6, has_side_effects=True, vmem_limit_bytes=32 * 2**20
+        ),
     )(rows, gates)
 
 
@@ -1130,6 +1134,7 @@
     row_grads = jnp.concatenate([gate_grad_part, up_grad_part], axis=-1).astype(jnp.bfloat16)
     down_grad = jnp.einsum("etf,td->efd", gated, upstream, preferred_element_type=jnp.float32)
     gate_up_grad = jnp.einsum("td,etf->edf", rows, row_grads, preferred_element_type=jnp.float32)
+    gate_up_grad = with_layout_constraint(gate_up_grad.astype(jnp.bfloat16), Layout((0, 1, 2)))
     act_part = jnp.einsum("etf,edf->td", row_grads, w_gate_up, preferred_element_type=jnp.float32)
     return (mix_part, gate_grad, act_part, gate_up_grad, down_grad)
 
@@ -1184,7 +1189,6 @@
     w_gate_up_early = lax.all_gather(
         lax.dynamic_slice_in_dim(gate_up_weight, first_expert, half - 1), "shard", axis=1, tiled=True
     )
-    queries, w_gate_up_early = lax.optimization_barrier((queries, w_gate_up_early))
     own_kv = projected[:, width_q:].astype(jnp.bfloat16).reshape(seg_dev, SEG, 2 * width_kv)
     bias = jnp.where(path_alive, 0.0, NEG).astype(jnp.float32)
     attended, log_totals, group_kv, w_gate_up, w_down, w_out, cot_all = attend_gather(
@@ -1196,6 +1200,7 @@
         down_weight,
         out_weight,
         cotangent,
+        w_gate_up_early.reshape(half - 1, shard_count, -1, 2 * FF),
         depth,
         shard_count,
         rep_count,
@@ -1210,7 +1215,7 @@
     )
     w_gate_up_late = lax.all_gather(gate_up_late, "shard", axis=1, tiled=True)
     w_down_late = lax.all_gather(down_late, "shard", axis=1, tiled=True)
-    w_gate_up = jnp.concatenate([w_gate_up_early, w_gate_up.reshape(1, D, -1)], axis=0)
+    w_gate_up = w_gate_up.reshape(half, D, -1)
     w_down = w_down.reshape(half, FF, D)
     w_out = w_out.reshape(H * HD, D)
     cot_all = cot_all.reshape(-1, D)
@@ -1229,7 +1234,10 @@
     own_gate = lax.dynamic_slice_in_dim(gate_all, first_expert, own_experts, axis=1)
     own_gate = own_gate.transpose(1, 0, 2).reshape(own_experts, -1, 1)
     first_half = expert_forward(act_all, own_gate[:half], w_gate_up, w_down, cot_all)
-    first_half = first_half[:3] + (
+    first_half = (
+        first_half[0].astype(jnp.bfloat16),
+        first_half[1],
+        first_half[2].astype(jnp.bfloat16),
         row_pieces(first_half[3], shard_count),
         row_pieces(first_half[4], shard_count),
     )
@@ -1237,7 +1245,7 @@
         (first_half, w_gate_up_late, w_down_late)
     )
     second_half = expert_forward(act_all, own_gate[half:], w_gate_up_late, w_down_late, cot_all)
-    mix_part = first_half[0] + second_half[0]
+    mix_part = first_half[0].astype(jnp.float32) + second_half[0]
     gate_grad_own = jnp.concatenate([first_half[1], second_half[1]], axis=0)
     gate_up_early = lax.psum_scatter(first_half[3], "shard", scatter_dimension=0, tiled=False)
     down_early = lax.psum_scatter(first_half[4], "shard", scatter_dimension=0, tiled=False)
@@ -1255,7 +1263,7 @@
         precision=lax.Precision.HIGHEST,
         preferred_element_type=jnp.float32,
     )
-    act_part = (first_half[2] + second_half[2]).astype(jnp.bfloat16)
+    act_part = (first_half[2].astype(jnp.float32) + second_half[2]).astype(jnp.bfloat16)
     act_second_grad = join_reps(act_part.reshape(rep_count, token_count, D))
     act_second_grad = act_second_grad + jnp.dot(
         logit_grad,

time: 1060 us -> 1010 us (0.953); the launches traced: 1050 us -> 1010 us
  local copies, waits for them, and re-layouts: 66.9 us -> 42 us
  Pallas kernels: 626 us -> 602 us
    convert_element_type x2 -> x0, local copies, waits for them, and re-layouts: 17.4 us -> none  [the longest x1 8.7 us: shards(): gate_up_grad.astype(jnp.bfloat16).reshape(half, shard_count, -1, 2 * FF)]
    pallas_call x1, Pallas kernels: 63 us -> 47.7 us  [share_rows(): pl.pallas_call(functools.partial(share_kernel, chunks), out_shape=[jax.Sh...]
  transfers between devices with their start and end apart: 6 -> 6, of which waited for: 1 -> 1; matrix products, arithmetic and copies ran while one was open for 36% -> 35% of each run, Pallas kernels for 28% -> 26%
where the time goes in v6:
time: 1010 us
  Pallas kernels  602 us (60%)
  matrix products  300 us (30%)
  local copies, waits for them, and re-layouts  42 us (4%)
  other arithmetic  32.6 us (3%)
  between operations  15.2 us (2%)
  waiting for transfers between devices  10.2 us (1%)
    pallas_call x1, Pallas kernels, attend_back(): pl.pallas_call(functools.partial(back_kernel, depth, shards), out_shape=o...  171 us
    pallas_call x1, Pallas kernels, attend_gather(): pl.pallas_call(functools.partial(attend_gather_kernel, depth, shards, exp...  164 us
    pallas_call x1, Pallas kernels, finish_grads(): pl.pallas_call(functools.partial(finish_kernel, shards, arrays, 2 * parts...  119 us
    pallas_call x1, Pallas kernels, gather_weights(): pl.pallas_call(functools.partial(weights_kernel, shards), out_shape=[jax....  53.1 us
    dot_general x2, matrix products, expert_forward(): jnp.einsum('etf,edf->td', row_grads, w_gate_up, preferred_element_type=jn...  47.9 us
    pallas_call x1, Pallas kernels, share_rows(): pl.pallas_call(functools.partial(share_kernel, chunks), out_shape=[jax.Sh...  47.7 us
    pallas_call x1, Pallas kernels, join_reps(): pl.pallas_call(join_kernel, out_shape=jax.ShapeDtypeStruct(block, jnp.flo...  47.2 us
    dot_general x2, matrix products, expert_forward(): jnp.einsum('td,etf->edf', rows, row_grads, preferred_element_type=jnp.flo...  47.1 us
  transfers between devices with their start and end apart: 6, of which 1 were waited for; matrix products, arithmetic and copies ran while one was open for 35% of the time, Pallas kernels for 26%

profile of v6, /device:TPU:9, one launch (start us, length us, event | category | flops | bytes accessed | tf_op | source)
XLA Modules:
  0.0 1008.7 jit_solution(10744213792506341676)
XLA Ops:
  7.2 1.8 constant_dynamic-slice_fusion
  9.1 0.8 copy.196
  9.9 0.8 copy.197
  10.9 0.7 maximum_maximum_fusion.1.small
  11.6 53.1 %shard_map.170 = (bf16[8,192,2560]{2,1,0:T(8,128)(2,1)}, bf16[8,192,128]{2,1,0:T(8,128)(2,1)}) custom-call(bf16[192,2560]{1,0:T(8,128)(2,1)} %qkv.1, bf16[192,128]{1,0:T(8,128)(2,1)} %maximum_maximum_fusion.1.small), custom_call_target="tpu_custom_call" | custom-call | bytes 200000000 | tf_op jit(solution)/shard_map/pallas_call | solution.py:353
  64.6 1.2 slice.62
  66.1 2.0 fusion.26
  69.3 8.3 convolution_convert_fusion.2
  77.8 1.4 slice.64.q_ref
  83.6 2.1 constant_dynamic-slice_fusion.3
  85.6 1.8 constant_dynamic-slice_fusion.2
  87.4 163.9 %shard_map.171 = (bf16[640,1536]{1,0:T(8,128)(2,1)S(1)}, f32[20,8,768]{2,1,0:T(8,128)S(1)}, bf16[20,128,1024]{2,1,0:T(8,128)(2,1)}, bf16[2,8,192,1024]{3,2,1,0:T...) custom-call(s32[5,10]{1,0:T(8,128)S(1)} %stack.73.slots, ...), custom_call_target="tpu_custom_call" | custom-call | flops 20000000000 | bytes 700000000 | tf_op jit(solution)/shard_map/pallas_call | solution.py:488
  251.4 1.3 copy-done.17
  252.6 0.8 copy-done.18
  253.5 6.9 multiply_reduce_fusion.2
  261.0 1.3 copy-done.19
  262.7 0.6 fusion.41
  263.5 47.7 %shard_map.172 = (bf16[4,640,1536]{2,1,0:T(8,128)(2,1)S(1)}, f32[4,16,640]{2,1,0:T(8,128)S(1)}) custom-call(bf16[640,1536]{1,0:T(8,128)(2,1)S(1)} %multiply_convert_fusion.2.rows_ref, f32[16,640]{1,0:T(8,128)S(1)} %bitcast.161), custom_call_target="tpu_custom_call" | custom-call | bytes 160000000 | tf_op jit(solution)/shard_map/pallas_call | solution.py:528
  311.2 0.6 copy-done.6
  311.8 3.1 copy-done.15
  314.9 0.6 fusion.68
  316.0 22.6 %convolution_bitcast_fusion.1 = bf16[2,2560,1024]{1,2,0:T(8,128)(2,1)} fusion(bf16[2,1536,1024]{2,1,0:T(8,128)(2,1)} %bitcast.208, bf16[2560,1536,1]{1,0,2:T(8,128)(2,1)} %bitcast.164), kind=kOutput, calls=%fused_computation.57 | convolution fusion | flops 16106127360 | bytes 24641536 | tf_op jit(solution)/shard_map/td,edf->etf/dot_general | solution.py:1122
  338.6 19.7 %fusion.4 = (bf16[2,2560,512]{1,2,0:T(8,128)(2,1)}, bf16[2,2560,512]{1,2,0:T(8,128)(2,1)}, f32[2,2560]{1,0:T(2,128)}) fusion(f32[2,2560]{1,0:T(2,128)S(1)} %bitcast.183, bf16[2,2560,1024]{1,2,0:T(8,128)(2,1)} %convolution_bitcast_fusion.1, bf16[2,512,1536]{2,1,0:T(8,128)(2,1)S(1)} %bitcast.215, bf16[2560,1536,1]{1,0,2:T(8,128)(2,1)} %bitcast.202), kind=kOutput, calls=%fused_computation.21 | convolution fusion | flops 8105487360 | bytes 32022528 | tf_op jit(solution)/shard_map/td,efd->etf/dot_general | solution.py:1129
  358.3 14.4 %convolution_convert_fusion.4 = bf16[2,512,1536]{2,1,0:T(8,128)(2,1)S(1)} fusion(bf16[2560,1536,1]{1,0,2:T(8,128)(2,1)} %bitcast.203, f32[2,2560]{1,0:T(2,128)S(1)} %bitcast.184, bf16[2,2560,1024]{1,2,0:T(8,128)(2,1)} %convolution_bitcast_fusion.1), kind=kOutput, calls=%fused_computation.79 | convolution fusion | flops 8078229504 | bytes 21516288 | tf_op jit(solution)/shard_map/etf,td->efd/dot_general | solution.py:1135
  372.7 2.0 copy.234
  374.7 23.4 %fusion.24 = bf16[2,1024,1536]{1,2,0:T(8,128)(2,1)} fusion(bf16[2560,1536,1]{1,0,2:T(8,128)(2,1)} %bitcast.165, bf16[2,2560,512]{1,2,0:T(8,128)(2,1)} %get-tuple-element.144, bf16[2,2560,512]{1,2,0:T(8,128)(2,1)} %get-tuple-element.143), kind=kOutput, calls=%fused_computation.60 | convolution fusion | flops 16130244608 | bytes 24641536 | tf_op jit(solution)/shard_map/td,etf->edf/dot_general | solution.py:1136
  398.1 6.3 copy.233
  404.4 23.6 %bitcast_convert_fusion = bf16[2560,1536]{1,0:T(8,128)(2,1)} fusion(bf16[2,1536,1024]{2,1,0:T(8,128)(2,1)} %bitcast.209, bf16[2,2560,512]{1,2,0:T(8,128)(2,1)} %get-tuple-element.144, bf16[2,2560,512]{1,2,0:T(8,128)(2,1)} %get-tuple-element.143), kind=kOutput, calls=%fused_computation.12 | convolution fusion | flops 16131031040 | bytes 24641536 | tf_op jit(solution)/shard_map/etf,edf->td/dot_general | solution.py:1138
  428.1 14.7 %bitcast_convert_fusion.1 = bf16[2560,1536]{1,0:T(8,128)(2,1)} fusion(bf16[2,512,1536]{2,1,0:T(8,128)(2,1)S(1)} %bitcast.216, f32[2,2560]{1,0:T(2,128)S(1)} %bitcast.185, bf16[2,2560,1024]{1,2,0:T(8,128)(2,1)} %convolution_bitcast_fusion.1), kind=kOutput, calls=%fused_computation.13 | convolution fusion | flops 8080588800 | bytes 21516288 | tf_op jit(solution)/shard_map/etf,efd->td/dot_general | solution.py:1128
  443.1 0.6 broadcast_subtract_fusion.inv
  443.7 22.4 %convolution_bitcast_fusion = bf16[2,2560,1024]{1,2,0:T(8,128)(2,1)} fusion(bf16[2,1536,1024]{2,1,0:T(8,128)(2,1)} %all-gather.7.cloned.1.call-done, bf16[2560,1536,1]{1,0,2:T(8,128)(2,1)} %bitcast.166), kind=kOutput, calls=%fused_computation.56 | convolution fusion | flops 16106127360 | bytes 24641536 | tf_op jit(solution)/shard_map/td,edf->etf/dot_general | solution.py:1122
  466.2 0.7 copy-done.39
  466.9 20.9 %fusion.7 = (bf16[2,2560,512]{1,2,0:T(8,128)(2,1)}, bf16[2,2560,512]{1,2,0:T(8,128)(2,1)}, f32[2,2560]{1,0:T(2,128)S(1)}) fusion(f32[2,2560]{1,0:T(2,128)S(1)} %bitcast.180, bf16[2,2560,1024]{1,2,0:T(8,128)(2,1)} %convolution_bitcast_fusion, bf16[2,512,1536]{2,1,0:T(8,128)(2,1)} %all-gather.9.cloned.1.call-done, bf16[2560,1536,1]{1,0,2:T(8,128)(2,1)} %bitcast.204), kind=kOutput, calls=%fused_computation.24 | convolution fusion | flops 8105487360 | bytes 32022528 | tf_op jit(solution)/shard_map/td,efd->etf/dot_general | solution.py:1129
  487.8 24.2 %fusion = bf16[2560,1536]{1,0:T(8,128)(2,1)} fusion(bf16[2560,1536]{1,0:T(8,128)(2,1)} %bitcast_convert_fusion, bf16[2,1536,1024]{2,1,0:T(8,128)(2,1)} %all-gather.7.cloned.1.call-done, bf16[2,2560,512]{1,2,0:T(8,128)(2,1)} %get-tuple-element.142, bf16[2,2560,512]{1,2,0:T(8,128)(2,1)} %get-tuple-element.141), kind=kOutput, calls=%fused_computation.9 | convolution fusion | flops 16138895360 | bytes 32505856 | tf_op jit(solution)/shard_map/etf,edf->td/dot_general | solution.py:1138
  512.0 3.2 copy-done.3
  515.3 47.2 %shard_map.173 = f32[640,1536]{1,0:T(8,128)S(1)} custom-call(bf16[4,640,1536]{2,1,0:T(8,128)(2,1)S(1)} %bitcast.159), custom_call_target="tpu_custom_call" | custom-call | bytes 160000000 | tf_op jit(solution)/shard_map/pallas_call | solution.py:602
  562.5 1.9 copy-done.2
  564.4 6.0 all-gather
  570.7 6.9 multiply_reduce_fusion
  577.6 1.0 subtract_add_fusion
  578.7 4.5 convolution_convert_fusion.5.do_ref
  583.2 13.3 %convolution_convert_fusion.3 = bf16[2,512,1536]{2,1,0:T(8,128)(2,1)} fusion(bf16[2560,1536,1]{1,0,2:T(8,128)(2,1)S(1)} %bitcast.207, f32[2,2560]{1,0:T(2,128)S(1)} %bitcast.181, bf16[2,2560,1024]{1,2,0:T(8,128)(2,1)} %convolution_bitcast_fusion), kind=kOutput, calls=%fused_computation.78 | convolution fusion | flops 8078229504 | bytes 21516288 | tf_op jit(solution)/shard_map/etf,td->efd/dot_general | solution.py:1135
  596.5 23.7 %fusion.25 = bf16[2,1024,1536]{1,2,0:T(8,128)(2,1)} fusion(bf16[2560,1536,1]{1,0,2:T(8,128)(2,1)} %bitcast.167, bf16[2,2560,512]{1,2,0:T(8,128)(2,1)} %get-tuple-element.142, bf16[2,2560,512]{1,2,0:T(8,128)(2,1)} %get-tuple-element.141), kind=kOutput, calls=%fused_computation.61 | convolution fusion | flops 16130244608 | bytes 24641536 | tf_op jit(solution)/shard_map/td,etf->edf/dot_general | solution.py:1136
  620.2 17.2 %fusion.1 = bf16[2560,1536]{1,0:T(8,128)(2,1)} fusion(bf16[2560,1536]{1,0:T(8,128)(2,1)} %bitcast_convert_fusion.1, bf16[2,512,1536]{2,1,0:T(8,128)(2,1)} %all-gather.9.cloned.1.call-done, f32[2,2560]{1,0:T(2,128)S(1)} %bitcast.182, bf16[2,2560,1024]{1,2,0:T(8,128)(2,1)} %convolution_bitcast_fusion), kind=kOutput, calls=%fused_computation.11 | convolution fusion | flops 8088453120 | bytes 29380608 | tf_op jit(solution)/shard_map/etf,efd->td/dot_general | solution.py:1128
  637.4 10.1 reduce-scatter.4.cloned.1.call-done
  647.5 171.4 %shard_map.174 = (bf16[640,1536]{1,0:T(8,128)(2,1)}, bf16[5,128,1024]{2,1,0:T(8,128)(2,1)}, bf16[2,192,1024]{2,1,0:T(8,128)(2,1)}, bf16[2,64,1536]{2,1,0:T(8,128...) custom-call(s32[5,10]{1,0:T(8,128)} %copy-done.13, ...), custom_call_target="tpu_custom_call" | custom-call | flops 49999998976 | bytes 700000000 | tf_op jit(solution)/shard_map/pallas_call | solution.py:899
  818.9 0.7 copy-done.8
  819.7 1.6 convolution_convert_fusion.6
  821.6 0.7 concatenate.44
  822.3 9.5 convolution_convert_fusion.1
  831.9 9.6 fusion.34
  841.5 0.7 concatenate.43
  842.6 11.8 %convolution_convert_fusion = bf16[1536,2560]{1,0:T(8,128)(2,1)} fusion(bf16[640,1024]{1,0:T(8,128)(2,1)} %bitcast.218, bf16[640,1536]{1,0:T(8,128)(2,1)} %get-tuple-element.67, bf16[640,1536]{1,0:T(8,128)(2,1)} %param.11, f32[1536]{0:T(1024)S(1)} %copy-done.38, f32[640]{0:T(1024)S(1)} %copy-done.43), kind=kOutput, calls=%fused_computation.18 | convolution fusion | flops 5047582720 | bytes 13115904 | tf_op jit(solution)/shard_map/dot_general | solution.py:1306
  854.5 119.0 %shard_map.175 = (bf16[1,192,2560]{2,1,0:T(8,128)(2,1)S(1)}, bf16[1,192,1536]{2,1,0:T(8,128)(2,1)S(1)}, bf16[1,192,128]{2,1,0:T(8,128)(2,1)S(1)}, bf16[4,4,192,1...) custom-call(bf16[8,1,192,2560]{3,2,1,0:T(8,128)(2,1)} %bitcast.170, ...), custom_call_target="tpu_custom_call" | custom-call | bytes 400000000 | tf_op jit(solution)/shard_map/pallas_call | solution.py:1047
  973.5 1.7 copy-done.4
  975.3 0.7 copy.217
  975.9 0.7 copy.216
  976.6 1.1 bitcast_convert_fusion.5
  977.8 9.3 bitcast_convert_fusion.2
  987.0 1.5 bitcast_convert_fusion.4
  988.5 4.3 bitcast_convert_fusion.3
  992.8 1.3 copy-done.24
  994.1 2.9 fusion.31
  997.0 4.6 add_convert_fusion
  (200 shorter events, 9.2 us)
Async XLA Ops:
  7.2 72.1 %copy-start = (s32[8,20]{1,0:T(8,128)S(1)}, s32[8,20]{1,0:T(8,128)}, u32[]{:S(2)}) copy-start(s32[8,20]{1,0:T(8,128)} %param.20) | copy-start | bytes 1924
  7.2 80.2 %all-gather.5.cloned.1.call-start = ((), (), s32[]{:S(2)}) async-start(), calls=%async_computation.3 | async-start | bytes 3538944 | tf_op jit(solution)/shard_map/all_gather | solution.py:1189
  9.0 433.7 %all-gather.9.cloned.1.call-start = ((), (), s32[]{:S(2)}) async-start(), calls=%async_computation.5 | async-start | bytes 3538944 | tf_op jit(solution)/shard_map/all_gather | solution.py:1217
  10.8 53.8 %copy-start.48 = (bf16[128]{0:T(256)(128)(2,1)}, bf16[128]{0:T(256)(128)(2,1)S(1)}, u32[]{:S(2)}) copy-start(bf16[128]{0:T(256)(128)(2,1)S(1)} %pad.14.clone) | copy-start | bytes 772
  66.0 2.6 copy-start.37
  66.1 194.9 %copy-start.30 = (f32[1536]{0:T(1024)}, f32[1536]{0:T(1024)S(1)}, u32[]{:S(2)}) copy-start(f32[1536]{0:T(1024)S(1)} %get-tuple-element.122) | copy-start | bytes 18436
  77.6 1.6 copy-start.50
  77.6 9.8 copy-start.16
  83.5 167.9 %copy-start.46 = (pred[5,10]{1,0:T(8,128)(4,1)}, pred[5,10]{1,0:T(8,128)(4,1)S(1)}, u32[]{:S(2)}) copy-start(pred[5,10]{1,0:T(8,128)(4,1)S(1)} %stack.83) | copy-start | bytes 154
  83.6 359.3 %copy-start.13 = (s32[5,10]{1,0:T(8,128)}, s32[5,10]{1,0:T(8,128)S(1)}, u32[]{:S(2)}) copy-start(s32[5,10]{1,0:T(8,128)S(1)} %stack.73.slots) | copy-start | bytes 604
  85.6 165.7 %copy-start.14 = (f32[5,10]{1,0:T(8,128)}, f32[5,10]{1,0:T(8,128)S(1)}, u32[]{:S(2)}) copy-start(f32[5,10]{1,0:T(8,128)S(1)} %broadcast_select_fusion.bias) | copy-start | bytes 604
  251.3 1.3 copy-start.17
  252.6 0.8 copy-start.18
  253.4 189.4 %all-gather.7.cloned.1.call-start = ((), (), s32[]{:S(2)}) async-start(), calls=%async_computation.4 | async-start | bytes 7077888 | tf_op jit(solution)/shard_map/all_gather | solution.py:1216
  260.3 1.9 copy-start.19
  260.3 2.3 copy-start.26
  260.4 2.9 copy-start.32
  261.0 1.7 copy-start.33
  311.2 0.6 copy-start.6
  311.8 3.1 copy-start.15
  315.6 321.9 %reduce-scatter.6.cloned.1.call-start = ((), (), s32[]{:S(2)}) async-start(), calls=%async_computation.7 | async-start | bytes 3538944 | tf_op jit(solution)/shard_map/reduce_scatter | solution.py:1251
  316.0 22.6 %copy-start.51 = (bf16[2,8,64,1536]{3,2,1,0:T(8,128)(2,1)S(1)}, bf16[2,8,64,1536]{3,2,1,0:T(8,128)(2,1)}, u32[]{:S(2)}) copy-start(bf16[2,8,64,1536]{3,2,1,0:T(8,128)(2,1)} %get-tuple-element.51) | copy-start | bytes 9437188
  404.4 23.6 %copy-start.52 = (bf16[2,8,64,1536]{3,2,1,0:T(8,128)(2,1)S(1)}, bf16[2,8,64,1536]{3,2,1,0:T(8,128)(2,1)}, u32[]{:S(2)}) copy-start(bf16[2,8,64,1536]{3,2,1,0:T(8,128)(2,1)} %get-tuple-element.51) | copy-start | bytes 9437188
  428.1 14.8 %copy-start.47 = (pred[5,10]{1,0:T(8,128)(4,1)S(1)}, pred[5,10]{1,0:T(8,128)(4,1)}, u32[]{:S(2)}) copy-start(pred[5,10]{1,0:T(8,128)(4,1)} %copy-done.46) | copy-start | bytes 154
  442.8 204.7 %reduce-scatter.4.cloned.1.call-start = ((), (), s32[]{:S(2)}) async-start(), calls=%async_computation.6 | async-start | bytes 7077888 | tf_op jit(solution)/shard_map/reduce_scatter | solution.py:1250
  466.1 0.7 copy-start.39
  466.2 530.9 %reduce-scatter.8.cloned.1.call-start = ((), (), s32[]{:S(2)}) async-start(), calls=%async_computation.8 | async-start | bytes 9830400 | tf_op jit(solution)/shard_map/reduce_scatter | solution.py:1301
  487.8 24.2 %copy-start.40 = (f32[2,2560]{1,0:T(2,128)S(1)}, f32[2,2560]{1,0:T(2,128)}, u32[]{:S(2)}) copy-start(f32[2,2560]{1,0:T(2,128)} %get-tuple-element.60) | copy-start | bytes 61444
  512.0 3.2 copy-start.3
  515.3 55.3 %copy-start.7 = (f32[640,16]{0,1:T(8,128)S(1)}, f32[640,16]{0,1:T(8,128)}, u32[]{:S(2)}) copy-start(f32[640,16]{0,1:T(8,128)} %copy-done.6) | copy-start | bytes 122884
  515.3 55.3 %copy-start.27 = (bf16[8,192,128]{2,1,0:T(8,128)(2,1)S(1)}, bf16[8,192,128]{2,1,0:T(8,128)(2,1)}, u32[]{:S(2)}) copy-start(bf16[8,192,128]{2,1,0:T(8,128)(2,1)} %get-tuple-element.43) | copy-start | bytes 1179652
  515.3 55.3 %copy-start.31 = (f32[1536]{0:T(1024)S(1)}, f32[1536]{0:T(1024)}, u32[]{:S(2)}) copy-start(f32[1536]{0:T(1024)} %copy-done.30) | copy-start | bytes 18436
  515.3 55.3 %copy-start.34 = (f32[640]{0:T(1024)S(1)}, f32[640]{0:T(1024)}, u32[]{:S(2)}) copy-start(f32[640]{0:T(1024)} %copy-done.33) | copy-start | bytes 7684
  562.5 1.9 copy-start.2
  570.5 7.0 copy-start.29
  570.6 6.9 copy-start.35
  570.6 6.9 copy-start.20
  570.6 6.9 copy-start.28
  570.6 6.9 copy-start.44
  570.6 8.0 slice-start.2
  577.6 1.0 slice-start.3
  577.6 5.6 slice-start
  578.6 4.5 copy-start.21
  578.6 4.5 slice-start.1
  818.9 0.8 copy-start.8
  818.9 0.8 copy-start.36
  818.9 2.6 copy-start.45
  822.3 9.5 copy-start.23
  822.3 9.5 copy-start.38
  822.3 9.5 copy-start.43
  822.3 9.5 copy-start.53
  822.3 9.5 copy-start.54
  831.9 10.3 %copy-start.49 = (bf16[128]{0:T(256)(128)(2,1)S(1)}, bf16[128]{0:T(256)(128)(2,1)}, u32[]{:S(2)}) copy-start(bf16[128]{0:T(256)(128)(2,1)} %copy-done.48) | copy-start | bytes 772
  842.6 11.9 %copy-start.9 = (bf16[1,2,192,1024]{3,2,1,0:T(8,128)(2,1)S(1)}, bf16[1,2,192,1024]{3,2,1,0:T(8,128)(2,1)}, u32[]{:S(2)}) copy-start(bf16[1,2,192,1024]{3,2,1,0:T(8,128)(2,1)} %reduce-scatter.4.cloned.1.call-done) | copy-start | bytes 2359300
  842.6 11.9 %copy-start.10 = (bf16[2,192,1024]{2,1,0:T(8,128)(2,1)S(1)}, bf16[2,192,1024]{2,1,0:T(8,128)(2,1)}, u32[]{:S(2)}) copy-start(bf16[2,192,1024]{2,1,0:T(8,128)(2,1)} %get-tuple-element.70.refs_4_) | copy-start | bytes 2359300
  842.6 11.8 %copy-start.11 = (bf16[1,2,64,1536]{3,2,1,0:T(8,128)(2,1)S(1)}, bf16[1,2,64,1536]{3,2,1,0:T(8,128)(2,1)}, u32[]{:S(2)}) copy-start(bf16[1,2,64,1536]{3,2,1,0:T(8,128)(2,1)} %reduce-scatter.6.cloned.1.call-done) | copy-start | bytes 1179652
  842.6 11.8 %copy-start.12 = (bf16[2,64,1536]{2,1,0:T(8,128)(2,1)S(1)}, bf16[2,64,1536]{2,1,0:T(8,128)(2,1)}, u32[]{:S(2)}) copy-start(bf16[2,64,1536]{2,1,0:T(8,128)(2,1)} %get-tuple-element.72.refs_6_) | copy-start | bytes 1179652
  973.5 1.7 copy-start.4
  977.8 10.8 %copy-start.5 = (bf16[4,4,64,1536]{3,2,1,0:T(8,128)(2,1)S(1)}, bf16[4,4,64,1536]{3,2,1,0:T(8,128)(2,1)}, u32[]{:S(2)}) copy-start(bf16[4,4,64,1536]{3,2,1,0:T(8,128)(2,1)} %copy-done.4) | copy-start | bytes 9437188
  987.0 5.8 copy-start.25
  988.5 4.3 copy-start.22
  988.5 5.5 copy-start.24
  988.5 5.5 copy-start.41
  994.1 7.5 copy-start.1
  (1 other events, 0.6 us)
Sparse Core Ops, SparseCore 0:
  10.8 72.5 all-gather.4
  253.5 70.1 all-gather.8
  326.5 96.6 all-gather.6
  442.9 83.9 reduce-scatter.5
  530.4 117.0 reduce-scatter.3
  819.1 95.7 reduce-scatter.7

commit v7 on v6

--- a/solution.py
+++ b/solution.py
@@ -541,81 +541,8 @@
     )(rows, gates)
 
 
-def join_kernel(part, total, near_buf, cross_out, cross_buf, near_sems, cross_sems):
-    rep = lax.axis_index("rep")
-    near = rep + 1 - 2 * (rep % 2)
-    far = lax.rem(rep + 2, 4)
-    diagonal = lax.rem(near + 2, 4)
-    greet(rep_neighbours())
-    sends = Sends()
-    chunks = near_sems.shape[2]
-    size = total.shape[0] // chunks
-    for slot, owner in ((1, diagonal), (0, near)):
-        for c in range(chunks):
-            rows = pl.ds(c * size, size)
-            sends.start(
-                None,
-                part.at[owner, rows],
-                near_buf.at[slot, rows],
-                near_sems.at[0, slot, c],
-                near_sems.at[1, slot, c],
-                {"rep": near},
-            )
-
-    def got(slot, c):
-        here = near_buf.at[slot, pl.ds(c * size, size)]
-        received(None, here, near_sems.at[0, slot, c], near_sems.at[1, slot, c], {"rep": near})
-
-    step = 32 if size % 32 == 0 else size
-    for c in range(chunks):
-        got(1, c)
-
-        def first(i, carry, c=c):
-            rows = pl.ds(pl.multiple_of(c * size + i * step, step), step)
-            value = part[far, rows].astype(jnp.float32) + near_buf[1, rows].astype(jnp.float32)
-            cross_out[rows] = value.astype(cross_out.dtype)
-            return carry
-
-        lax.fori_loop(0, size // step, first, 0)
-        rows = pl.ds(c * size, size)
-        sends.start(
-            None, cross_out.at[rows], cross_buf.at[rows], cross_sems.at[0, c], cross_sems.at[1, c], {"rep": far}
-        )
-    for c in range(chunks):
-        got(0, c)
-        here = cross_buf.at[pl.ds(c * size, size)]
-        received(None, here, cross_sems.at[0, c], cross_sems.at[1, c], {"rep": far})
-
-        def second(i, carry, c=c):
-            rows = pl.ds(pl.multiple_of(c * size + i * step, step), step)
-            value = part[rep, rows].astype(jnp.float32) + near_buf[0, rows].astype(jnp.float32)
-            total[rows] = value + cross_buf[rows].astype(jnp.float32)
-            return carry
-
-        lax.fori_loop(0, size // step, second, 0)
-    sends.drain()
-
-
-def join_reps(part):
-    block = part.shape[1:]
-    chunks = 4
-    return pl.pallas_call(
-        join_kernel,
-        out_shape=jax.ShapeDtypeStruct(block, jnp.float32),
-        in_specs=[VMEM],
-        out_specs=VMEM,
-        scratch_shapes=[
-            pltpu.VMEM((2,) + block, jnp.bfloat16),
-            pltpu.VMEM(block, jnp.bfloat16),
-            pltpu.VMEM(block, jnp.bfloat16),
-            pltpu.SemaphoreType.DMA((2, 2, chunks)),
-            pltpu.SemaphoreType.DMA((2, chunks)),
-        ],
-        cost_estimate=work(0, 1.6e8),
-        compiler_params=pltpu.CompilerParams(
-            collective_id=5, has_side_effects=True, vmem_limit_bytes=40 * 2**20
-        ),
-    )(part)
+def swap_reps(part, flip):
+    return lax.ppermute(part, "rep", [(i, i ^ flip) for i in range(4)])
 
 
 class LineScatter:
@@ -1118,6 +1045,14 @@
     return grad.astype(jnp.bfloat16).reshape(experts, shards, rows // shards, width).transpose(1, 0, 2, 3)
 
 
+def expert_grads(rows, gated, row_parts, upstream):
+    row_grads = jnp.concatenate(row_parts, axis=-1)
+    down_grad = jnp.einsum("etf,td->efd", gated, upstream, preferred_element_type=jnp.float32)
+    gate_up_grad = jnp.einsum("td,etf->edf", rows, row_grads, preferred_element_type=jnp.float32)
+    gate_up_grad = with_layout_constraint(gate_up_grad.astype(jnp.bfloat16), Layout((0, 1, 2)))
+    return (gate_up_grad, down_grad)
+
+
 def expert_forward(rows, gates, w_gate_up, w_down, upstream):
     gate_up = jnp.einsum("td,edf->etf", rows, w_gate_up, preferred_element_type=jnp.bfloat16)
     gate_part = gate_up[..., :FF].astype(jnp.float32)
@@ -1131,12 +1066,11 @@
     hidden_grad = raw_grad * gates
     gate_grad_part = hidden_grad * up_part * sig_gate * (1.0 + gate_part * (1.0 - sig_gate))
     up_grad_part = hidden_grad * gate_part * sig_gate
-    row_grads = jnp.concatenate([gate_grad_part, up_grad_part], axis=-1).astype(jnp.bfloat16)
-    down_grad = jnp.einsum("etf,td->efd", gated, upstream, preferred_element_type=jnp.float32)
-    gate_up_grad = jnp.einsum("td,etf->edf", rows, row_grads, preferred_element_type=jnp.float32)
-    gate_up_grad = with_layout_constraint(gate_up_grad.astype(jnp.bfloat16), Layout((0, 1, 2)))
+    row_parts = (gate_grad_part.astype(jnp.bfloat16), up_grad_part.astype(jnp.bfloat16))
+    row_grads = jnp.concatenate(row_parts, axis=-1)
+    gate_up_grad, down_grad = expert_grads(rows, gated, row_parts, upstream)
     act_part = jnp.einsum("etf,edf->td", row_grads, w_gate_up, preferred_element_type=jnp.float32)
-    return (mix_part, gate_grad, act_part, gate_up_grad, down_grad)
+    return (mix_part, gate_grad, act_part, gate_up_grad, down_grad, gated, row_parts)
 
 
 def shards(
@@ -1249,8 +1183,6 @@
     gate_grad_own = jnp.concatenate([first_half[1], second_half[1]], axis=0)
     gate_up_early = lax.psum_scatter(first_half[3], "shard", scatter_dimension=0, tiled=False)
     down_early = lax.psum_scatter(first_half[4], "shard", scatter_dimension=0, tiled=False)
-    down_grad = second_half[4]
-    gate_up_grad = second_half[3]
     gate_grad_all = lax.all_gather(gate_grad_own, "rep", axis=0, tiled=True)
     gate_grad_table = lax.dynamic_slice_in_dim(
         gate_grad_all, rep_index * token_count, token_count, axis=1
@@ -1264,7 +1196,19 @@
         preferred_element_type=jnp.float32,
     )
     act_part = (first_half[2].astype(jnp.float32) + second_half[2]).astype(jnp.bfloat16)
-    act_second_grad = join_reps(act_part.reshape(rep_count, token_count, D))
+    part_at = functools.partial(
+        lax.dynamic_index_in_dim, act_part.reshape(rep_count, token_count, D), axis=0, keepdims=False
+    )
+    near = rep_index + 1 - 2 * (rep_index % 2)
+    far = lax.rem(rep_index + 2, 4)
+    far_near = swap_reps(part_at(lax.rem(near + 2, 4)), 1)
+    far_sum = (part_at(far).astype(jnp.float32) + far_near.astype(jnp.float32)).astype(jnp.bfloat16)
+    far_sum, late_gated, late_rows = lax.optimization_barrier((far_sum, second_half[5], second_half[6]))
+    far_got = swap_reps(far_sum, 2)
+    gate_up_grad, down_grad = expert_grads(act_all, late_gated, late_rows, cot_all)
+    own_near = swap_reps(part_at(near), 1)
+    own_sum = part_at(rep_index).astype(jnp.float32) + own_near.astype(jnp.float32)
+    act_second_grad = own_sum + far_got.astype(jnp.float32)
     act_second_grad = act_second_grad + jnp.dot(
         logit_grad,
         w_router.astype(jnp.float32).T,

time: 1010 us -> 1010 us (level)
  Pallas kernels: 602 us -> 553 us
  waiting for transfers between devices: 10.2 us -> 50.6 us
    pallas_call x1 -> x0, Pallas kernels: 47.2 us -> none  [join_reps(): pl.pallas_call(join_kernel, out_shape=jax.ShapeDtypeStruct(block, jnp.flo...]
    reduce_scatter x1, waiting for transfers between devices: 10.1 us -> 44.2 us  [shards(): lax.psum_scatter(first_half[3], 'shard', scatter_dimension=0, tiled=False)]
    unnamed x124 -> x112, local copies, waits for them, and re-layouts: 20.5 us -> 16.8 us
  transfers between devices with their start and end apart: 6 -> 9, of which waited for: 1 -> 2; matrix products, arithmetic and copies ran while one was open for 35% -> 36% of each run, Pallas kernels for 26% -> 22%
where the time goes in v7:
time: 1010 us
  Pallas kernels  553 us (55%)
  matrix products  294 us (29%)
  waiting for transfers between devices  50.6 us (5%)
  local copies, waits for them, and re-layouts  42.8 us (4%)
  other arithmetic  42.1 us (4%)
  between operations  15.3 us (2%)
    pallas_call x1, Pallas kernels, attend_back(): pl.pallas_call(functools.partial(back_kernel, depth, shards), out_shape=o...  168 us
    pallas_call x1, Pallas kernels, attend_gather(): pl.pallas_call(functools.partial(attend_gather_kernel, depth, shards, exp...  163 us
    pallas_call x1, Pallas kernels, finish_grads(): pl.pallas_call(functools.partial(finish_kernel, shards, arrays, 2 * parts...  122 us
    pallas_call x1, Pallas kernels, gather_weights(): pl.pallas_call(functools.partial(weights_kernel, shards), out_shape=[jax....  53.1 us
    dot_general x2, matrix products, expert_forward(): jnp.einsum('etf,edf->td', row_grads, w_gate_up, preferred_element_type=jn...  48 us
    pallas_call x1, Pallas kernels, share_rows(): pl.pallas_call(functools.partial(share_kernel, chunks), out_shape=[jax.Sh...  47.7 us
    dot_general x2, matrix products, expert_grads(): jnp.einsum('td,etf->edf', rows, row_grads, preferred_element_type=jnp.flo...  46.6 us
    dot_general x2, matrix products, expert_forward(): jnp.einsum('td,edf->etf', rows, w_gate_up, preferred_element_type=jnp.bfl...  45 us
  transfers between devices with their start and end apart: 9, of which 2 were waited for; matrix products, arithmetic and copies ran while one was open for 36% of the time, Pallas kernels for 22%

profile of v7, /device:TPU:9, one launch (start us, length us, event | category | flops | bytes accessed | tf_op | source)
XLA Modules:
  0.0 1006.4 jit_solution(3727444594775093641)
XLA Ops:
  7.2 1.9 constant_dynamic-slice_fusion
  9.3 0.8 copy.196
  10.1 0.8 copy.197
  11.6 0.7 maximum_maximum_fusion.1.small
  12.3 53.1 %shard_map.170 = (bf16[8,192,2560]{2,1,0:T(8,128)(2,1)}, bf16[8,192,128]{2,1,0:T(8,128)(2,1)}) custom-call(bf16[192,2560]{1,0:T(8,128)(2,1)} %qkv.1, bf16[192,128]{1,0:T(8,128)(2,1)} %maximum_maximum_fusion.1.small), custom_call_target="tpu_custom_call" | custom-call | bytes 200000000 | tf_op jit(solution)/shard_map/pallas_call | solution.py:353
  65.4 1.2 slice.62
  66.8 2.0 fusion.34
  69.4 8.9 convolution_convert_fusion.2
  78.5 1.4 slice.64.q_ref
  84.3 2.1 constant_dynamic-slice_fusion.3
  86.4 1.8 constant_dynamic-slice_fusion.2
  88.1 162.8 %shard_map.171 = (bf16[640,1536]{1,0:T(8,128)(2,1)S(1)}, f32[20,8,768]{2,1,0:T(8,128)S(1)}, bf16[20,128,1024]{2,1,0:T(8,128)(2,1)}, bf16[2,8,192,1024]{3,2,1,0:T...) custom-call(s32[5,10]{1,0:T(8,128)S(1)} %stack.73.slots, ...), custom_call_target="tpu_custom_call" | custom-call | flops 20000000000 | bytes 700000000 | tf_op jit(solution)/shard_map/pallas_call | solution.py:488
  251.0 1.3 copy-done.15
  252.3 0.8 copy-done.16
  253.1 6.9 multiply_reduce_fusion.2
  260.6 1.4 copy-done.17
  263.3 47.7 %shard_map.172 = (bf16[4,640,1536]{2,1,0:T(8,128)(2,1)S(1)}, f32[4,16,640]{2,1,0:T(8,128)S(1)}) custom-call(bf16[640,1536]{1,0:T(8,128)(2,1)S(1)} %multiply_convert_fusion.2.rows_ref, f32[16,640]{1,0:T(8,128)S(1)} %bitcast.171), custom_call_target="tpu_custom_call" | custom-call | bytes 160000000 | tf_op jit(solution)/shard_map/pallas_call | solution.py:528
  311.6 3.1 copy-done.13
  314.7 0.6 fusion.81
  315.8 22.6 %convolution_bitcast_fusion.1 = bf16[2,2560,1024]{1,2,0:T(8,128)(2,1)} fusion(bf16[2,1536,1024]{2,1,0:T(8,128)(2,1)} %bitcast.217, bf16[2560,1536,1]{1,0,2:T(8,128)(2,1)} %bitcast.174), kind=kOutput, calls=%fused_computation.62 | convolution fusion | flops 16106127360 | bytes 24641536 | tf_op jit(solution)/shard_map/td,edf->etf/dot_general | solution.py:1057
  338.4 19.4 %fusion.4 = (bf16[2,2560,512]{1,2,0:T(8,128)(2,1)}, bf16[2,2560,512]{1,2,0:T(8,128)(2,1)}, f32[2,2560]{1,0:T(2,128)}) fusion(f32[2,2560]{1,0:T(2,128)S(1)} %bitcast.194, bf16[2,2560,1024]{1,2,0:T(8,128)(2,1)} %convolution_bitcast_fusion.1, bf16[2,512,1536]{2,1,0:T(8,128)(2,1)S(1)} %bitcast.222, bf16[2560,1536,1]{1,0,2:T(8,128)(2,1)} %bitcast.213), kind=kOutput, calls=%fused_computation.21 | convolution fusion | flops 8105487360 | bytes 32022528 | tf_op jit(solution)/shard_map/td,efd->etf/dot_general | solution.py:1064
  357.8 14.4 %convolution_convert_fusion.4 = bf16[2,512,1536]{2,1,0:T(8,128)(2,1)S(1)} fusion(bf16[2560,1536,1]{1,0,2:T(8,128)(2,1)} %bitcast.214, f32[2,2560]{1,0:T(2,128)S(1)} %bitcast.195, bf16[2,2560,1024]{1,2,0:T(8,128)(2,1)} %convolution_bitcast_fusion.1), kind=kOutput, calls=%fused_computation.89 | convolution fusion | flops 8078229504 | bytes 21516288 | tf_op jit(solution)/shard_map/etf,td->efd/dot_general | solution.py:1050
  372.2 1.9 copy.234
  374.1 23.4 %fusion.30 = bf16[2,1024,1536]{1,2,0:T(8,128)(2,1)} fusion(bf16[2560,1536,1]{1,0,2:T(8,128)(2,1)} %bitcast.175, bf16[2,2560,512]{1,2,0:T(8,128)(2,1)} %get-tuple-element.153, bf16[2,2560,512]{1,2,0:T(8,128)(2,1)} %get-tuple-element.152), kind=kOutput, calls=%fused_computation.65 | convolution fusion | flops 16130244608 | bytes 24641536 | tf_op jit(solution)/shard_map/td,etf->edf/dot_general | solution.py:1051
  397.5 6.3 copy.233
  403.8 23.9 %bitcast_convert_fusion = bf16[2560,1536]{1,0:T(8,128)(2,1)} fusion(bf16[2,1536,1024]{2,1,0:T(8,128)(2,1)} %bitcast.218, bf16[2,2560,512]{1,2,0:T(8,128)(2,1)} %get-tuple-element.153, bf16[2,2560,512]{1,2,0:T(8,128)(2,1)} %get-tuple-element.152), kind=kOutput, calls=%fused_computation.12 | convolution fusion | flops 16131031040 | bytes 24641536 | tf_op jit(solution)/shard_map/etf,edf->td/dot_general | solution.py:1072
  427.7 14.5 %bitcast_convert_fusion.1 = bf16[2560,1536]{1,0:T(8,128)(2,1)} fusion(bf16[2,512,1536]{2,1,0:T(8,128)(2,1)S(1)} %bitcast.223, f32[2,2560]{1,0:T(2,128)S(1)} %bitcast.196, bf16[2,2560,1024]{1,2,0:T(8,128)(2,1)} %convolution_bitcast_fusion.1), kind=kOutput, calls=%fused_computation.13 | convolution fusion | flops 8080588800 | bytes 21516288 | tf_op jit(solution)/shard_map/etf,efd->td/dot_general | solution.py:1063
  443.1 22.4 %convolution_bitcast_fusion = bf16[2,2560,1024]{1,2,0:T(8,128)(2,1)} fusion(bf16[2,1536,1024]{2,1,0:T(8,128)(2,1)} %all-gather.7.cloned.1.call-done, bf16[2560,1536,1]{1,0,2:T(8,128)(2,1)} %bitcast.176), kind=kOutput, calls=%fused_computation.61 | convolution fusion | flops 16106127360 | bytes 24641536 | tf_op jit(solution)/shard_map/td,edf->etf/dot_general | solution.py:1057
  465.6 0.7 copy-done.36
  466.3 22.1 %fusion.7 = (bf16[2,2560,512]{1,2,0:T(8,128)(2,1)}, bf16[2,2560,512]{1,2,0:T(8,128)(2,1)}, f32[2,2560]{1,0:T(2,128)S(1)}, bf16[2,2560,512]{1,2,0:T(8,128)(2,1)}) fusion(f32[2,2560]{1,0:T(2,128)S(1)} %bitcast.193, bf16[2,2560,1024]{1,2,0:T(8,128)(2,1)} %convolution_bitcast_fusion, bf16[2,512,1536]{2,1,0:T(8,128)(2,1)} %all-gather.9.cloned.1.call-done, ...), kind=kOutput, calls=%fused_computation.24 | convolution fusion | flops 8110730240 | bytes 37265408 | tf_op jit(solution)/shard_map/td,efd->etf/dot_general | solution.py:1064
  488.4 24.1 %fusion = bf16[2560,1536]{1,0:T(8,128)(2,1)} fusion(bf16[2560,1536]{1,0:T(8,128)(2,1)} %bitcast_convert_fusion, bf16[2,1536,1024]{2,1,0:T(8,128)(2,1)} %all-gather.7.cloned.1.call-done, bf16[2,2560,512]{1,2,0:T(8,128)(2,1)} %get-tuple-element.71, bf16[2,2560,512]{1,2,0:T(8,128)(2,1)} %get-tuple-element.70), kind=kOutput, calls=%fused_computation.9 | convolution fusion | flops 16138895360 | bytes 32505856 | tf_op jit(solution)/shard_map/etf,edf->td/dot_general | solution.py:1072
  512.6 5.6 all-gather
  518.3 4.6 dynamic-slice_bitcast_fusion.1
  523.4 3.7 fusion.51
  527.1 12.5 %fusion.1 = bf16[2560,1536]{1,0:T(8,128)(2,1)} fusion(bf16[2560,1536]{1,0:T(8,128)(2,1)} %bitcast_convert_fusion.1, bf16[2,2560,512]{1,2,0:T(8,128)(2,1)S(1)} %copy-done.52, bf16[2,512,1536]{2,1,0:T(8,128)(2,1)S(1)} %copy-done.47), kind=kOutput, calls=%fused_computation.11 | convolution fusion | flops 8064860160 | bytes 24117248 | tf_op jit(solution)/shard_map/etf,efd->td/dot_general | solution.py:1063
  539.6 3.9 fusion.43
  543.5 1.4 collective-permute-start.2
  544.9 23.3 %fusion.31 = bf16[2,1024,1536]{1,2,0:T(8,128)(2,1)} fusion(bf16[2560,1536,1]{1,0,2:T(8,128)(2,1)} %bitcast.177, bf16[2,2560,512]{1,2,0:T(8,128)(2,1)} %get-tuple-element.71, bf16[2,2560,512]{1,2,0:T(8,128)(2,1)} %get-tuple-element.70), kind=kOutput, calls=%fused_computation.66 | convolution fusion | flops 16130244608 | bytes 24641536 | tf_op jit(solution)/shard_map/td,etf->edf/dot_general | solution.py:1051
  568.2 13.7 %convolution_convert_fusion.3 = bf16[2,512,1536]{2,1,0:T(8,128)(2,1)} fusion(bf16[2,2560,512]{1,2,0:T(8,128)(2,1)} %get-tuple-element.72, bf16[2560,1536,1]{1,0,2:T(8,128)(2,1)} %bitcast.216), kind=kOutput, calls=%fused_computation.88 | convolution fusion | flops 8054636544 | bytes 16252928 | tf_op jit(solution)/shard_map/etf,td->efd/dot_general | solution.py:1050
  581.9 6.2 collective-permute-done.2
  588.1 4.6 multiply_reduce_fusion
  592.8 1.0 subtract_add_fusion
  593.8 1.9 copy-done.19
  595.7 6.9 convolution_convert_fusion.5.do_ref
  602.6 44.2 %reduce-scatter.4.cloned.1.call-done = bf16[1,2,192,1024]{3,2,1,0:T(8,128)(2,1)} async-done(((bf16[8,2,192,1024]{3,2,1,0:T(8,128)(2,1)}), bf16[1,2,192,1024]{3,2,1,0:T(8,128)(2,1)}) %reduce-scatter.4.cloned.1.call-update) | async-done | bytes 786448 | tf_op jit(solution)/shard_map/reduce_scatter | solution.py:1184
  646.8 168.3 %shard_map.173 = (bf16[640,1536]{1,0:T(8,128)(2,1)}, bf16[5,128,1024]{2,1,0:T(8,128)(2,1)}, bf16[2,192,1024]{2,1,0:T(8,128)(2,1)}, bf16[2,64,1536]{2,1,0:T(8,128...) custom-call(s32[5,10]{1,0:T(8,128)} %copy-done.11, ...), custom_call_target="tpu_custom_call" | custom-call | flops 49999998976 | bytes 700000000 | tf_op jit(solution)/shard_map/pallas_call | solution.py:826
  815.2 0.9 convolution_convert_fusion.6
  816.3 0.7 concatenate.47
  817.1 8.9 convolution_convert_fusion.1
  826.0 10.2 %fusion.42 = (bf16[1536]{0:T(1024)(128)(2,1)S(1)}, f32[640]{0:T(1024)S(1)}, f32[640,1536]{1,0:T(8,128)}) fusion(bf16[640,1536]{1,0:T(8,128)(2,1)S(1)} %copy-done.23, f32[640]{0:T(1024)S(1)} %copy-done.40, f32[1536]{0:T(1024)S(1)} %copy-done.35, bf16[1536,2560]{1,0:T(8,128)(2,1)} %bitcast.211, bf16[640,1024]{1,0:T(8,128)(2,1)S(1)} %bitcast.226, ...), kind=kOutput, calls=%fused_computation.76 | convolution fusion | flops 5046597632 | bytes 17053696 | tf_op jit(solution)/shard_map/dot_general | solution.py:1251
  836.3 0.7 concatenate.46
  837.4 10.8 %convolution_convert_fusion = bf16[1536,2560]{1,0:T(8,128)(2,1)} fusion(bf16[640,1024]{1,0:T(8,128)(2,1)} %bitcast.225, bf16[640,1536]{1,0:T(8,128)(2,1)} %get-tuple-element.75, bf16[640,1536]{1,0:T(8,128)(2,1)S(1)} %copy-done.23, f32[1536]{0:T(1024)S(1)} %copy-done.35, f32[640]{0:T(1024)S(1)} %copy-done.40), kind=kOutput, calls=%fused_computation.18 | convolution fusion | flops 5047582720 | bytes 13115904 | tf_op jit(solution)/shard_map/dot_general | solution.py:1250
  848.2 121.5 %shard_map.174 = (bf16[1,192,2560]{2,1,0:T(8,128)(2,1)S(1)}, bf16[1,192,1536]{2,1,0:T(8,128)(2,1)S(1)}, bf16[1,192,128]{2,1,0:T(8,128)(2,1)S(1)}, bf16[4,4,192,1...) custom-call(bf16[8,1,192,2560]{3,2,1,0:T(8,128)(2,1)} %bitcast.183, ...), custom_call_target="tpu_custom_call" | custom-call | bytes 400000000 | tf_op jit(solution)/shard_map/pallas_call | solution.py:974
  969.8 0.9 copy-done.4
  970.7 0.8 copy-done.8
  971.6 0.7 copy.217
  972.3 0.7 copy.216
  973.0 2.2 bitcast_convert_fusion.5
  975.2 9.2 bitcast_convert_fusion.2
  984.4 1.5 bitcast_convert_fusion.4
  985.9 4.3 bitcast_convert_fusion.3
  990.2 1.3 copy-done.24
  991.5 2.9 fusion.39
  994.4 4.7 add_convert_fusion
  (194 shorter events, 11.5 us)
Async XLA Ops:
  7.2 72.8 %copy-start = (s32[8,20]{1,0:T(8,128)S(1)}, s32[8,20]{1,0:T(8,128)}, u32[]{:S(2)}) copy-start(s32[8,20]{1,0:T(8,128)} %param.20) | copy-start | bytes 1924
  7.2 62.2 %copy-start.22 = (bf16[640,1536]{1,0:T(8,128)(2,1)S(1)}, bf16[640,1536]{1,0:T(8,128)(2,1)}, u32[]{:S(2)}) copy-start(bf16[640,1536]{1,0:T(8,128)(2,1)} %param.11) | copy-start | bytes 5898244
  7.2 81.0 %all-gather.5.cloned.1.call-start = ((), (), s32[]{:S(2)}) async-start(), calls=%async_computation.3 | async-start | bytes 3538944 | tf_op jit(solution)/shard_map/all_gather | solution.py:1123
  9.2 433.0 %all-gather.9.cloned.1.call-start = ((), (), s32[]{:S(2)}) async-start(), calls=%async_computation.5 | async-start | bytes 3538944 | tf_op jit(solution)/shard_map/all_gather | solution.py:1151
  11.0 0.6 copy-start.44
  66.8 11.6 %copy-start.34 = (f32[1536]{0:T(1024)}, f32[1536]{0:T(1024)S(1)}, u32[]{:S(2)}) copy-start(f32[1536]{0:T(1024)S(1)} %get-tuple-element.131) | copy-start | bytes 18436
  66.8 193.8 %copy-start.29 = (f32[1536]{0:T(1024)}, f32[1536]{0:T(1024)S(1)}, u32[]{:S(2)}) copy-start(f32[1536]{0:T(1024)S(1)} %get-tuple-element.130) | copy-start | bytes 18436
  69.4 8.9 copy-start.39
  78.3 1.6 copy-start.46
  78.3 9.8 copy-start.14
  84.2 166.7 %copy-start.42 = (pred[5,10]{1,0:T(8,128)(4,1)}, pred[5,10]{1,0:T(8,128)(4,1)S(1)}, u32[]{:S(2)}) copy-start(pred[5,10]{1,0:T(8,128)(4,1)S(1)} %stack.83) | copy-start | bytes 154
  84.3 358.0 %copy-start.11 = (s32[5,10]{1,0:T(8,128)}, s32[5,10]{1,0:T(8,128)S(1)}, u32[]{:S(2)}) copy-start(s32[5,10]{1,0:T(8,128)S(1)} %stack.73.slots) | copy-start | bytes 604
  86.4 164.6 %copy-start.12 = (f32[5,10]{1,0:T(8,128)}, f32[5,10]{1,0:T(8,128)S(1)}, u32[]{:S(2)}) copy-start(f32[5,10]{1,0:T(8,128)S(1)} %broadcast_select_fusion.bias) | copy-start | bytes 604
  251.0 1.3 copy-start.15
  252.2 0.8 copy-start.16
  253.1 189.1 %all-gather.7.cloned.1.call-start = ((), (), s32[]{:S(2)}) async-start(), calls=%async_computation.4 | async-start | bytes 7077888 | tf_op jit(solution)/shard_map/all_gather | solution.py:1150
  260.0 2.1 copy-start.17
  260.0 2.5 copy-start.26
  260.0 3.1 copy-start.31
  260.6 1.8 copy-start.32
  311.0 0.6 copy-start.2
  311.6 3.1 copy-start.13
  315.3 287.3 %reduce-scatter.6.cloned.1.call-start = ((), (), s32[]{:S(2)}) async-start(), calls=%async_computation.7 | async-start | bytes 3538944 | tf_op jit(solution)/shard_map/reduce_scatter | solution.py:1185
  315.8 22.6 %copy-start.48 = (bf16[2,8,64,1536]{3,2,1,0:T(8,128)(2,1)S(1)}, bf16[2,8,64,1536]{3,2,1,0:T(8,128)(2,1)}, u32[]{:S(2)}) copy-start(bf16[2,8,64,1536]{3,2,1,0:T(8,128)(2,1)} %get-tuple-element.55) | copy-start | bytes 9437188
  403.8 23.9 %copy-start.49 = (bf16[2,8,64,1536]{3,2,1,0:T(8,128)(2,1)S(1)}, bf16[2,8,64,1536]{3,2,1,0:T(8,128)(2,1)}, u32[]{:S(2)}) copy-start(bf16[2,8,64,1536]{3,2,1,0:T(8,128)(2,1)} %get-tuple-element.55) | copy-start | bytes 9437188
  427.7 14.6 %copy-start.43 = (pred[5,10]{1,0:T(8,128)(4,1)S(1)}, pred[5,10]{1,0:T(8,128)(4,1)}, u32[]{:S(2)}) copy-start(pred[5,10]{1,0:T(8,128)(4,1)} %copy-done.42) | copy-start | bytes 154
  442.2 204.6 %reduce-scatter.4.cloned.1.call-start = ((), (), s32[]{:S(2)}) async-start(), calls=%async_computation.6 | async-start | bytes 7077888 | tf_op jit(solution)/shard_map/reduce_scatter | solution.py:1184
  465.6 0.7 copy-start.36
  465.6 528.8 %reduce-scatter.8.cloned.1.call-start = ((), (), s32[]{:S(2)}) async-start(), calls=%async_computation.8 | async-start | bytes 9830400 | tf_op jit(solution)/shard_map/reduce_scatter | solution.py:1245
  488.4 24.1 %copy-start.37 = (f32[2,2560]{1,0:T(2,128)S(1)}, f32[2,2560]{1,0:T(2,128)}, u32[]{:S(2)}) copy-start(f32[2,2560]{1,0:T(2,128)} %get-tuple-element.65) | copy-start | bytes 61444
  512.5 10.9 %copy-start.3 = (f32[640,16]{0,1:T(8,128)S(1)}, f32[640,16]{0,1:T(8,128)}, u32[]{:S(2)}) copy-start(f32[640,16]{0,1:T(8,128)} %copy-done.2) | copy-start | bytes 122884
  512.5 10.9 %copy-start.27 = (bf16[8,192,128]{2,1,0:T(8,128)(2,1)S(1)}, bf16[8,192,128]{2,1,0:T(8,128)(2,1)}, u32[]{:S(2)}) copy-start(bf16[8,192,128]{2,1,0:T(8,128)(2,1)} %get-tuple-element.47) | copy-start | bytes 1179652
  518.3 8.9 copy-start.47
  518.3 8.9 copy-start.52
  522.9 59.0 %collective-permute-start = (bf16[640,1536]{1,0:T(8,128)(2,1)}, bf16[640,1536]{1,0:T(8,128)(2,1)}, u32[]{:S(2)}, u32[]{:S(2)}) collective-permute-start(bf16[640,1536]{1,0:T(8,128)(2,1)} %get-tuple-element.157), channel_id=1, source_target_pairs={{0,8},{8,0},{16,24},{24,16},{1,9},{9,1},{17,25},{25,17},{2,10},{10... | collective-permute-start | bytes 5898248 | tf_op jit(solution)/shard_map/ppermute | solution.py:545
  523.0 16.6 %collective-permute-start.1 = (bf16[640,1536]{1,0:T(8,128)(2,1)}, bf16[640,1536]{1,0:T(8,128)(2,1)}, u32[]{:S(2)}, u32[]{:S(2)}) collective-permute-start(bf16[640,1536]{1,0:T(8,128)(2,1)} %get-tuple-element.158), channel_id=1, source_target_pairs={{0,8},{8,0},{16,24},{24,16},{1,9},{9,1},{17,25},{25,17},{2,10},{10... | collective-permute-start | bytes 5898248 | tf_op jit(solution)/shard_map/ppermute | solution.py:545
  543.5 44.6 %collective-permute-start.2 = (bf16[640,1536]{1,0:T(8,128)(2,1)}, bf16[640,1536]{1,0:T(8,128)(2,1)}, u32[]{:S(2)}, u32[]{:S(2)}) collective-permute-start(bf16[640,1536]{1,0:T(8,128)(2,1)} %fusion.43), channel_id=1, source_target_pairs={{0,16},{8,24},{16,0},{24,8},{1,17},{9,25},{17,1},{25,9},{2,18},{10... | collective-permute-start | bytes 5898248 | tf_op jit(solution)/shard_map/ppermute | solution.py:545
  568.1 20.0 %copy-start.18 = (f32[640,1536]{1,0:T(8,128)S(1)}, f32[640,1536]{1,0:T(8,128)}, u32[]{:S(2)}) copy-start(f32[640,1536]{1,0:T(8,128)} %copy-done.17) | copy-start | bytes 11796484
  568.1 20.0 %copy-start.21 = (f32[640,1536]{1,0:T(8,128)S(1)}, f32[640,1536]{1,0:T(8,128)}, u32[]{:S(2)}) copy-start(f32[640,1536]{1,0:T(8,128)} %fusion.51) | copy-start | bytes 11796484
  568.1 20.0 %copy-start.30 = (f32[1536]{0:T(1024)S(1)}, f32[1536]{0:T(1024)}, u32[]{:S(2)}) copy-start(f32[1536]{0:T(1024)} %copy-done.29) | copy-start | bytes 18436
  568.2 20.0 %copy-start.33 = (f32[640]{0:T(1024)S(1)}, f32[640]{0:T(1024)}, u32[]{:S(2)}) copy-start(f32[640]{0:T(1024)} %copy-done.32) | copy-start | bytes 7684
  581.9 10.9 %copy-start.28 = (bf16[640,1536]{1,0:T(8,128)(2,1)S(1)}, bf16[640,1536]{1,0:T(8,128)(2,1)}, u32[]{:S(2)}) copy-start(bf16[640,1536]{1,0:T(8,128)(2,1)} %cot_ref.1) | copy-start | bytes 5898244
  581.9 10.9 %copy-start.41 = (f32[640]{0:T(1024)S(1)}, f32[640]{0:T(1024)}, u32[]{:S(2)}) copy-start(f32[640]{0:T(1024)} %get-tuple-element.163) | copy-start | bytes 7684
  593.8 1.9 copy-start.19
  817.0 9.0 copy-start.23
  817.0 9.0 copy-start.35
  817.0 9.0 copy-start.40
  817.0 9.0 copy-start.50
  817.0 9.0 copy-start.51
  826.0 11.0 %copy-start.45 = (bf16[128]{0:T(256)(128)(2,1)S(1)}, bf16[128]{0:T(256)(128)(2,1)}, u32[]{:S(2)}) copy-start(bf16[128]{0:T(256)(128)(2,1)} %copy-done.44) | copy-start | bytes 772
  837.4 10.8 %copy-start.6 = (bf16[1,2,192,1024]{3,2,1,0:T(8,128)(2,1)S(1)}, bf16[1,2,192,1024]{3,2,1,0:T(8,128)(2,1)}, u32[]{:S(2)}) copy-start(bf16[1,2,192,1024]{3,2,1,0:T(8,128)(2,1)} %reduce-scatter.4.cloned.1.call-done) | copy-start | bytes 2359300
  837.4 10.8 %copy-start.7 = (bf16[2,192,1024]{2,1,0:T(8,128)(2,1)S(1)}, bf16[2,192,1024]{2,1,0:T(8,128)(2,1)}, u32[]{:S(2)}) copy-start(bf16[2,192,1024]{2,1,0:T(8,128)(2,1)} %get-tuple-element.78.refs_4_) | copy-start | bytes 2359300
  837.4 10.8 %copy-start.9 = (bf16[1,2,64,1536]{3,2,1,0:T(8,128)(2,1)S(1)}, bf16[1,2,64,1536]{3,2,1,0:T(8,128)(2,1)}, u32[]{:S(2)}) copy-start(bf16[1,2,64,1536]{3,2,1,0:T(8,128)(2,1)} %reduce-scatter.6.cloned.1.call-done) | copy-start | bytes 1179652
  837.4 10.8 %copy-start.10 = (bf16[2,64,1536]{2,1,0:T(8,128)(2,1)S(1)}, bf16[2,64,1536]{2,1,0:T(8,128)(2,1)}, u32[]{:S(2)}) copy-start(bf16[2,64,1536]{2,1,0:T(8,128)(2,1)} %get-tuple-element.80.refs_6_) | copy-start | bytes 1179652
  969.8 0.9 copy-start.4
  970.7 0.8 copy-start.8
  975.2 9.2 copy-start.5
  984.4 5.8 copy-start.25
  985.9 4.3 copy-start.20
  985.9 5.5 copy-start.24
  985.9 5.5 copy-start.38
  991.5 7.6 copy-start.1
Sparse Core Ops, SparseCore 0:
  10.8 73.2 all-gather.4
  253.2 70.1 all-gather.8
  326.1 96.8 all-gather.6
  442.3 83.8 reduce-scatter.5
  529.7 117.1 reduce-scatter.3
  815.3 99.6 reduce-scatter.7
